TPU v7x, 32 devices: a whole 2x2x4 slice. The times are simulated.
32 devices in a mesh: parts: 2 (over x), tm: 2 (over core), pix: 8 (over z, y).
Axes of the slice: x: 2, y: 2, z: 4, core: 2. Of those that a mesh axis runs over, the one named last changes fastest.
Arguments:
- frames: bfloat16 [64, 256, 2048], P(('parts', 'tm', 'pix')), parts along dimension 0, may hold values from 2.2 to 19
- dark: bfloat16 [8, 256, 2048], P('parts', None, 'pix'), parts along dimension 0, may hold values from 0 to 2
- dark_index: int32 [64], P(('parts', 'tm')), parts along dimension 0, may hold values from 0 to 3
- cycle_counts: int32 [256], replicated, may hold values from 1024 to 2048, as said below
Outputs:
- correlation: float32 [256, 64, 32], P('pix', ('parts', 'tm')), parts along dimension 1
There are 2 independent parts, one for each index of `parts`. A program takes and returns all parts, laid end to end along the dimension named above; an argument that names none is the same for every part. Nothing has to cross between parts.
Inputs may be any that keep to these rules, and one draw needn't show every extreme that they name: `cycle_counts`: at least one cycle has all 2048 slots live and at least one has exactly half of them.
All inputs are finite; a program needn't handle non-finite values.
Results may differ from a plain program's by a relative error of at most 0.0003.
Values may be sent and summed in bfloat16 or wider, within the bound.
No kernel may reach another device: no remote copies, remote signals or barrier semaphores. Data moves between devices by JAX's collectives and lax.ppermute only.
A program may use at most 128 MiB of HBM per device.

v0:
```python
import jax
import jax.numpy as jnp
from jax import lax
from jax.sharding import PartitionSpec as P


def subtract_dark(raw_frames, dark_frames, dark_index, live_slot):
    values = raw_frames.astype(jnp.float32)
    for dark_level in range(dark_frames.shape[0]):
        picked = (dark_index == dark_level)[:, None, None]
        values = values - jnp.where(
            picked, dark_frames[dark_level].astype(jnp.float32)[None], jnp.float32(0.0)
        )
    return jnp.where(live_slot[None], values, jnp.float32(0.0)).astype(jnp.bfloat16)


def correlate(row_signal, col_signal):
    gram_tiles = jnp.einsum(
        "tqs,uqs->qtu", row_signal, col_signal, preferred_element_type=jnp.float32
    )
    totals = jnp.sum(col_signal, axis=2, dtype=jnp.float32).T
    return (gram_tiles, totals)


def local(frames, dark, dark_index, cycle_counts):
    pix_count = lax.axis_size("pix")
    pix_index = lax.axis_index("pix")
    tm_index = lax.axis_index("tm")
    owned_cycles = frames.shape[1] // pix_count
    regrouped = lax.all_to_all(frames, "pix", split_axis=1, concat_axis=0, tiled=True)
    dark_cycles = lax.all_to_all(dark, "pix", split_axis=1, concat_axis=2, tiled=True)
    block_counts = lax.dynamic_slice_in_dim(cycle_counts, pix_index * owned_cycles, owned_cycles, 0)
    live_slot = jnp.arange(regrouped.shape[2], dtype=jnp.int32)[None, :] < block_counts[:, None]
    signal = subtract_dark(regrouped, dark_cycles, dark_index, live_slot)
    half_frames = signal.shape[0]
    all_frames = lax.all_gather(signal, "tm", axis=0, tiled=True)
    gram_tiles, totals = correlate(signal, all_frames)
    live_counts = lax.dynamic_slice_in_dim(
        cycle_counts, pix_index * owned_cycles, owned_cycles, 0
    ).astype(jnp.float32)
    row_totals = lax.dynamic_slice_in_dim(totals, tm_index * half_frames, half_frames, 1)
    return gram_tiles * live_counts[:, None, None] / (row_totals[:, :, None] * totals[:, None, :])


def solution(mesh):
    in_specs = (
        P(("parts", "tm", "pix"), None, None),
        P("parts", None, "pix"),
        P(("parts", "tm")),
        P(),
    )
    out_specs = P("pix", ("parts", "tm"), None)
    return jax.shard_map(local, mesh=mesh, in_specs=in_specs, out_specs=out_specs, check_vma=False)
```

profile of v0, /device:TPU:17, one launch (start us, length us, event | category | flops | bytes accessed | tf_op | source)
XLA Modules:
  0.0 122.0 jit_solution(14759421002541125091)
XLA Ops:
  6.5 2.2 %copy.22 = bf16[4,256,256]{2,0,1:T(4,128)(2,1)} copy(bf16[4,256,256]{2,1,0:T(8,128)(2,1)} %param.5) | data formatting | bytes 1048576 | tf_op args[1]
  8.8 5.6 %all-to-all-start.1 = ((bf16[4,256,256]{2,0,1:T(4,128)(2,1)}), bf16[4,256,256]{2,0,1:T(4,128)(2,1)S(1)}, u32[]{:S(2)}, u32[]{:S(2)}) async-start(bf16[4,256,256]{2,0,1:T(4,128)(2,1)} %copy.22), calls=%async_computation.1 | async-start | bytes 1048576 | tf_op jit(solution)/shard_map/all_to_all | solution.py:31
  14.4 5.1 %copy.20 = bf16[2,256,2048]{2,0,1:T(2,128)(2,1)} copy(bf16[2,256,2048]{2,1,0:T(8,128)(2,1)} %param.4) | data formatting | bytes 4194304 | tf_op args[0]
  19.5 7.3 %all-to-all-done.1 = bf16[4,256,256]{2,0,1:T(4,128)(2,1)S(1)} async-done(((bf16[4,256,256]{2,0,1:T(4,128)(2,1)}), bf16[4,256,256]{2,0,1:T(4,128)(2,1)S(1)}, u32[]{:S(2)}, u32[]{:S(2)}) %all-to-all-start.1) | async-done | bytes 524320 | tf_op jit(solution)/shard_map/all_to_all | solution.py:31
  26.7 5.9 %all-to-all-start = ((bf16[2,256,2048]{2,0,1:T(2,128)(2,1)}), bf16[2,256,2048]{2,0,1:T(2,128)(2,1)S(1)}, u32[]{:S(2)}, u32[]{:S(2)}) async-start(bf16[2,256,2048]{2,0,1:T(2,128)(2,1)} %copy.20), calls=%async_computation | async-start | bytes 4194304 | tf_op jit(solution)/shard_map/all_to_all | solution.py:30
  32.7 0.1 fusion.1
  32.8 0.0 copy-done.2
  32.8 0.1 iota_compare_fusion
  32.9 0.3 copy.33
  33.2 0.1 slice_convert_fusion.3
  33.3 0.1 copy.30
  33.4 0.1 copy.29
  33.5 0.1 copy.28
  33.6 0.1 copy.27
  33.7 43.6 %all-to-all-done = bf16[2,256,2048]{2,0,1:T(2,128)(2,1)S(1)} async-done(((bf16[2,256,2048]{2,0,1:T(2,128)(2,1)}), bf16[2,256,2048]{2,0,1:T(2,128)(2,1)S(1)}, u32[]{:S(2)}, u32[]{:S(2)}) %all-to-all-start) | async-done | bytes 2097184 | tf_op jit(solution)/shard_map/all_to_all | solution.py:30
  77.3 4.4 %copy_bitcast_fusion = f32[8,2,32,2048]{3,1,0,2:T(2,128)} fusion(bf16[2,8,32,2048]{3,0,2,1:T(2,128)(2,1)S(1)} %bitcast.27), kind=kLoop, calls=%fused_computation.1 | loop fusion | flops 1048576 | bytes 6291456 | tf_op jit(solution)/shard_map/convert_element_type | solution.py:8
  81.7 6.1 %reshape.65 = f32[16,32,2048]{2,0,1:T(8,128)} reshape(f32[8,2,32,2048]{3,1,0,2:T(2,128)} %copy_bitcast_fusion) | data formatting | bytes 8388608 | tf_op jit(solution)/shard_map/convert_element_type | solution.py:8
  87.7 4.8 %select_convert_fusion = bf16[16,32,2048]{2,0,1:T(8,128)(2,1)} fusion(f32[16,32,2048]{2,0,1:T(8,128)} %reshape.65, f32[32,2048]{1,0:T(8,128)S(1)} %bitcast.30, f32[32,2048]{1,0:T(8,128)S(1)} %bitcast.31, f32[32,2048]{1,0:T(8,128)S(1)} %bitcast.32, f32[32,2048]{1,0:T(8,128)S(1)} %bitcast.33, pred[16]{0:T(512)(128)(4,1)S(1)} %get-tuple-element.13, ...), kind=kLoop, calls=%fused_computation.2 | loop fusion | flops 10485760 | bytes 7405632 | tf_op jit(solution)/shard_map/convert_element_type | solution.py:14
  92.5 0.0 all-gather.2.cloned.1.call-update
  92.5 17.3 %all-gather.2.cloned.1.call-done = bf16[32,32,2048]{2,0,1:T(8,128)(2,1)} async-done(((bf16[16,32,2048]{2,0,1:T(8,128)(2,1)}), bf16[32,32,2048]{2,0,1:T(8,128)(2,1)}) %all-gather.2.cloned.1.call-update) | async-done | bytes 4194320 | tf_op jit(solution)/shard_map/all_gather | solution.py:36
  109.8 3.0 %convert_reduce_fusion = f32[32,32]{0,1:T(8,128)S(1)} fusion(bf16[32,32,2048]{2,0,1:T(8,128)(2,1)} %all-gather.2.cloned.1.call-done), kind=kLoop, calls=%fused_computation | loop fusion | flops 4193280 | bytes 4198400 | tf_op jit(solution)/shard_map/reduce_sum | solution.py:21
  112.8 0.1 dynamic-slice_bitcast_fusion
  112.9 0.4 copy-done.1
  113.3 1.9 %fusion = f32[32,16,32]{2,1,0:T(8,128)} fusion(bf16[16,32,2048]{2,0,1:T(8,128)(2,1)S(1)} %copy-done, bf16[32,32,2048]{2,0,1:T(8,128)(2,1)S(1)} %copy-done.1, f32[32,32]{1,0:T(8,128)S(1)} %bitcast.38, f32[32,16]{1,0:T(8,128)S(1)} %dynamic-slice_bitcast_fusion, f32[32]{0:T(128)S(1)} %get-tuple-element.5), kind=kOutput, calls=%fused_computation.4 | convolution fusion | flops 67158016 | bytes 6363264 | tf_op jit(solution)/shard_map/tqs,uqs->qtu/dot_general | solution.py:18
  (8 shorter events, 0.0 us)
Async XLA Ops:
  8.8 18.0 %all-to-all-start.1 = ((bf16[4,256,256]{2,0,1:T(4,128)(2,1)}), bf16[4,256,256]{2,0,1:T(4,128)(2,1)S(1)}, u32[]{:S(2)}, u32[]{:S(2)}) async-start(bf16[4,256,256]{2,0,1:T(4,128)(2,1)} %copy.22), calls=%async_computation.1 | async-start | bytes 1048576 | tf_op jit(solution)/shard_map/all_to_all | solution.py:31
  14.4 18.3 %copy-start.3 = (s32[256]{0:T(256)S(1)}, s32[256]{0:T(256)}, u32[]{:S(2)}) copy-start(s32[256]{0:T(256)} %param.7) | copy-start | bytes 3076
  14.4 18.4 %copy-start.2 = (s32[16]{0:T(128)S(1)}, s32[16]{0:T(128)}, u32[]{:S(2)}) copy-start(s32[16]{0:T(128)} %param.6) | copy-start | bytes 196
  26.7 50.5 %all-to-all-start = ((bf16[2,256,2048]{2,0,1:T(2,128)(2,1)}), bf16[2,256,2048]{2,0,1:T(2,128)(2,1)S(1)}, u32[]{:S(2)}, u32[]{:S(2)}) async-start(bf16[2,256,2048]{2,0,1:T(2,128)(2,1)} %copy.20), calls=%async_computation | async-start | bytes 4194304 | tf_op jit(solution)/shard_map/all_to_all | solution.py:30
  32.7 77.1 %all-gather.2.cloned.1.call-start = ((), (), s32[]{:S(2)}) async-start(), calls=%async_computation.2 | async-start | bytes 6291456 | tf_op jit(solution)/shard_map/all_gather | solution.py:36
  92.5 20.4 %copy-start = (bf16[16,32,2048]{2,0,1:T(8,128)(2,1)S(1)}, bf16[16,32,2048]{2,0,1:T(8,128)(2,1)}, u32[]{:S(2)}) copy-start(bf16[16,32,2048]{2,0,1:T(8,128)(2,1)} %select_convert_fusion) | copy-start | bytes 6291460
  109.8 3.4 %copy-start.1 = (bf16[32,32,2048]{2,0,1:T(8,128)(2,1)S(1)}, bf16[32,32,2048]{2,0,1:T(8,128)(2,1)}, u32[]{:S(2)}) copy-start(bf16[32,32,2048]{2,0,1:T(8,128)(2,1)} %all-gather.2.cloned.1.call-done) | copy-start | bytes 12582916
Sparse Core Ops, SparseCore 0:
  92.6 17.1 all-gather.1
where the time goes:
time: 123 us; the launch traced here: 122 us
  waiting for transfers between devices  68.2 us (55%)
  local copies, waits for them, and re-layouts  14.5 us (12%)
  between operations  13.5 us (11%)
  other arithmetic  12.4 us (10%)
  starting transfers between devices  11.6 us (9%)
  matrix products  1.92 us (2%)
    all_to_all x1, waiting for transfers between devices, local(): lax.all_to_all(frames, 'pix', split_axis=1, concat_axis=0, tiled=True)  43.6 us
    all_gather x1, waiting for transfers between devices, local(): all_frames = lax.all_gather(signal, 'tm', axis=0, tiled=True)  17.3 us
    unnamed x14, local copies, waits for them, and re-layouts  8.08 us
    all_to_all x1, waiting for transfers between devices, local(): lax.all_to_all(dark, 'pix', split_axis=1, concat_axis=2, tiled=True)  7.26 us
    convert_element_type x1, local copies, waits for them, and re-layouts, subtract_dark(): values = raw_frames.astype(jnp.float32)  6.08 us
    all_to_all x1, starting transfers between devices, local(): lax.all_to_all(frames, 'pix', split_axis=1, concat_axis=0, tiled=True)  5.94 us
    all_to_all x1, starting transfers between devices, local(): lax.all_to_all(dark, 'pix', split_axis=1, concat_axis=2, tiled=True)  5.61 us
    convert_element_type x1, other arithmetic, subtract_dark(): jnp.where(live_slot[None], values, jnp.float32(0.0)).astype(jnp.bfloat16)  4.77 us
  transfers between devices with their start and end apart: 3, of which 3 were waited for; matrix products, arithmetic and copies ran while one was open for 5% of the time, Pallas kernels for 0%

commit v1 on v0

--- a/solution.py
+++ b/solution.py
@@ -1,7 +1,16 @@
+import functools
+
 import jax
 import jax.numpy as jnp
+import numpy as np
 from jax import lax
+from jax.experimental import pallas as pl
+from jax.experimental.pallas import tpu as pltpu
 from jax.sharding import PartitionSpec as P
+
+LANES = 128
+ROWS = 16
+VMEM_LIMIT = 48 * 1024 * 1024
 
 
 def subtract_dark(raw_frames, dark_frames, dark_index, live_slot):
@@ -22,7 +31,7 @@
     return (gram_tiles, totals)
 
 
-def local(frames, dark, dark_index, cycle_counts):
+def plain_local(frames, dark, dark_index, cycle_counts):
     pix_count = lax.axis_size("pix")
     pix_index = lax.axis_index("pix")
     tm_index = lax.axis_index("tm")
@@ -42,7 +51,183 @@
     return gram_tiles * live_counts[:, None, None] / (row_totals[:, :, None] * totals[:, None, :])
 
 
+def pack_kernel(n_pix, place, frames, other, dark, *outs):
+    per_device, slots = frames.shape[0], frames.shape[-1]
+    tiles = slots // LANES
+    for k in range(n_pix):
+        dest = place[0] ^ k
+        row = 0
+        for f in range(2 * per_device):
+            for j in range(tiles):
+                lanes = pl.ds(j * LANES, LANES)
+                if f < per_device:
+                    block = frames[f, dest, 0, :, lanes]
+                else:
+                    block = other[f - per_device, dest, :, lanes]
+                outs[k][pl.ds(row, ROWS), :] = block
+                row += ROWS
+        for level in range(dark.shape[0]):
+            for j in range(dark.shape[-1] // LANES):
+                outs[k][pl.ds(row, ROWS), :] = dark[level, dest, 0, :, pl.ds(j * LANES, LANES)]
+                row += ROWS
+
+
+def split3(x):
+    high = x.astype(jnp.bfloat16)
+    rest = x - high.astype(jnp.float32)
+    middle = rest.astype(jnp.bfloat16)
+    low = (rest - middle.astype(jnp.float32)).astype(jnp.bfloat16)
+    return high, middle, low
+
+
+def pick(x, chosen):
+    return sum(jnp.dot(part, chosen, preferred_element_type=jnp.float32) for part in split3(x))
+
+
+def gram_kernel(n_pix, per_device, levels, place, own_index, other_index, counts_col, counts_row, repeat, reorder, *refs):
+    bufs, (out, signal, dark) = refs[:n_pix], refs[n_pix:]
+    me, core = place[0], place[1]
+    frames_half = per_device * n_pix
+    n_frames = 2 * frames_half
+    slots = signal.shape[1]
+    tiles = slots // LANES
+    dark_tiles = tiles // n_pix
+    dark_row = 2 * per_device * tiles * ROWS
+    counts = counts_col[...]
+    lane = lax.broadcasted_iota(jnp.int32, (ROWS, LANES), 1)
+    live = [lane + j * LANES < counts for j in range(tiles)]
+    for k in range(n_pix):
+        source = me ^ k
+        for j in range(dark_tiles):
+            for level in range(levels):
+                row = dark_row + (level * dark_tiles + j) * ROWS
+                dark[source * dark_tiles + j, pl.ds(level * ROWS, ROWS), :] = bufs[k][
+                    pl.ds(row, ROWS), :
+                ].astype(jnp.float32)
+    for k in range(n_pix):
+        source = me ^ k
+        for f in range(2 * per_device):
+            local_frame = source * per_device + f % per_device
+            if f < per_device:
+                level, half = own_index[local_frame], core
+            else:
+                level, half = other_index[local_frame], 1 - core
+            first = pl.multiple_of((half * frames_half + local_frame) * ROWS, ROWS)
+            dark_first = pl.multiple_of(level * ROWS, ROWS)
+            for j in range(tiles):
+                raw = bufs[k][pl.ds((f * tiles + j) * ROWS, ROWS), :].astype(jnp.float32)
+                value = raw - dark[j, pl.ds(dark_first, ROWS), :]
+                value = jnp.where(live[j], value, 0.0)
+                signal[pl.ds(first, ROWS), pl.ds(j * LANES, LANES)] = value.astype(jnp.bfloat16)
+    contract = (((1,), (1,)), ((), ()))
+    width = n_frames * ROWS
+    every = signal[...]
+    totals = lax.dot_general(
+        jnp.ones((ROWS, slots), jnp.bfloat16), every, contract, preferred_element_type=jnp.float32
+    )
+    same = (
+        lax.broadcasted_iota(jnp.int32, (ROWS, width), 0)
+        == lax.broadcasted_iota(jnp.int32, (ROWS, width), 1) % ROWS
+    )
+    diagonal = []
+    step = 8
+    for block in range(n_frames // step):
+        part = lax.dot_general(
+            signal[pl.ds(block * step * ROWS, step * ROWS), :], every, contract,
+            preferred_element_type=jnp.float32,
+        ).reshape(step, ROWS, width)
+        diagonal.append(jnp.sum(jnp.where(same[None], part, 0.0), axis=1))
+    gram = jnp.concatenate(diagonal, axis=0)
+    mine = (
+        lax.broadcasted_iota(jnp.int32, (n_frames, width), 0)
+        == lax.broadcasted_iota(jnp.int32, (n_frames, width), 1) // ROWS
+    )
+    col_totals = totals[0:1, :]
+    row_totals = pick(jnp.where(mine, col_totals, 0.0), repeat[...])
+    ratio = gram * counts_row[...] / (row_totals * col_totals)
+    ordered = pick(ratio, reorder[...])
+    for q in range(ROWS):
+        out[q] = ordered[:, q * n_frames : (q + 1) * n_frames]
+
+
+def in_vmem(count):
+    return [pl.BlockSpec(memory_space=pltpu.VMEM)] * count
+
+
+def in_smem(count):
+    return [pl.BlockSpec(memory_space=pltpu.SMEM)] * count
+
+
+def packed_local(frames, dark, dark_index, cycle_counts):
+    n_pix, core, me = lax.axis_size("pix"), lax.axis_index("tm"), lax.axis_index("pix")
+    per_device, _, slots = frames.shape
+    levels, _, dark_slots = dark.shape
+    n_frames = 2 * per_device * n_pix
+    swap = [(0, 1), (1, 0)]
+    split_frames = frames.reshape(per_device, n_pix, 2, ROWS, slots)
+    split_dark = dark.reshape(levels, n_pix, 2, ROWS, dark_slots)
+    place = jnp.stack([me, core]).astype(jnp.int32)
+    other = lax.ppermute(
+        lax.dynamic_index_in_dim(split_frames, 1 - core, 2, keepdims=False), "tm", swap
+    )
+    other_index = lax.ppermute(dark_index, "tm", swap)
+    own_frames = lax.dynamic_slice_in_dim(split_frames, core, 1, 2)
+    own_dark = lax.dynamic_slice_in_dim(split_dark, core, 1, 2)
+    rows = (2 * per_device * slots + levels * dark_slots) // LANES * ROWS
+    packed = pl.pallas_call(
+        functools.partial(pack_kernel, n_pix),
+        out_shape=[jax.ShapeDtypeStruct((rows, LANES), frames.dtype)] * n_pix,
+        in_specs=in_smem(1) + in_vmem(3),
+        out_specs=in_vmem(n_pix),
+        compiler_params=pltpu.CompilerParams(vmem_limit_bytes=VMEM_LIMIT),
+        name="pack",
+    )(place, own_frames, other, own_dark)
+    received = [packed[0]] + [None] * (n_pix - 1)
+    half = n_pix // 2
+    order = [k for pair in zip(range(half, n_pix), range(1, half + 1)) for k in pair if k != half or pair[0] == half]
+    order = list(dict.fromkeys(order))
+    for k in order:
+        received[k] = lax.ppermute(packed[k], "pix", [(i, i ^ k) for i in range(n_pix)])
+    counts = lax.dynamic_slice_in_dim(cycle_counts, (2 * me + core) * ROWS, ROWS, 0)
+    width = n_frames * ROWS
+    counts_col = jnp.broadcast_to(counts[:, None], (ROWS, LANES))
+    counts_row = jnp.tile(counts.astype(jnp.float32), n_frames)[None]
+    index = np.arange(width)
+    cycle, frame = index % ROWS, index // ROWS
+    repeat = jnp.asarray(cycle[:, None] == cycle[None, :], jnp.bfloat16)
+    reorder = jnp.asarray((cycle * n_frames + frame)[:, None] == index[None, :], jnp.bfloat16)
+    blocks = pl.pallas_call(
+        functools.partial(gram_kernel, n_pix, per_device, levels),
+        out_shape=jax.ShapeDtypeStruct((ROWS, n_frames, n_frames), jnp.float32),
+        in_specs=in_smem(3) + in_vmem(4 + n_pix),
+        out_specs=in_vmem(1)[0],
+        scratch_shapes=[
+            pltpu.VMEM((width, slots), jnp.bfloat16),
+            pltpu.VMEM((slots // LANES, levels * ROWS, LANES), jnp.float32),
+        ],
+        compiler_params=pltpu.CompilerParams(vmem_limit_bytes=VMEM_LIMIT),
+        name="gram",
+    )(place, dark_index, other_index, counts_col, counts_row, repeat, reorder, *received)
+    n_half = n_frames // 2
+    mine = lax.dynamic_slice_in_dim(blocks, core * n_half, n_half, 1)
+    theirs = lax.ppermute(
+        lax.dynamic_slice_in_dim(blocks, (1 - core) * n_half, n_half, 1), "tm", swap
+    )
+    lower = core == 0
+    return jnp.concatenate(
+        [jnp.where(lower, mine, theirs), jnp.where(lower, theirs, mine)], axis=0
+    )
+
+
 def solution(mesh):
+    n_pix, n_tm = mesh.shape["pix"], mesh.shape["tm"]
+
+    def local(frames, dark, dark_index, cycle_counts):
+        owned, slots = frames.shape[1] // n_pix, frames.shape[2]
+        fits = n_tm == 2 and owned == 2 * ROWS and n_pix & (n_pix - 1) == 0 and n_pix <= 8
+        fits = fits and dark.shape[2] % LANES == 0 and slots == dark.shape[2] * n_pix
+        return (packed_local if fits else plain_local)(frames, dark, dark_index, cycle_counts)
+
     in_specs = (
         P(("parts", "tm", "pix"), None, None),
         P("parts", None, "pix"),

time: 123 us -> 76.3 us (0.62)
  between operations: 13.5 us -> 0.04 us
  waiting for transfers between devices: 68.2 us -> 55.3 us
  other arithmetic: 12.4 us -> 0.9 us
  local copies, waits for them, and re-layouts: 14.5 us -> 4.03 us
  Pallas kernels: 0 us -> 7.59 us
  starting transfers between devices: 11.6 us -> 8.22 us
  matrix products: 1.92 us -> 0 us
    ppermute x0 -> x10, waiting for transfers between devices: none -> 55.3 us  [the longest x7 51.2 us: packed_local(): lax.ppermute(packed[k], 'pix', [(i, i ^ k) for i in range(n_pix)])]
    all_to_all x2 -> x0, waiting for transfers between devices: 50.9 us -> none  [the longest x1 43.6 us: local(): lax.all_to_all(frames, 'pix', split_axis=1, concat_axis=0, tiled=True)]
    all_gather x1 -> x0, waiting for transfers between devices: 17.3 us -> none  [local(): all_frames = lax.all_gather(signal, 'tm', axis=0, tiled=True)]
    all_to_all x2 -> x0, starting transfers between devices: 11.5 us -> none  [the longest x1 5.94 us: local(): lax.all_to_all(frames, 'pix', split_axis=1, concat_axis=0, tiled=True)]
    convert_element_type x4 -> x1, other arithmetic: 9.31 us -> 0.07 us  [packed_local(): counts_row = jnp.tile(counts.astype(jnp.float32), n_frames)[None]]
    ppermute x0 -> x10, starting transfers between devices: none -> 8.22 us  [the longest x7 5.44 us: packed_local(): lax.ppermute(packed[k], 'pix', [(i, i ^ k) for i in range(n_pix)])]
    pallas_call x0 -> x2, Pallas kernels: none -> 7.59 us  [the longest x1 5.72 us: packed_local(): pl.pallas_call(functools.partial(gram_kernel, n_pix, per_device, levels),...]
    unnamed x14 -> x10, local copies, waits for them, and re-layouts: 8.08 us -> 1.06 us
  transfers between devices with their start and end apart: 3 -> 10, of which waited for: 3 -> 9; matrix products, arithmetic and copies ran while one was open for 5% -> 0% of each run, Pallas kernels for 0% -> 0%
where the time goes in v1:
time: 76.3 us; the launch traced here: 76.1 us
  waiting for transfers between devices  55.3 us (72%)
  starting transfers between devices  8.22 us (11%)
  Pallas kernels  7.59 us (10%)
  local copies, waits for them, and re-layouts  4.03 us (5%)
  other arithmetic  0.9 us (1%)
    ppermute x7, waiting for transfers between devices, packed_local(): lax.ppermute(packed[k], 'pix', [(i, i ^ k) for i in range(n_pix)])  51.2 us
    pallas_call x1, Pallas kernels, packed_local(): pl.pallas_call(functools.partial(gram_kernel, n_pix, per_device, levels),...  5.72 us
    ppermute x7, starting transfers between devices, packed_local(): lax.ppermute(packed[k], 'pix', [(i, i ^ k) for i in range(n_pix)])  5.44 us
    squeeze x1, local copies, waits for them, and re-layouts, packed_local(): lax.dynamic_index_in_dim(split_frames, 1 - core, 2, keepdims=False)  2.77 us
    ppermute x1, waiting for transfers between devices, packed_local(): lax.ppermute(lax.dynamic_index_in_dim(split_frames, 1 - core, 2, keepdims...  2.4 us
    pallas_call x1, Pallas kernels, packed_local(): pl.pallas_call(functools.partial(pack_kernel, n_pix), out_shape=[jax.Shap...  1.87 us
  transfers between devices with their start and end apart: 10, of which 9 were waited for; matrix products, arithmetic and copies ran while one was open for 0% of the time, Pallas kernels for 0%

profile of v1, /device:TPU:17, one launch (start us, length us, event | category | flops | bytes accessed | tf_op | source)
XLA Modules:
  0.0 76.1 jit_solution(8797944205226247471)
XLA Ops:
  0.0 2.8 %dynamic-slice_bitcast_fusion = (bf16[2,8,16,2048]{3,2,1,0:T(8,128)(2,1)}, bf16[2,8,1,16,2048]{4,3,2,1,0:T(8,128)(2,1)S(1)}) fusion(bf16[2,8,2,16,2048]{4,3,2,1,0:T(8,128)(2,1)} %bitcast.7, s32[]{:T(128)S(6)} %select_n.32, s32[]{:T(128)S(6)} %select_n.31), kind=kLoop, calls=%fused_computation | loop fusion | bytes 4194312 | tf_op jit(solution)/shard_map/jit(dynamic_index_in_dim)/squeeze | solution.py:171
  2.8 0.7 collective-permute-start.1
  3.5 0.1 pad_add_fusion.place
  3.6 2.4 %collective-permute-done.1.other = bf16[2,8,16,2048]{3,2,1,0:T(8,128)(2,1)S(1)} collective-permute-done((bf16[2,8,16,2048]{3,2,1,0:T(8,128)(2,1)}, bf16[2,8,16,2048]{3,2,1,0:T(8,128)(2,1)S(1)}, u32[]{:S(2)}, u32[]{:S(2)}) %collective-permute-start.1) | collective-permute-done | bytes 1048608 | tf_op jit(solution)/shard_map/ppermute | solution.py:170
  6.0 1.9 %pack.1 = (bf16[1152,128]{1,0:T(8,128)(2,1)S(1)}, bf16[1152,128]{1,0:T(8,128)(2,1)S(1)}, bf16[1152,128]{1,0:T(8,128)(2,1)S(1)}, bf16[1152,128]{1,0:T(8,128)(2,1)...) custom-call(s32[2]{0:T(128)S(1)} %pad_add_fusion.place, ...), custom_call_target="tpu_custom_call" | custom-call | tf_op jit(solution)/shard_map/pack/pallas_call | solution.py:177
  7.8 1.2 %collective-permute-start.2 = (bf16[1152,128]{1,0:T(8,128)(2,1)S(1)}, bf16[1152,128]{1,0:T(8,128)(2,1)S(1)}, u32[]{:S(2)}, u32[]{:S(2)}) collective-permute-start(bf16[1152,128]{1,0:T(8,128)(2,1)S(1)} %get-tuple-element.14), channel_id=1, source_target_pairs={{0,1},{1,0},{2,3},{3,2},{4,5},{5,4},{6,7},{7,6},{8,9},{9,8},{10,11... | collective-permute-start | bytes 884744 | tf_op jit(solution)/shard_map/ppermute | solution.py:190
  9.1 1.3 %collective-permute-start.3 = (bf16[1152,128]{1,0:T(8,128)(2,1)S(1)}, bf16[1152,128]{1,0:T(8,128)(2,1)S(1)}, u32[]{:S(2)}, u32[]{:S(2)}) collective-permute-start(bf16[1152,128]{1,0:T(8,128)(2,1)S(1)} %get-tuple-element.15), channel_id=1, source_target_pairs={{0,2},{1,3},{2,0},{3,1},{4,6},{5,7},{6,4},{7,5},{8,10},{9,11},{10,... | collective-permute-start | bytes 884744 | tf_op jit(solution)/shard_map/ppermute | solution.py:190
  10.4 0.9 %collective-permute-start = (s32[16]{0:T(128)S(1)}, s32[16]{0:T(128)S(1)}, u32[]{:S(2)}, u32[]{:S(2)}) collective-permute-start(s32[16]{0:T(128)S(1)} %copy-done.3), channel_id=1, source_target_pairs={{0,8},{8,0},{1,9},{9,1},{2,10},{10,2},{3,11},{11,3},{4,12},{12,4},... | collective-permute-start | bytes 200 | tf_op jit(solution)/shard_map/ppermute | solution.py:173
  11.3 0.1 collective-permute-start.4
  11.4 0.7 collective-permute-done.other_index
  12.1 2.6 %collective-permute-start.6 = (bf16[1152,128]{1,0:T(8,128)(2,1)}, bf16[1152,128]{1,0:T(8,128)(2,1)S(1)}, u32[]{:S(2)}, u32[]{:S(2)}) collective-permute-start(bf16[1152,128]{1,0:T(8,128)(2,1)} %get-tuple-element.18), channel_id=1, source_target_pairs={{0,5},{1,4},{2,7},{3,6},{4,1},{5,0},{6,3},{7,2},{8,13},{9,12},{10,... | collective-permute-start | bytes 884744 | tf_op jit(solution)/shard_map/ppermute | solution.py:190
  14.7 1.3 %collective-permute-done.2.refs_1_ = bf16[1152,128]{1,0:T(8,128)(2,1)S(1)} collective-permute-done((bf16[1152,128]{1,0:T(8,128)(2,1)S(1)}, bf16[1152,128]{1,0:T(8,128)(2,1)S(1)}, u32[]{:S(2)}, u32[]{:S(2)}) %collective-permute-start.2) | collective-permute-done | bytes 294944 | tf_op jit(solution)/shard_map/ppermute | solution.py:190
  16.1 0.2 collective-permute-start.7
  16.2 8.7 %collective-permute-done.3.refs_2_ = bf16[1152,128]{1,0:T(8,128)(2,1)S(1)} collective-permute-done((bf16[1152,128]{1,0:T(8,128)(2,1)S(1)}, bf16[1152,128]{1,0:T(8,128)(2,1)S(1)}, u32[]{:S(2)}, u32[]{:S(2)}) %collective-permute-start.3) | collective-permute-done | bytes 294944 | tf_op jit(solution)/shard_map/ppermute | solution.py:190
  25.0 0.1 broadcast_in_dim_tile.3.counts_row
  25.1 6.4 %collective-permute-done.4.refs_3_ = bf16[1152,128]{1,0:T(8,128)(2,1)S(1)} collective-permute-done((bf16[1152,128]{1,0:T(8,128)(2,1)}, bf16[1152,128]{1,0:T(8,128)(2,1)S(1)}, u32[]{:S(2)}, u32[]{:S(2)}) %collective-permute-start.4) | collective-permute-done | bytes 294944 | tf_op jit(solution)/shard_map/ppermute | solution.py:190
  31.5 18.3 %collective-permute-done.6.refs_5_ = bf16[1152,128]{1,0:T(8,128)(2,1)S(1)} collective-permute-done((bf16[1152,128]{1,0:T(8,128)(2,1)}, bf16[1152,128]{1,0:T(8,128)(2,1)S(1)}, u32[]{:S(2)}, u32[]{:S(2)}) %collective-permute-start.6) | collective-permute-done | bytes 294944 | tf_op jit(solution)/shard_map/ppermute | solution.py:190
  49.8 9.1 %collective-permute-done.7.refs_6_ = bf16[1152,128]{1,0:T(8,128)(2,1)S(1)} collective-permute-done((bf16[1152,128]{1,0:T(8,128)(2,1)}, bf16[1152,128]{1,0:T(8,128)(2,1)S(1)}, u32[]{:S(2)}, u32[]{:S(2)}) %collective-permute-start.7) | collective-permute-done | bytes 294944 | tf_op jit(solution)/shard_map/ppermute | solution.py:190
  58.9 7.4 %collective-permute-done.8.refs_7_ = bf16[1152,128]{1,0:T(8,128)(2,1)} collective-permute-done((bf16[1152,128]{1,0:T(8,128)(2,1)}, bf16[1152,128]{1,0:T(8,128)(2,1)}, u32[]{:S(2)}, u32[]{:S(2)}) %collective-permute-start.8) | collective-permute-done | bytes 294944 | tf_op jit(solution)/shard_map/ppermute | solution.py:190
  66.4 1.0 %copy-done.2 = bf16[512,512]{1,0:T(8,128)(2,1)S(1)} copy-done((bf16[512,512]{1,0:T(8,128)(2,1)S(1)}, bf16[512,512]{1,0:T(8,128)(2,1)}, u32[]{:S(2)}) %copy-start.2) | copy-done | bytes 524312
  67.4 5.7 %gram.1 = f32[16,32,32]{2,1,0:T(8,128)S(1)} custom-call(s32[2]{0:T(128)S(1)} %pad_add_fusion.place, s32[16]{0:T(128)S(1)} %copy-done.3, s32[16]{0:T(128)S(1)} %collective-permute-done.other_index, s32[16,128]{1,0:T(8,128)S(1)} %broadcast_in_dim.2.counts_col, f32[1,512]{1,0:T(1,128)S(1)} %broadcast_in_dim_tile.3.counts_row, bf16[512,512]{1,0:T(8,128)(2,1)S(1)} %copy-done.1, ...), custom_call_target="tpu_custom_call" | custom-call | tf_op jit(solution)/shard_map/gram/pallas_call | solution.py:199
  73.2 1.2 %collective-permute-start.9 = (f32[16,16,32]{2,1,0:T(8,128)S(1)}, f32[16,16,32]{2,1,0:T(8,128)S(1)}, u32[]{:S(2)}, u32[]{:S(2)}) collective-permute-start(f32[16,16,32]{2,1,0:T(8,128)S(1)} %constant_dynamic-slice_fusion), channel_id=1, source_target_pairs={{0,8},{8,0},{1,9},{9,1},{2,10},{10,2},{3,11},{11,3},{4,12},{12,4},... | collective-permute-start | bytes 98312 | tf_op jit(solution)/shard_map/ppermute | solution.py:213
  74.3 1.0 %collective-permute-done.9 = f32[16,16,32]{2,1,0:T(8,128)S(1)} collective-permute-done((f32[16,16,32]{2,1,0:T(8,128)S(1)}, f32[16,16,32]{2,1,0:T(8,128)S(1)}, u32[]{:S(2)}, u32[]{:S(2)}) %collective-permute-start.9) | collective-permute-done | bytes 32800 | tf_op jit(solution)/shard_map/ppermute | solution.py:213
  75.4 0.7 pad_maximum_fusion
  (18 shorter events, 0.2 us)
Async XLA Ops:
  0.0 3.5 %copy-start = (bf16[4,256,256]{2,1,0:T(8,128)(2,1)S(1)}, bf16[4,256,256]{2,1,0:T(8,128)(2,1)}, u32[]{:S(2)}) copy-start(bf16[4,256,256]{2,1,0:T(8,128)(2,1)} %param.7) | copy-start | bytes 1572868
  2.8 7.6 %copy-start.3 = (s32[16]{0:T(128)S(1)}, s32[16]{0:T(128)}, u32[]{:S(2)}) copy-start(s32[16]{0:T(128)} %own_index.1) | copy-start | bytes 196
  2.8 22.2 %copy-start.4 = (s32[256]{0:T(256)S(1)}, s32[256]{0:T(256)}, u32[]{:S(2)}) copy-start(s32[256]{0:T(256)} %param.9) | copy-start | bytes 3076
  2.8 63.6 %copy-start.1 = (bf16[512,512]{1,0:T(8,128)(2,1)S(1)}, bf16[512,512]{1,0:T(8,128)(2,1)}, u32[]{:S(2)}) copy-start(bf16[512,512]{1,0:T(8,128)(2,1)} %constant.31.clone.repeat) | copy-start | bytes 1572868
  2.8 3.2 %collective-permute-start.1 = (bf16[2,8,16,2048]{3,2,1,0:T(8,128)(2,1)}, bf16[2,8,16,2048]{3,2,1,0:T(8,128)(2,1)S(1)}, u32[]{:S(2)}, u32[]{:S(2)}) collective-permute-start(bf16[2,8,16,2048]{3,2,1,0:T(8,128)(2,1)} %get-tuple-element.23), channel_id=1, source_target_pairs={{0,8},{8,0},{1,9},{9,1},{2,10},{10,2},{3,11},{11,3},{4,12},{12,4},... | collective-permute-start | bytes 3145736 | tf_op jit(solution)/shard_map/ppermute | solution.py:170
  7.8 8.2 %collective-permute-start.2 = (bf16[1152,128]{1,0:T(8,128)(2,1)S(1)}, bf16[1152,128]{1,0:T(8,128)(2,1)S(1)}, u32[]{:S(2)}, u32[]{:S(2)}) collective-permute-start(bf16[1152,128]{1,0:T(8,128)(2,1)S(1)} %get-tuple-element.14), channel_id=1, source_target_pairs={{0,1},{1,0},{2,3},{3,2},{4,5},{5,4},{6,7},{7,6},{8,9},{9,8},{10,11... | collective-permute-start | bytes 884744 | tf_op jit(solution)/shard_map/ppermute | solution.py:190
  9.1 15.9 %collective-permute-start.3 = (bf16[1152,128]{1,0:T(8,128)(2,1)S(1)}, bf16[1152,128]{1,0:T(8,128)(2,1)S(1)}, u32[]{:S(2)}, u32[]{:S(2)}) collective-permute-start(bf16[1152,128]{1,0:T(8,128)(2,1)S(1)} %get-tuple-element.15), channel_id=1, source_target_pairs={{0,2},{1,3},{2,0},{3,1},{4,6},{5,7},{6,4},{7,5},{8,10},{9,11},{10,... | collective-permute-start | bytes 884744 | tf_op jit(solution)/shard_map/ppermute | solution.py:190
  10.4 1.8 %collective-permute-start = (s32[16]{0:T(128)S(1)}, s32[16]{0:T(128)S(1)}, u32[]{:S(2)}, u32[]{:S(2)}) collective-permute-start(s32[16]{0:T(128)S(1)} %copy-done.3), channel_id=1, source_target_pairs={{0,8},{8,0},{1,9},{9,1},{2,10},{10,2},{3,11},{11,3},{4,12},{12,4},... | collective-permute-start | bytes 200 | tf_op jit(solution)/shard_map/ppermute | solution.py:173
  11.3 20.2 %collective-permute-start.4 = (bf16[1152,128]{1,0:T(8,128)(2,1)}, bf16[1152,128]{1,0:T(8,128)(2,1)S(1)}, u32[]{:S(2)}, u32[]{:S(2)}) collective-permute-start(bf16[1152,128]{1,0:T(8,128)(2,1)} %get-tuple-element.16), channel_id=1, source_target_pairs={{0,3},{1,2},{2,1},{3,0},{4,7},{5,6},{6,5},{7,4},{8,11},{9,10},{10,... | collective-permute-start | bytes 884744 | tf_op jit(solution)/shard_map/ppermute | solution.py:190
  11.4 20.1 %collective-permute-start.5 = (bf16[1152,128]{1,0:T(8,128)(2,1)}, bf16[1152,128]{1,0:T(8,128)(2,1)S(1)}, u32[]{:S(2)}, u32[]{:S(2)}) collective-permute-start(bf16[1152,128]{1,0:T(8,128)(2,1)} %get-tuple-element.17), channel_id=1, source_target_pairs={{0,4},{1,5},{2,6},{3,7},{4,0},{5,1},{6,2},{7,3},{8,12},{9,13},{10,... | collective-permute-start | bytes 884744 | tf_op jit(solution)/shard_map/ppermute | solution.py:190
  12.1 37.7 %collective-permute-start.6 = (bf16[1152,128]{1,0:T(8,128)(2,1)}, bf16[1152,128]{1,0:T(8,128)(2,1)S(1)}, u32[]{:S(2)}, u32[]{:S(2)}) collective-permute-start(bf16[1152,128]{1,0:T(8,128)(2,1)} %get-tuple-element.18), channel_id=1, source_target_pairs={{0,5},{1,4},{2,7},{3,6},{4,1},{5,0},{6,3},{7,2},{8,13},{9,12},{10,... | collective-permute-start | bytes 884744 | tf_op jit(solution)/shard_map/ppermute | solution.py:190
  16.1 42.9 %collective-permute-start.7 = (bf16[1152,128]{1,0:T(8,128)(2,1)}, bf16[1152,128]{1,0:T(8,128)(2,1)S(1)}, u32[]{:S(2)}, u32[]{:S(2)}) collective-permute-start(bf16[1152,128]{1,0:T(8,128)(2,1)} %get-tuple-element.19), channel_id=1, source_target_pairs={{0,6},{1,7},{2,4},{3,5},{4,2},{5,3},{6,0},{7,1},{8,14},{9,15},{10,... | collective-permute-start | bytes 884744 | tf_op jit(solution)/shard_map/ppermute | solution.py:190
  24.9 41.4 %collective-permute-start.8 = (bf16[1152,128]{1,0:T(8,128)(2,1)}, bf16[1152,128]{1,0:T(8,128)(2,1)}, u32[]{:S(2)}, u32[]{:S(2)}) collective-permute-start(bf16[1152,128]{1,0:T(8,128)(2,1)} %get-tuple-element.20), channel_id=1, source_target_pairs={{0,7},{1,6},{2,5},{3,4},{4,3},{5,2},{6,1},{7,0},{8,15},{9,14},{10,... | collective-permute-start | bytes 884744 | tf_op jit(solution)/shard_map/ppermute | solution.py:190
  66.4 1.0 %copy-start.2 = (bf16[512,512]{1,0:T(8,128)(2,1)S(1)}, bf16[512,512]{1,0:T(8,128)(2,1)}, u32[]{:S(2)}) copy-start(bf16[512,512]{1,0:T(8,128)(2,1)} %constant.32.clone.reorder) | copy-start | bytes 1572868
  73.2 2.2 %collective-permute-start.9 = (f32[16,16,32]{2,1,0:T(8,128)S(1)}, f32[16,16,32]{2,1,0:T(8,128)S(1)}, u32[]{:S(2)}, u32[]{:S(2)}) collective-permute-start(f32[16,16,32]{2,1,0:T(8,128)S(1)} %constant_dynamic-slice_fusion), channel_id=1, source_target_pairs={{0,8},{8,0},{1,9},{9,1},{2,10},{10,2},{3,11},{11,3},{4,12},{12,4},... | collective-permute-start | bytes 98312 | tf_op jit(solution)/shard_map/ppermute | solution.py:213

commit v2 on v1

--- a/solution.py
+++ b/solution.py
@@ -10,6 +10,7 @@
 
 LANES = 128
 ROWS = 16
+FIRST = 2
 VMEM_LIMIT = 48 * 1024 * 1024
 
 
@@ -51,25 +52,31 @@
     return gram_tiles * live_counts[:, None, None] / (row_totals[:, :, None] * totals[:, None, :])
 
 
-def pack_kernel(n_pix, place, frames, other, dark, *outs):
+def pack_kernel(n_pix, messages, place, frames, dark, *refs):
+    count = len(messages)
+    outs, (raw, shade, raw_sem, shade_sem) = refs[:count], refs[count:]
     per_device, slots = frames.shape[0], frames.shape[-1]
-    tiles = slots // LANES
-    for k in range(n_pix):
-        dest = place[0] ^ k
+    share = shade.shape[1]
+    copies = []
+    for n, k in enumerate(messages):
+        dest, half = place[0] ^ (k % n_pix), place[1] ^ (k // n_pix)
+        copies.append((
+            pltpu.make_async_copy(frames.at[:, dest, half], raw.at[n], raw_sem.at[n]),
+            pltpu.make_async_copy(
+                dark.at[pl.ds(place[1] * share, share), dest, half], shade.at[n], shade_sem.at[n]
+            ),
+        ))
+        for copy in copies[-1]:
+            copy.start()
+    for n in range(count):
+        for copy in copies[n]:
+            copy.wait()
         row = 0
-        for f in range(2 * per_device):
-            for j in range(tiles):
-                lanes = pl.ds(j * LANES, LANES)
-                if f < per_device:
-                    block = frames[f, dest, 0, :, lanes]
-                else:
-                    block = other[f - per_device, dest, :, lanes]
-                outs[k][pl.ds(row, ROWS), :] = block
-                row += ROWS
-        for level in range(dark.shape[0]):
-            for j in range(dark.shape[-1] // LANES):
-                outs[k][pl.ds(row, ROWS), :] = dark[level, dest, 0, :, pl.ds(j * LANES, LANES)]
-                row += ROWS
+        for block, depth in ((raw, per_device), (shade, share)):
+            for f in range(depth):
+                for j in range(block.shape[-1] // LANES):
+                    outs[n][pl.ds(row, ROWS), :] = block[n, f, :, pl.ds(j * LANES, LANES)]
+                    row += ROWS
 
 
 def split3(x):
@@ -85,35 +92,35 @@
 
 
 def gram_kernel(n_pix, per_device, levels, place, own_index, other_index, counts_col, counts_row, repeat, reorder, *refs):
-    bufs, (out, signal, dark) = refs[:n_pix], refs[n_pix:]
+    n_bufs = 2 * n_pix
+    bufs, (out, signal, dark) = refs[:n_bufs], refs[n_bufs:]
     me, core = place[0], place[1]
+    share = levels // 2
     frames_half = per_device * n_pix
     n_frames = 2 * frames_half
     slots = signal.shape[1]
     tiles = slots // LANES
     dark_tiles = tiles // n_pix
-    dark_row = 2 * per_device * tiles * ROWS
+    dark_row = per_device * tiles * ROWS
     counts = counts_col[...]
     lane = lax.broadcasted_iota(jnp.int32, (ROWS, LANES), 1)
     live = [lane + j * LANES < counts for j in range(tiles)]
-    for k in range(n_pix):
-        source = me ^ k
+    for k in range(n_bufs):
+        source, half = me ^ (k % n_pix), core ^ (k // n_pix)
         for j in range(dark_tiles):
-            for level in range(levels):
-                row = dark_row + (level * dark_tiles + j) * ROWS
-                dark[source * dark_tiles + j, pl.ds(level * ROWS, ROWS), :] = bufs[k][
+            for n in range(share):
+                level = pl.multiple_of((half * share + n) * ROWS, ROWS)
+                row = dark_row + (n * dark_tiles + j) * ROWS
+                dark[source * dark_tiles + j, pl.ds(level, ROWS), :] = bufs[k][
                     pl.ds(row, ROWS), :
                 ].astype(jnp.float32)
-    for k in range(n_pix):
-        source = me ^ k
-        for f in range(2 * per_device):
-            local_frame = source * per_device + f % per_device
-            if f < per_device:
-                level, half = own_index[local_frame], core
-            else:
-                level, half = other_index[local_frame], 1 - core
-            first = pl.multiple_of((half * frames_half + local_frame) * ROWS, ROWS)
-            dark_first = pl.multiple_of(level * ROWS, ROWS)
+    for k in range(n_bufs):
+        source, half = me ^ (k % n_pix), core ^ (k // n_pix)
+        index = own_index if k < n_pix else other_index
+        for f in range(per_device):
+            frame = source * per_device + f
+            first = pl.multiple_of((half * frames_half + frame) * ROWS, ROWS)
+            dark_first = pl.multiple_of(index[frame] * ROWS, ROWS)
             for j in range(tiles):
                 raw = bufs[k][pl.ds((f * tiles + j) * ROWS, ROWS), :].astype(jnp.float32)
                 value = raw - dark[j, pl.ds(dark_first, ROWS), :]
@@ -129,15 +136,9 @@
         lax.broadcasted_iota(jnp.int32, (ROWS, width), 0)
         == lax.broadcasted_iota(jnp.int32, (ROWS, width), 1) % ROWS
     )
-    diagonal = []
-    step = 8
-    for block in range(n_frames // step):
-        part = lax.dot_general(
-            signal[pl.ds(block * step * ROWS, step * ROWS), :], every, contract,
-            preferred_element_type=jnp.float32,
-        ).reshape(step, ROWS, width)
-        diagonal.append(jnp.sum(jnp.where(same[None], part, 0.0), axis=1))
-    gram = jnp.concatenate(diagonal, axis=0)
+    products = lax.dot_general(every, every, contract, preferred_element_type=jnp.float32)
+    products = products.reshape(n_frames, ROWS, width)
+    gram = jnp.sum(jnp.where(same[None], products, 0.0), axis=1)
     mine = (
         lax.broadcasted_iota(jnp.int32, (n_frames, width), 0)
         == lax.broadcasted_iota(jnp.int32, (n_frames, width), 1) // ROWS
@@ -166,28 +167,37 @@
     swap = [(0, 1), (1, 0)]
     split_frames = frames.reshape(per_device, n_pix, 2, ROWS, slots)
     split_dark = dark.reshape(levels, n_pix, 2, ROWS, dark_slots)
+    share = levels // 2
     place = jnp.stack([me, core]).astype(jnp.int32)
-    other = lax.ppermute(
-        lax.dynamic_index_in_dim(split_frames, 1 - core, 2, keepdims=False), "tm", swap
-    )
+    rows = (per_device * slots + share * dark_slots) // LANES * ROWS
+    half = n_pix // 2
+    far = [t * n_pix + k for t in range(2) for k in range(half, n_pix)]
+    near = [t * n_pix + k for t in range(2) for k in range(1, half)] + [n_pix]
+    order = [k for pair in zip(far, near) for k in pair] + far[len(near) :]
+    packed = {}
+    for messages in (order[:FIRST], order[FIRST:] + [0]):
+        count = len(messages)
+        buffers = pl.pallas_call(
+            functools.partial(pack_kernel, n_pix, messages),
+            out_shape=[jax.ShapeDtypeStruct((rows, LANES), frames.dtype)] * count,
+            in_specs=in_smem(1) + [pl.BlockSpec(memory_space=pl.ANY)] * 2,
+            out_specs=in_vmem(count),
+            scratch_shapes=[
+                pltpu.VMEM((count, per_device, ROWS, slots), frames.dtype),
+                pltpu.VMEM((count, share, ROWS, dark_slots), dark.dtype),
+                pltpu.SemaphoreType.DMA((count,)),
+                pltpu.SemaphoreType.DMA((count,)),
+            ],
+            compiler_params=pltpu.CompilerParams(vmem_limit_bytes=VMEM_LIMIT),
+            name="pack",
+        )(place, split_frames, split_dark)
+        packed.update(zip(messages, buffers))
+    received = [packed[0]] + [None] * (2 * n_pix - 1)
+    for k in order:
+        received[k] = lax.ppermute(
+            packed[k], ("tm", "pix"), [(i, i ^ k) for i in range(2 * n_pix)]
+        )
     other_index = lax.ppermute(dark_index, "tm", swap)
-    own_frames = lax.dynamic_slice_in_dim(split_frames, core, 1, 2)
-    own_dark = lax.dynamic_slice_in_dim(split_dark, core, 1, 2)
-    rows = (2 * per_device * slots + levels * dark_slots) // LANES * ROWS
-    packed = pl.pallas_call(
-        functools.partial(pack_kernel, n_pix),
-        out_shape=[jax.ShapeDtypeStruct((rows, LANES), frames.dtype)] * n_pix,
-        in_specs=in_smem(1) + in_vmem(3),
-        out_specs=in_vmem(n_pix),
-        compiler_params=pltpu.CompilerParams(vmem_limit_bytes=VMEM_LIMIT),
-        name="pack",
-    )(place, own_frames, other, own_dark)
-    received = [packed[0]] + [None] * (n_pix - 1)
-    half = n_pix // 2
-    order = [k for pair in zip(range(half, n_pix), range(1, half + 1)) for k in pair if k != half or pair[0] == half]
-    order = list(dict.fromkeys(order))
-    for k in order:
-        received[k] = lax.ppermute(packed[k], "pix", [(i, i ^ k) for i in range(n_pix)])
     counts = lax.dynamic_slice_in_dim(cycle_counts, (2 * me + core) * ROWS, ROWS, 0)
     width = n_frames * ROWS
     counts_col = jnp.broadcast_to(counts[:, None], (ROWS, LANES))
@@ -199,7 +209,7 @@
     blocks = pl.pallas_call(
         functools.partial(gram_kernel, n_pix, per_device, levels),
         out_shape=jax.ShapeDtypeStruct((ROWS, n_frames, n_frames), jnp.float32),
-        in_specs=in_smem(3) + in_vmem(4 + n_pix),
+        in_specs=in_smem(3) + in_vmem(4 + 2 * n_pix),
         out_specs=in_vmem(1)[0],
         scratch_shapes=[
             pltpu.VMEM((width, slots), jnp.bfloat16),
@@ -225,7 +235,7 @@
     def local(frames, dark, dark_index, cycle_counts):
         owned, slots = frames.shape[1] // n_pix, frames.shape[2]
         fits = n_tm == 2 and owned == 2 * ROWS and n_pix & (n_pix - 1) == 0 and n_pix <= 8
-        fits = fits and dark.shape[2] % LANES == 0 and slots == dark.shape[2] * n_pix
+        fits = fits and dark.shape[0] % 2 == 0 and dark.shape[2] % LANES == 0 and slots == dark.shape[2] * n_pix
         return (packed_local if fits else plain_local)(frames, dark, dark_index, cycle_counts)
 
     in_specs = (

time: 76.3 us -> 73.3 us (0.961)
  the two profiles are of different devices: /device:TPU:17 before, /device:TPU:0 now
where the time goes in v2:
time: 73.3 us; the launch traced here: 73.1 us
  waiting for transfers between devices  32.5 us (44%)
  starting transfers between devices  26.6 us (36%)
  Pallas kernels  8.58 us (12%)
  local copies, waits for them, and re-layouts  4.39 us (6%)
  other arithmetic  0.9 us (1%)
    ppermute x15, waiting for transfers between devices, packed_local(): lax.ppermute(packed[k], ('tm', 'pix'), [(i, i ^ k) for i in range(2 * n_p...  30.4 us
    ppermute x15, starting transfers between devices, packed_local(): lax.ppermute(packed[k], ('tm', 'pix'), [(i, i ^ k) for i in range(2 * n_p...  26 us
    pallas_call x2, Pallas kernels, packed_local(): pl.pallas_call(functools.partial(pack_kernel, n_pix, messages), out_shape...  4.85 us
    unnamed x16, local copies, waits for them, and re-layouts  4.22 us
    pallas_call x1, Pallas kernels, packed_local(): pl.pallas_call(functools.partial(gram_kernel, n_pix, per_device, levels),...  3.72 us
  transfers between devices with their start and end apart: 17, of which 7 were waited for; matrix products, arithmetic and copies ran while one was open for 0% of the time, Pallas kernels for 2%

profile of v2, /device:TPU:0, one launch (start us, length us, event | category | flops | bytes accessed | tf_op | source)
XLA Modules:
  0.0 73.1 jit_solution(13184159298730373162)
XLA Ops:
  0.1 1.6 %copy-done = bf16[2,256,2048]{2,1,0:T(8,128)(2,1)S(1)} copy-done((bf16[2,256,2048]{2,1,0:T(8,128)(2,1)S(1)}, bf16[2,256,2048]{2,1,0:T(8,128)(2,1)}, u32[]{:S(2)}) %copy-start) | copy-done | bytes 2097176
  1.7 1.0 %copy-done.1 = bf16[4,256,256]{2,1,0:T(8,128)(2,1)S(1)} copy-done((bf16[4,256,256]{2,1,0:T(8,128)(2,1)S(1)}, bf16[4,256,256]{2,1,0:T(8,128)(2,1)}, u32[]{:S(2)}) %copy-start.1) | copy-done | bytes 524312
  2.7 3.3 %pack.2 = (bf16[576,128]{1,0:T(8,128)(2,1)S(1)}, bf16[576,128]{1,0:T(8,128)(2,1)S(1)}, bf16[576,128]{1,0:T(8,128)(2,1)S(1)}, bf16[576,128]{1,0:T(8,128)(2,1)S(1)...) custom-call(s32[2]{0:T(128)S(1)} %pad_add_fusion.place, ...), custom_call_target="tpu_custom_call" | custom-call | tf_op jit(solution)/shard_map/pack/pallas_call | solution.py:180
  6.1 2.5 %collective-permute-start.10 = (bf16[576,128]{1,0:T(8,128)(2,1)S(1)}, bf16[576,128]{1,0:T(8,128)(2,1)S(1)}, u32[]{:S(2)}, u32[]{:S(2)}) collective-permute-start(bf16[576,128]{1,0:T(8,128)(2,1)S(1)} %get-tuple-element.31), channel_id=1, source_target_pairs={{0,10},{1,11},{2,8},{3,9},{4,14},{5,15},{6,12},{7,13},{8,2},{9,3},... | collective-permute-start | bytes 442376 | tf_op jit(solution)/shard_map/ppermute | solution.py:197
  8.6 1.7 %collective-permute-start.11 = (bf16[576,128]{1,0:T(8,128)(2,1)S(1)}, bf16[576,128]{1,0:T(8,128)(2,1)S(1)}, u32[]{:S(2)}, u32[]{:S(2)}) collective-permute-start(bf16[576,128]{1,0:T(8,128)(2,1)S(1)} %get-tuple-element.32), channel_id=1, source_target_pairs={{0,11},{1,10},{2,9},{3,8},{4,15},{5,14},{6,13},{7,12},{8,3},{9,2},... | collective-permute-start | bytes 442376 | tf_op jit(solution)/shard_map/ppermute | solution.py:197
  10.3 2.2 %collective-permute-start.12 = (bf16[576,128]{1,0:T(8,128)(2,1)S(1)}, bf16[576,128]{1,0:T(8,128)(2,1)S(1)}, u32[]{:S(2)}, u32[]{:S(2)}) collective-permute-start(bf16[576,128]{1,0:T(8,128)(2,1)S(1)} %get-tuple-element.33), channel_id=1, source_target_pairs={{0,12},{1,13},{2,14},{3,15},{4,8},{5,9},{6,10},{7,11},{8,4},{9,5},... | collective-permute-start | bytes 442376 | tf_op jit(solution)/shard_map/ppermute | solution.py:197
  13.0 0.8 %collective-permute-done.other_index = s32[16]{0:T(128)S(1)} collective-permute-done((s32[16]{0:T(128)S(1)}, s32[16]{0:T(128)S(1)}, u32[]{:S(2)}, u32[]{:S(2)}) %collective-permute-start) | collective-permute-done | bytes 96 | tf_op jit(solution)/shard_map/ppermute | solution.py:200
  13.8 2.8 %collective-permute-start.14 = (bf16[576,128]{1,0:T(8,128)(2,1)S(1)}, bf16[576,128]{1,0:T(8,128)(2,1)S(1)}, u32[]{:S(2)}, u32[]{:S(2)}) collective-permute-start(bf16[576,128]{1,0:T(8,128)(2,1)S(1)} %get-tuple-element.35), channel_id=1, source_target_pairs={{0,14},{1,15},{2,12},{3,13},{4,10},{5,11},{6,8},{7,9},{8,6},{9,7},... | collective-permute-start | bytes 442376 | tf_op jit(solution)/shard_map/ppermute | solution.py:197
  16.6 5.0 %collective-permute-start.15 = (bf16[576,128]{1,0:T(8,128)(2,1)S(1)}, bf16[576,128]{1,0:T(8,128)(2,1)S(1)}, u32[]{:S(2)}, u32[]{:S(2)}) collective-permute-start(bf16[576,128]{1,0:T(8,128)(2,1)S(1)} %get-tuple-element.36), channel_id=1, source_target_pairs={{0,15},{1,14},{2,13},{3,12},{4,11},{5,10},{6,9},{7,8},{8,7},{9,6},... | collective-permute-start | bytes 442376 | tf_op jit(solution)/shard_map/ppermute | solution.py:197
  21.6 1.4 %collective-permute-done.11.refs_11_ = bf16[576,128]{1,0:T(8,128)(2,1)S(1)} collective-permute-done((bf16[576,128]{1,0:T(8,128)(2,1)S(1)}, bf16[576,128]{1,0:T(8,128)(2,1)S(1)}, u32[]{:S(2)}, u32[]{:S(2)}) %collective-permute-start.11) | collective-permute-done | bytes 147488 | tf_op jit(solution)/shard_map/ppermute | solution.py:197
  23.6 9.9 %collective-permute-done.13.refs_13_ = bf16[576,128]{1,0:T(8,128)(2,1)S(1)} collective-permute-done((bf16[576,128]{1,0:T(8,128)(2,1)S(1)}, bf16[576,128]{1,0:T(8,128)(2,1)S(1)}, u32[]{:S(2)}, u32[]{:S(2)}) %collective-permute-start.13) | collective-permute-done | bytes 147488 | tf_op jit(solution)/shard_map/ppermute | solution.py:197
  33.5 1.7 %collective-permute-start.5 = (bf16[576,128]{1,0:T(8,128)(2,1)S(1)}, bf16[576,128]{1,0:T(8,128)(2,1)S(1)}, u32[]{:S(2)}, u32[]{:S(2)}) collective-permute-start(bf16[576,128]{1,0:T(8,128)(2,1)S(1)} %get-tuple-element.26), channel_id=1, source_target_pairs={{0,5},{1,4},{2,7},{3,6},{4,1},{5,0},{6,3},{7,2},{8,13},{9,12},{10,... | collective-permute-start | bytes 442376 | tf_op jit(solution)/shard_map/ppermute | solution.py:197
  35.2 1.6 %collective-permute-start.6 = (bf16[576,128]{1,0:T(8,128)(2,1)S(1)}, bf16[576,128]{1,0:T(8,128)(2,1)S(1)}, u32[]{:S(2)}, u32[]{:S(2)}) collective-permute-start(bf16[576,128]{1,0:T(8,128)(2,1)S(1)} %get-tuple-element.27), channel_id=1, source_target_pairs={{0,6},{1,7},{2,4},{3,5},{4,2},{5,3},{6,0},{7,1},{8,14},{9,15},{10,... | collective-permute-start | bytes 442376 | tf_op jit(solution)/shard_map/ppermute | solution.py:197
  36.8 1.5 %pack.3 = (bf16[576,128]{1,0:T(8,128)(2,1)}, bf16[576,128]{1,0:T(8,128)(2,1)}) custom-call(s32[2]{0:T(128)S(1)} %pad_add_fusion.place, bf16[2,8,2,16,2048]{4,3,2,1,0:T(8,128)(2,1)S(1)} %bitcast.5, bf16[4,8,2,16,256]{4,3,2,1,0:T(8,128)(2,1)S(1)} %bitcast.7), custom_call_target="tpu_custom_call" | custom-call | tf_op jit(solution)/shard_map/pack/pallas_call | solution.py:180
  38.3 1.0 %collective-permute-start.7 = (bf16[576,128]{1,0:T(8,128)(2,1)}, bf16[576,128]{1,0:T(8,128)(2,1)S(1)}, u32[]{:S(2)}, u32[]{:S(2)}) collective-permute-start(bf16[576,128]{1,0:T(8,128)(2,1)} %get-tuple-element.28), channel_id=1, source_target_pairs={{0,7},{1,6},{2,5},{3,4},{4,3},{5,2},{6,1},{7,0},{8,15},{9,14},{10,... | collective-permute-start | bytes 442376 | tf_op jit(solution)/shard_map/ppermute | solution.py:197
  39.4 2.8 %collective-permute-start.9 = (bf16[576,128]{1,0:T(8,128)(2,1)}, bf16[576,128]{1,0:T(8,128)(2,1)S(1)}, u32[]{:S(2)}, u32[]{:S(2)}) collective-permute-start(bf16[576,128]{1,0:T(8,128)(2,1)} %get-tuple-element.30), channel_id=1, source_target_pairs={{0,9},{1,8},{2,11},{3,10},{4,13},{5,12},{6,15},{7,14},{8,1},{9,0},... | collective-permute-start | bytes 442376 | tf_op jit(solution)/shard_map/ppermute | solution.py:197
  42.2 11.7 %collective-permute-done.5.refs_5_ = bf16[576,128]{1,0:T(8,128)(2,1)S(1)} collective-permute-done((bf16[576,128]{1,0:T(8,128)(2,1)S(1)}, bf16[576,128]{1,0:T(8,128)(2,1)S(1)}, u32[]{:S(2)}, u32[]{:S(2)}) %collective-permute-start.5) | collective-permute-done | bytes 147488 | tf_op jit(solution)/shard_map/ppermute | solution.py:197
  54.4 3.6 %collective-permute-start.4 = (bf16[576,128]{1,0:T(8,128)(2,1)}, bf16[576,128]{1,0:T(8,128)(2,1)S(1)}, u32[]{:S(2)}, u32[]{:S(2)}) collective-permute-start(bf16[576,128]{1,0:T(8,128)(2,1)} %get-tuple-element.25), channel_id=1, source_target_pairs={{0,4},{1,5},{2,6},{3,7},{4,0},{5,1},{6,2},{7,3},{8,12},{9,13},{10,... | collective-permute-start | bytes 442376 | tf_op jit(solution)/shard_map/ppermute | solution.py:197
  58.2 1.3 %collective-permute-done.1.refs_1_ = bf16[576,128]{1,0:T(8,128)(2,1)S(1)} collective-permute-done((bf16[576,128]{1,0:T(8,128)(2,1)}, bf16[576,128]{1,0:T(8,128)(2,1)S(1)}, u32[]{:S(2)}, u32[]{:S(2)}) %collective-permute-start.1) | collective-permute-done | bytes 147488 | tf_op jit(solution)/shard_map/ppermute | solution.py:197
  59.5 6.0 %collective-permute-done.4.refs_4_ = bf16[576,128]{1,0:T(8,128)(2,1)S(1)} collective-permute-done((bf16[576,128]{1,0:T(8,128)(2,1)}, bf16[576,128]{1,0:T(8,128)(2,1)S(1)}, u32[]{:S(2)}, u32[]{:S(2)}) %collective-permute-start.4) | collective-permute-done | bytes 147488 | tf_op jit(solution)/shard_map/ppermute | solution.py:197
  66.2 0.9 %copy-done.5 = bf16[576,128]{1,0:T(8,128)(2,1)S(1)} copy-done((bf16[576,128]{1,0:T(8,128)(2,1)S(1)}, bf16[576,128]{1,0:T(8,128)(2,1)}, u32[]{:S(2)}) %copy-start.5) | copy-done | bytes 147480
  67.2 3.7 %gram.1 = f32[16,32,32]{2,1,0:T(8,128)S(1)} custom-call(s32[2]{0:T(128)S(1)} %pad_add_fusion.place, s32[16]{0:T(128)S(1)} %copy-done.6, s32[16]{0:T(128)S(1)} %collective-permute-done.other_index, s32[16,128]{1,0:T(8,128)S(1)} %broadcast_in_dim.2.counts_col, f32[1,512]{1,0:T(1,128)S(1)} %broadcast_in_dim_tile.3.counts_row, bf16[512,512]{1,0:T(8,128)(2,1)S(1)} %copy-done.2, ...), custom_call_target="tpu_custom_call" | custom-call | tf_op jit(solution)/shard_map/gram/pallas_call | solution.py:209
  71.0 1.3 %collective-permute-done.16 = f32[16,16,32]{2,1,0:T(8,128)S(1)} collective-permute-done((f32[16,16,32]{2,1,0:T(8,128)S(1)}, f32[16,16,32]{2,1,0:T(8,128)S(1)}, u32[]{:S(2)}, u32[]{:S(2)}) %collective-permute-start.16) | collective-permute-done | bytes 32800 | tf_op jit(solution)/shard_map/ppermute | solution.py:223
  72.4 0.7 pad_maximum_fusion
  (37 shorter events, 2.7 us)
Async XLA Ops:
  0.0 12.5 %copy-start.6 = (s32[16]{0:T(128)S(1)}, s32[16]{0:T(128)}, u32[]{:S(2)}) copy-start(s32[16]{0:T(128)} %own_index.1) | copy-start | bytes 196
  0.1 1.6 %copy-start = (bf16[2,256,2048]{2,1,0:T(8,128)(2,1)S(1)}, bf16[2,256,2048]{2,1,0:T(8,128)(2,1)}, u32[]{:S(2)}) copy-start(bf16[2,256,2048]{2,1,0:T(8,128)(2,1)} %param.6) | copy-start | bytes 6291460
  1.7 1.0 %copy-start.1 = (bf16[4,256,256]{2,1,0:T(8,128)(2,1)S(1)}, bf16[4,256,256]{2,1,0:T(8,128)(2,1)}, u32[]{:S(2)}) copy-start(bf16[4,256,256]{2,1,0:T(8,128)(2,1)} %param.7) | copy-start | bytes 1572868
  2.7 55.3 %copy-start.7 = (s32[256]{0:T(256)S(1)}, s32[256]{0:T(256)}, u32[]{:S(2)}) copy-start(s32[256]{0:T(256)} %param.9) | copy-start | bytes 3076
  2.7 63.5 %copy-start.2 = (bf16[512,512]{1,0:T(8,128)(2,1)S(1)}, bf16[512,512]{1,0:T(8,128)(2,1)}, u32[]{:S(2)}) copy-start(bf16[512,512]{1,0:T(8,128)(2,1)} %constant.25.clone.repeat) | copy-start | bytes 1572868
  2.7 63.5 %copy-start.3 = (bf16[512,512]{1,0:T(8,128)(2,1)S(1)}, bf16[512,512]{1,0:T(8,128)(2,1)}, u32[]{:S(2)}) copy-start(bf16[512,512]{1,0:T(8,128)(2,1)} %constant.26.clone.reorder) | copy-start | bytes 1572868
  6.1 10.5 %collective-permute-start.10 = (bf16[576,128]{1,0:T(8,128)(2,1)S(1)}, bf16[576,128]{1,0:T(8,128)(2,1)S(1)}, u32[]{:S(2)}, u32[]{:S(2)}) collective-permute-start(bf16[576,128]{1,0:T(8,128)(2,1)S(1)} %get-tuple-element.31), channel_id=1, source_target_pairs={{0,10},{1,11},{2,8},{3,9},{4,14},{5,15},{6,12},{7,13},{8,2},{9,3},... | collective-permute-start | bytes 442376 | tf_op jit(solution)/shard_map/ppermute | solution.py:197
  8.6 14.4 %collective-permute-start.11 = (bf16[576,128]{1,0:T(8,128)(2,1)S(1)}, bf16[576,128]{1,0:T(8,128)(2,1)S(1)}, u32[]{:S(2)}, u32[]{:S(2)}) collective-permute-start(bf16[576,128]{1,0:T(8,128)(2,1)S(1)} %get-tuple-element.32), channel_id=1, source_target_pairs={{0,11},{1,10},{2,9},{3,8},{4,15},{5,14},{6,13},{7,12},{8,3},{9,2},... | collective-permute-start | bytes 442376 | tf_op jit(solution)/shard_map/ppermute | solution.py:197
  10.3 12.7 %collective-permute-start.12 = (bf16[576,128]{1,0:T(8,128)(2,1)S(1)}, bf16[576,128]{1,0:T(8,128)(2,1)S(1)}, u32[]{:S(2)}, u32[]{:S(2)}) collective-permute-start(bf16[576,128]{1,0:T(8,128)(2,1)S(1)} %get-tuple-element.33), channel_id=1, source_target_pairs={{0,12},{1,13},{2,14},{3,15},{4,8},{5,9},{6,10},{7,11},{8,4},{9,5},... | collective-permute-start | bytes 442376 | tf_op jit(solution)/shard_map/ppermute | solution.py:197
  12.5 1.3 %collective-permute-start = (s32[16]{0:T(128)S(1)}, s32[16]{0:T(128)S(1)}, u32[]{:S(2)}, u32[]{:S(2)}) collective-permute-start(s32[16]{0:T(128)S(1)} %copy-done.6), channel_id=1, source_target_pairs={{0,8},{8,0},{1,9},{9,1},{2,10},{10,2},{3,11},{11,3},{4,12},{12,4},... | collective-permute-start | bytes 200 | tf_op jit(solution)/shard_map/ppermute | solution.py:200
  13.0 20.5 %collective-permute-start.13 = (bf16[576,128]{1,0:T(8,128)(2,1)S(1)}, bf16[576,128]{1,0:T(8,128)(2,1)S(1)}, u32[]{:S(2)}, u32[]{:S(2)}) collective-permute-start(bf16[576,128]{1,0:T(8,128)(2,1)S(1)} %get-tuple-element.34), channel_id=1, source_target_pairs={{0,13},{1,12},{2,15},{3,14},{4,9},{5,8},{6,11},{7,10},{8,5},{9,4},... | collective-permute-start | bytes 442376 | tf_op jit(solution)/shard_map/ppermute | solution.py:197
  13.8 21.4 %collective-permute-start.14 = (bf16[576,128]{1,0:T(8,128)(2,1)S(1)}, bf16[576,128]{1,0:T(8,128)(2,1)S(1)}, u32[]{:S(2)}, u32[]{:S(2)}) collective-permute-start(bf16[576,128]{1,0:T(8,128)(2,1)S(1)} %get-tuple-element.35), channel_id=1, source_target_pairs={{0,14},{1,15},{2,12},{3,13},{4,10},{5,11},{6,8},{7,9},{8,6},{9,7},... | collective-permute-start | bytes 442376 | tf_op jit(solution)/shard_map/ppermute | solution.py:197
  16.6 21.8 %collective-permute-start.15 = (bf16[576,128]{1,0:T(8,128)(2,1)S(1)}, bf16[576,128]{1,0:T(8,128)(2,1)S(1)}, u32[]{:S(2)}, u32[]{:S(2)}) collective-permute-start(bf16[576,128]{1,0:T(8,128)(2,1)S(1)} %get-tuple-element.36), channel_id=1, source_target_pairs={{0,15},{1,14},{2,13},{3,12},{4,11},{5,10},{6,9},{7,8},{8,7},{9,6},... | collective-permute-start | bytes 442376 | tf_op jit(solution)/shard_map/ppermute | solution.py:197
  23.0 16.4 %collective-permute-start.2 = (bf16[576,128]{1,0:T(8,128)(2,1)S(1)}, bf16[576,128]{1,0:T(8,128)(2,1)S(1)}, u32[]{:S(2)}, u32[]{:S(2)}) collective-permute-start(bf16[576,128]{1,0:T(8,128)(2,1)S(1)} %get-tuple-element.23), channel_id=1, source_target_pairs={{0,2},{1,3},{2,0},{3,1},{4,6},{5,7},{6,4},{7,5},{8,10},{9,11},{10,... | collective-permute-start | bytes 442376 | tf_op jit(solution)/shard_map/ppermute | solution.py:197
  23.0 16.4 %collective-permute-start.3 = (bf16[576,128]{1,0:T(8,128)(2,1)S(1)}, bf16[576,128]{1,0:T(8,128)(2,1)S(1)}, u32[]{:S(2)}, u32[]{:S(2)}) collective-permute-start(bf16[576,128]{1,0:T(8,128)(2,1)S(1)} %get-tuple-element.24), channel_id=1, source_target_pairs={{0,3},{1,2},{2,1},{3,0},{4,7},{5,6},{6,5},{7,4},{8,11},{9,10},{10,... | collective-permute-start | bytes 442376 | tf_op jit(solution)/shard_map/ppermute | solution.py:197
  33.5 20.3 %collective-permute-start.5 = (bf16[576,128]{1,0:T(8,128)(2,1)S(1)}, bf16[576,128]{1,0:T(8,128)(2,1)S(1)}, u32[]{:S(2)}, u32[]{:S(2)}) collective-permute-start(bf16[576,128]{1,0:T(8,128)(2,1)S(1)} %get-tuple-element.26), channel_id=1, source_target_pairs={{0,5},{1,4},{2,7},{3,6},{4,1},{5,0},{6,3},{7,2},{8,13},{9,12},{10,... | collective-permute-start | bytes 442376 | tf_op jit(solution)/shard_map/ppermute | solution.py:197
  35.2 19.2 %collective-permute-start.6 = (bf16[576,128]{1,0:T(8,128)(2,1)S(1)}, bf16[576,128]{1,0:T(8,128)(2,1)S(1)}, u32[]{:S(2)}, u32[]{:S(2)}) collective-permute-start(bf16[576,128]{1,0:T(8,128)(2,1)S(1)} %get-tuple-element.27), channel_id=1, source_target_pairs={{0,6},{1,7},{2,4},{3,5},{4,2},{5,3},{6,0},{7,1},{8,14},{9,15},{10,... | collective-permute-start | bytes 442376 | tf_op jit(solution)/shard_map/ppermute | solution.py:197
  38.3 19.9 %collective-permute-start.7 = (bf16[576,128]{1,0:T(8,128)(2,1)}, bf16[576,128]{1,0:T(8,128)(2,1)S(1)}, u32[]{:S(2)}, u32[]{:S(2)}) collective-permute-start(bf16[576,128]{1,0:T(8,128)(2,1)} %get-tuple-element.28), channel_id=1, source_target_pairs={{0,7},{1,6},{2,5},{3,4},{4,3},{5,2},{6,1},{7,0},{8,15},{9,14},{10,... | collective-permute-start | bytes 442376 | tf_op jit(solution)/shard_map/ppermute | solution.py:197
  39.4 18.8 %collective-permute-start.8 = (bf16[576,128]{1,0:T(8,128)(2,1)}, bf16[576,128]{1,0:T(8,128)(2,1)S(1)}, u32[]{:S(2)}, u32[]{:S(2)}) collective-permute-start(bf16[576,128]{1,0:T(8,128)(2,1)} %get-tuple-element.29), channel_id=1, source_target_pairs={{0,8},{1,9},{2,10},{3,11},{4,12},{5,13},{6,14},{7,15},{8,0},{9,1},... | collective-permute-start | bytes 442376 | tf_op jit(solution)/shard_map/ppermute | solution.py:197
  39.4 18.8 %collective-permute-start.9 = (bf16[576,128]{1,0:T(8,128)(2,1)}, bf16[576,128]{1,0:T(8,128)(2,1)S(1)}, u32[]{:S(2)}, u32[]{:S(2)}) collective-permute-start(bf16[576,128]{1,0:T(8,128)(2,1)} %get-tuple-element.30), channel_id=1, source_target_pairs={{0,9},{1,8},{2,11},{3,10},{4,13},{5,12},{6,15},{7,14},{8,1},{9,0},... | collective-permute-start | bytes 442376 | tf_op jit(solution)/shard_map/ppermute | solution.py:197
  53.8 5.7 %collective-permute-start.1 = (bf16[576,128]{1,0:T(8,128)(2,1)}, bf16[576,128]{1,0:T(8,128)(2,1)S(1)}, u32[]{:S(2)}, u32[]{:S(2)}) collective-permute-start(bf16[576,128]{1,0:T(8,128)(2,1)} %get-tuple-element.22), channel_id=1, source_target_pairs={{0,1},{1,0},{2,3},{3,2},{4,5},{5,4},{6,7},{7,6},{8,9},{9,8},{10,11... | collective-permute-start | bytes 442376 | tf_op jit(solution)/shard_map/ppermute | solution.py:197
  54.4 11.1 %collective-permute-start.4 = (bf16[576,128]{1,0:T(8,128)(2,1)}, bf16[576,128]{1,0:T(8,128)(2,1)S(1)}, u32[]{:S(2)}, u32[]{:S(2)}) collective-permute-start(bf16[576,128]{1,0:T(8,128)(2,1)} %get-tuple-element.25), channel_id=1, source_target_pairs={{0,4},{1,5},{2,6},{3,7},{4,0},{5,1},{6,2},{7,3},{8,12},{9,13},{10,... | collective-permute-start | bytes 442376 | tf_op jit(solution)/shard_map/ppermute | solution.py:197
  66.2 0.9 %copy-start.5 = (bf16[576,128]{1,0:T(8,128)(2,1)S(1)}, bf16[576,128]{1,0:T(8,128)(2,1)}, u32[]{:S(2)}) copy-start(bf16[576,128]{1,0:T(8,128)(2,1)} %copy-done.4) | copy-start | bytes 442372
  70.9 1.4 %collective-permute-start.16 = (f32[16,16,32]{2,1,0:T(8,128)S(1)}, f32[16,16,32]{2,1,0:T(8,128)S(1)}, u32[]{:S(2)}, u32[]{:S(2)}) collective-permute-start(f32[16,16,32]{2,1,0:T(8,128)S(1)} %constant_dynamic-slice_fusion), channel_id=1, source_target_pairs={{0,8},{8,0},{1,9},{9,1},{2,10},{10,2},{3,11},{11,3},{4,12},{12,4},... | collective-permute-start | bytes 98312 | tf_op jit(solution)/shard_map/ppermute | solution.py:223
  (1 other events, 0.7 us)

commit v3 on v2

--- a/solution.py
+++ b/solution.py
@@ -2,7 +2,6 @@
 
 import jax
 import jax.numpy as jnp
-import numpy as np
 from jax import lax
 from jax.experimental import pallas as pl
 from jax.experimental.pallas import tpu as pltpu
@@ -10,8 +9,7 @@
 
 LANES = 128
 ROWS = 16
-FIRST = 2
-VMEM_LIMIT = 48 * 1024 * 1024
+VMEM_LIMIT = 16 * 1024 * 1024
 
 
 def subtract_dark(raw_frames, dark_frames, dark_index, live_slot):
@@ -91,9 +89,9 @@
     return sum(jnp.dot(part, chosen, preferred_element_type=jnp.float32) for part in split3(x))
 
 
-def gram_kernel(n_pix, per_device, levels, place, own_index, other_index, counts_col, counts_row, repeat, reorder, *refs):
+def gram_kernel(n_pix, per_device, levels, order, place, own_index, other_index, cycle_counts, *refs):
     n_bufs = 2 * n_pix
-    bufs, (out, signal, dark) = refs[:n_bufs], refs[n_bufs:]
+    bufs, (mine, theirs, signal, dark) = dict(zip(order, refs)), refs[n_bufs:]
     me, core = place[0], place[1]
     share = levels // 2
     frames_half = per_device * n_pix
@@ -102,8 +100,12 @@
     tiles = slots // LANES
     dark_tiles = tiles // n_pix
     dark_row = per_device * tiles * ROWS
-    counts = counts_col[...]
     lane = lax.broadcasted_iota(jnp.int32, (ROWS, LANES), 1)
+    cycle = lax.broadcasted_iota(jnp.int32, (ROWS, LANES), 0)
+    counts = jnp.zeros((ROWS, LANES), jnp.int32)
+    for q in range(ROWS):
+        count = cycle_counts[(2 * me + core) * ROWS + q]
+        counts = jnp.where(cycle == q, count, counts)
     live = [lane + j * LANES < counts for j in range(tiles)]
     for k in range(n_bufs):
         source, half = me ^ (k % n_pix), core ^ (k // n_pix)
@@ -119,7 +121,7 @@
         index = own_index if k < n_pix else other_index
         for f in range(per_device):
             frame = source * per_device + f
-            first = pl.multiple_of((half * frames_half + frame) * ROWS, ROWS)
+            first = pl.multiple_of(((k // n_pix) * frames_half + frame) * ROWS, ROWS)
             dark_first = pl.multiple_of(index[frame] * ROWS, ROWS)
             for j in range(tiles):
                 raw = bufs[k][pl.ds((f * tiles + j) * ROWS, ROWS), :].astype(jnp.float32)
@@ -132,23 +134,23 @@
     totals = lax.dot_general(
         jnp.ones((ROWS, slots), jnp.bfloat16), every, contract, preferred_element_type=jnp.float32
     )
-    same = (
-        lax.broadcasted_iota(jnp.int32, (ROWS, width), 0)
-        == lax.broadcasted_iota(jnp.int32, (ROWS, width), 1) % ROWS
-    )
     products = lax.dot_general(every, every, contract, preferred_element_type=jnp.float32)
-    products = products.reshape(n_frames, ROWS, width)
-    gram = jnp.sum(jnp.where(same[None], products, 0.0), axis=1)
-    mine = (
-        lax.broadcasted_iota(jnp.int32, (n_frames, width), 0)
-        == lax.broadcasted_iota(jnp.int32, (n_frames, width), 1) // ROWS
-    )
-    col_totals = totals[0:1, :]
-    row_totals = pick(jnp.where(mine, col_totals, 0.0), repeat[...])
-    ratio = gram * counts_row[...] / (row_totals * col_totals)
-    ordered = pick(ratio, reorder[...])
-    for q in range(ROWS):
-        out[q] = ordered[:, q * n_frames : (q + 1) * n_frames]
+    products = jnp.concatenate([products, totals], axis=0)
+    row = lax.broadcasted_iota(jnp.int32, products.shape, 0)
+    col = lax.broadcasted_iota(jnp.int32, products.shape, 1)
+    products = jnp.where(row % ROWS == col % ROWS, products, 0.0)
+    frame = lax.broadcasted_iota(jnp.int32, (width, LANES), 0) // ROWS
+    lane = lax.broadcasted_iota(jnp.int32, (width, LANES), 1)
+    place_out = (frame + core * frames_half) % n_frames
+    fold = jnp.where((lane == place_out) | (lane == frame + n_frames), 1.0, 0.0)
+    folded = pick(products, fold.astype(jnp.bfloat16))
+    totals = folded[width:]
+    counts = counts.astype(jnp.float32)[:, :n_frames]
+    for t in range(n_frames):
+        scale = totals[:, n_frames + t : n_frames + t + 1] * totals[:, :n_frames]
+        block = folded[t * ROWS : (t + 1) * ROWS, :n_frames] * counts / scale
+        out = mine if t < frames_half else theirs
+        out[:, t % frames_half, :] = block
 
 
 def in_vmem(count):
@@ -165,8 +167,12 @@
     levels, _, dark_slots = dark.shape
     n_frames = 2 * per_device * n_pix
     swap = [(0, 1), (1, 0)]
-    split_frames = frames.reshape(per_device, n_pix, 2, ROWS, slots)
-    split_dark = dark.reshape(levels, n_pix, 2, ROWS, dark_slots)
+    split_frames = pltpu.with_memory_space_constraint(
+        frames.reshape(per_device, n_pix, 2, ROWS, slots), pltpu.HBM
+    )
+    split_dark = pltpu.with_memory_space_constraint(
+        dark.reshape(levels, n_pix, 2, ROWS, dark_slots), pltpu.HBM
+    )
     share = levels // 2
     place = jnp.stack([me, core]).astype(jnp.int32)
     rows = (per_device * slots + share * dark_slots) // LANES * ROWS
@@ -174,55 +180,42 @@
     far = [t * n_pix + k for t in range(2) for k in range(half, n_pix)]
     near = [t * n_pix + k for t in range(2) for k in range(1, half)] + [n_pix]
     order = [k for pair in zip(far, near) for k in pair] + far[len(near) :]
-    packed = {}
-    for messages in (order[:FIRST], order[FIRST:] + [0]):
-        count = len(messages)
-        buffers = pl.pallas_call(
-            functools.partial(pack_kernel, n_pix, messages),
-            out_shape=[jax.ShapeDtypeStruct((rows, LANES), frames.dtype)] * count,
-            in_specs=in_smem(1) + [pl.BlockSpec(memory_space=pl.ANY)] * 2,
-            out_specs=in_vmem(count),
-            scratch_shapes=[
-                pltpu.VMEM((count, per_device, ROWS, slots), frames.dtype),
-                pltpu.VMEM((count, share, ROWS, dark_slots), dark.dtype),
-                pltpu.SemaphoreType.DMA((count,)),
-                pltpu.SemaphoreType.DMA((count,)),
-            ],
-            compiler_params=pltpu.CompilerParams(vmem_limit_bytes=VMEM_LIMIT),
-            name="pack",
-        )(place, split_frames, split_dark)
-        packed.update(zip(messages, buffers))
-    received = [packed[0]] + [None] * (2 * n_pix - 1)
-    for k in order:
-        received[k] = lax.ppermute(
-            packed[k], ("tm", "pix"), [(i, i ^ k) for i in range(2 * n_pix)]
-        )
+    messages = order + [0]
+    count = len(messages)
+    packed = pl.pallas_call(
+        functools.partial(pack_kernel, n_pix, messages),
+        out_shape=[jax.ShapeDtypeStruct((rows, LANES), frames.dtype)] * count,
+        in_specs=in_smem(1) + [pl.BlockSpec(memory_space=pltpu.HBM)] * 2,
+        out_specs=in_vmem(count),
+        scratch_shapes=[
+            pltpu.VMEM((count, per_device, ROWS, slots), frames.dtype),
+            pltpu.VMEM((count, share, ROWS, dark_slots), dark.dtype),
+            pltpu.SemaphoreType.DMA((count,)),
+            pltpu.SemaphoreType.DMA((count,)),
+        ],
+        compiler_params=pltpu.CompilerParams(vmem_limit_bytes=VMEM_LIMIT),
+        name="pack",
+    )(place, split_frames, split_dark)
+    received = [
+        lax.ppermute(buffer, ("tm", "pix"), [(i, i ^ k) for i in range(2 * n_pix)]) if k else buffer
+        for k, buffer in zip(messages, packed)
+    ]
     other_index = lax.ppermute(dark_index, "tm", swap)
-    counts = lax.dynamic_slice_in_dim(cycle_counts, (2 * me + core) * ROWS, ROWS, 0)
     width = n_frames * ROWS
-    counts_col = jnp.broadcast_to(counts[:, None], (ROWS, LANES))
-    counts_row = jnp.tile(counts.astype(jnp.float32), n_frames)[None]
-    index = np.arange(width)
-    cycle, frame = index % ROWS, index // ROWS
-    repeat = jnp.asarray(cycle[:, None] == cycle[None, :], jnp.bfloat16)
-    reorder = jnp.asarray((cycle * n_frames + frame)[:, None] == index[None, :], jnp.bfloat16)
-    blocks = pl.pallas_call(
-        functools.partial(gram_kernel, n_pix, per_device, levels),
-        out_shape=jax.ShapeDtypeStruct((ROWS, n_frames, n_frames), jnp.float32),
-        in_specs=in_smem(3) + in_vmem(4 + 2 * n_pix),
-        out_specs=in_vmem(1)[0],
+    blocks = jax.ShapeDtypeStruct((ROWS, n_frames // 2, n_frames), jnp.float32)
+    mine, send = pl.pallas_call(
+        functools.partial(gram_kernel, n_pix, per_device, levels, messages),
+        out_shape=[blocks, blocks],
+        in_specs=in_smem(4) + in_vmem(2 * n_pix),
+        out_specs=in_vmem(2),
         scratch_shapes=[
             pltpu.VMEM((width, slots), jnp.bfloat16),
             pltpu.VMEM((slots // LANES, levels * ROWS, LANES), jnp.float32),
         ],
         compiler_params=pltpu.CompilerParams(vmem_limit_bytes=VMEM_LIMIT),
         name="gram",
-    )(place, dark_index, other_index, counts_col, counts_row, repeat, reorder, *received)
-    n_half = n_frames // 2
-    mine = lax.dynamic_slice_in_dim(blocks, core * n_half, n_half, 1)
-    theirs = lax.ppermute(
-        lax.dynamic_slice_in_dim(blocks, (1 - core) * n_half, n_half, 1), "tm", swap
-    )
+    )(place, dark_index, other_index, cycle_counts, *received)
+    theirs = lax.ppermute(send, "tm", swap)
     lower = core == 0
     return jnp.concatenate(
         [jnp.where(lower, mine, theirs), jnp.where(lower, theirs, mine)], axis=0

time: 73.3 us -> 64.1 us (0.87)
  the two profiles are of different devices: /device:TPU:0 before, /device:TPU:17 now
where the time goes in v3:
time: 64.1 us; the launch traced here: 64 us
  waiting for transfers between devices  28.9 us (45%)
  starting transfers between devices  27.8 us (43%)
  Pallas kernels  6.43 us (10%)
  other arithmetic  0.82 us (1%)
    ppermute x15, waiting for transfers between devices, packed_local(): lax.ppermute(buffer, ('tm', 'pix'), [(i, i ^ k) for i in range(2 * n_pix)])  27.9 us
    ppermute x15, starting transfers between devices, packed_local(): lax.ppermute(buffer, ('tm', 'pix'), [(i, i ^ k) for i in range(2 * n_pix)])  25.8 us
    pallas_call x1, Pallas kernels, packed_local(): pl.pallas_call(functools.partial(gram_kernel, n_pix, per_device, levels,...  3.85 us
    pallas_call x1, Pallas kernels, packed_local(): pl.pallas_call(functools.partial(pack_kernel, n_pix, messages), out_shape...  2.58 us
    ppermute x1, starting transfers between devices, packed_local(): other_index = lax.ppermute(dark_index, 'tm', swap)  1.52 us
  transfers between devices with their start and end apart: 17, of which 8 were waited for; matrix products, arithmetic and copies ran while one was open for 0% of the time, Pallas kernels for 0%

profile of v3, /device:TPU:17, one launch (start us, length us, event | category | flops | bytes accessed | tf_op | source)
XLA Modules:
  0.0 64.0 jit_solution(16056518503780955375)
XLA Ops:
  0.0 0.1 pad_add_fusion.place
  0.1 2.6 %pack.1 = (bf16[576,128]{1,0:T(8,128)(2,1)S(1)}, bf16[576,128]{1,0:T(8,128)(2,1)S(1)}, bf16[576,128]{1,0:T(8,128)(2,1)S(1)}, bf16[576,128]{1,0:T(8,128)(2,1)S(1)...) custom-call(s32[2]{0:T(128)S(1)} %pad_add_fusion.place, ...), custom_call_target="tpu_custom_call" | custom-call | tf_op jit(solution)/shard_map/pack/pallas_call | solution.py:185
  2.7 0.1 collective-permute-start.1
  2.7 1.3 %collective-permute-start.2 = (bf16[576,128]{1,0:T(8,128)(2,1)S(1)}, bf16[576,128]{1,0:T(8,128)(2,1)S(1)}, u32[]{:S(2)}, u32[]{:S(2)}) collective-permute-start(bf16[576,128]{1,0:T(8,128)(2,1)S(1)} %get-tuple-element.24), channel_id=1, source_target_pairs={{0,1},{1,0},{2,3},{3,2},{4,5},{5,4},{6,7},{7,6},{8,9},{9,8},{10,11... | collective-permute-start | bytes 442376 | tf_op jit(solution)/shard_map/ppermute | solution.py:200
  4.1 2.2 %collective-permute-start.3 = (bf16[576,128]{1,0:T(8,128)(2,1)S(1)}, bf16[576,128]{1,0:T(8,128)(2,1)S(1)}, u32[]{:S(2)}, u32[]{:S(2)}) collective-permute-start(bf16[576,128]{1,0:T(8,128)(2,1)S(1)} %get-tuple-element.25), channel_id=1, source_target_pairs={{0,5},{1,4},{2,7},{3,6},{4,1},{5,0},{6,3},{7,2},{8,13},{9,12},{10,... | collective-permute-start | bytes 442376 | tf_op jit(solution)/shard_map/ppermute | solution.py:200
  6.3 1.5 %collective-permute-start = (s32[16]{0:T(128)S(1)}, s32[16]{0:T(128)S(1)}, u32[]{:S(2)}, u32[]{:S(2)}) collective-permute-start(s32[16]{0:T(128)S(1)} %copy-done.1), channel_id=1, source_target_pairs={{0,8},{8,0},{1,9},{9,1},{2,10},{10,2},{3,11},{11,3},{4,12},{12,4},... | collective-permute-start | bytes 200 | tf_op jit(solution)/shard_map/ppermute | solution.py:203
  7.8 1.3 %collective-permute-start.4 = (bf16[576,128]{1,0:T(8,128)(2,1)S(1)}, bf16[576,128]{1,0:T(8,128)(2,1)S(1)}, u32[]{:S(2)}, u32[]{:S(2)}) collective-permute-start(bf16[576,128]{1,0:T(8,128)(2,1)S(1)} %get-tuple-element.26), channel_id=1, source_target_pairs={{0,2},{1,3},{2,0},{3,1},{4,6},{5,7},{6,4},{7,5},{8,10},{9,11},{10,... | collective-permute-start | bytes 442376 | tf_op jit(solution)/shard_map/ppermute | solution.py:200
  9.1 1.5 %collective-permute-done.1.refs_0_ = bf16[576,128]{1,0:T(8,128)(2,1)S(1)} collective-permute-done((bf16[576,128]{1,0:T(8,128)(2,1)S(1)}, bf16[576,128]{1,0:T(8,128)(2,1)S(1)}, u32[]{:S(2)}, u32[]{:S(2)}) %collective-permute-start.1) | collective-permute-done | bytes 147488 | tf_op jit(solution)/shard_map/ppermute | solution.py:200
  10.6 8.3 %collective-permute-start.6 = (bf16[576,128]{1,0:T(8,128)(2,1)S(1)}, bf16[576,128]{1,0:T(8,128)(2,1)S(1)}, u32[]{:S(2)}, u32[]{:S(2)}) collective-permute-start(bf16[576,128]{1,0:T(8,128)(2,1)S(1)} %get-tuple-element.28), channel_id=1, source_target_pairs={{0,3},{1,2},{2,1},{3,0},{4,7},{5,6},{6,5},{7,4},{8,11},{9,10},{10,... | collective-permute-start | bytes 442376 | tf_op jit(solution)/shard_map/ppermute | solution.py:200
  19.0 3.2 %collective-permute-start.8 = (bf16[576,128]{1,0:T(8,128)(2,1)S(1)}, bf16[576,128]{1,0:T(8,128)(2,1)S(1)}, u32[]{:S(2)}, u32[]{:S(2)}) collective-permute-start(bf16[576,128]{1,0:T(8,128)(2,1)S(1)} %get-tuple-element.30), channel_id=1, source_target_pairs={{0,9},{1,8},{2,11},{3,10},{4,13},{5,12},{6,15},{7,14},{8,1},{9,0},... | collective-permute-start | bytes 442376 | tf_op jit(solution)/shard_map/ppermute | solution.py:200
  22.2 3.3 %collective-permute-start.9 = (bf16[576,128]{1,0:T(8,128)(2,1)S(1)}, bf16[576,128]{1,0:T(8,128)(2,1)S(1)}, u32[]{:S(2)}, u32[]{:S(2)}) collective-permute-start(bf16[576,128]{1,0:T(8,128)(2,1)S(1)} %get-tuple-element.31), channel_id=1, source_target_pairs={{0,12},{1,13},{2,14},{3,15},{4,8},{5,9},{6,10},{7,11},{8,4},{9,5},... | collective-permute-start | bytes 442376 | tf_op jit(solution)/shard_map/ppermute | solution.py:200
  25.5 6.1 %collective-permute-done.5.refs_4_ = bf16[576,128]{1,0:T(8,128)(2,1)S(1)} collective-permute-done((bf16[576,128]{1,0:T(8,128)(2,1)S(1)}, bf16[576,128]{1,0:T(8,128)(2,1)S(1)}, u32[]{:S(2)}, u32[]{:S(2)}) %collective-permute-start.5) | collective-permute-done | bytes 147488 | tf_op jit(solution)/shard_map/ppermute | solution.py:200
  31.6 1.5 %collective-permute-start.11 = (bf16[576,128]{1,0:T(8,128)(2,1)S(1)}, bf16[576,128]{1,0:T(8,128)(2,1)S(1)}, u32[]{:S(2)}, u32[]{:S(2)}) collective-permute-start(bf16[576,128]{1,0:T(8,128)(2,1)S(1)} %get-tuple-element.33), channel_id=1, source_target_pairs={{0,13},{1,12},{2,15},{3,14},{4,9},{5,8},{6,11},{7,10},{8,5},{9,4},... | collective-permute-start | bytes 442376 | tf_op jit(solution)/shard_map/ppermute | solution.py:200
  33.1 2.6 %collective-permute-done.7.refs_6_ = bf16[576,128]{1,0:T(8,128)(2,1)S(1)} collective-permute-done((bf16[576,128]{1,0:T(8,128)(2,1)S(1)}, bf16[576,128]{1,0:T(8,128)(2,1)S(1)}, u32[]{:S(2)}, u32[]{:S(2)}) %collective-permute-start.7) | collective-permute-done | bytes 147488 | tf_op jit(solution)/shard_map/ppermute | solution.py:200
  35.7 0.6 collective-permute-start.13
  36.4 1.6 %collective-permute-done.10.refs_9_ = bf16[576,128]{1,0:T(8,128)(2,1)S(1)} collective-permute-done((bf16[576,128]{1,0:T(8,128)(2,1)S(1)}, bf16[576,128]{1,0:T(8,128)(2,1)S(1)}, u32[]{:S(2)}, u32[]{:S(2)}) %collective-permute-start.10) | collective-permute-done | bytes 147488 | tf_op jit(solution)/shard_map/ppermute | solution.py:200
  38.0 3.8 %collective-permute-start.15 = (bf16[576,128]{1,0:T(8,128)(2,1)S(1)}, bf16[576,128]{1,0:T(8,128)(2,1)S(1)}, u32[]{:S(2)}, u32[]{:S(2)}) collective-permute-start(bf16[576,128]{1,0:T(8,128)(2,1)S(1)} %get-tuple-element.37), channel_id=1, source_target_pairs={{0,15},{1,14},{2,13},{3,12},{4,11},{5,10},{6,9},{7,8},{8,7},{9,6},... | collective-permute-start | bytes 442376 | tf_op jit(solution)/shard_map/ppermute | solution.py:200
  41.8 3.3 %collective-permute-done.12.refs_11_ = bf16[576,128]{1,0:T(8,128)(2,1)S(1)} collective-permute-done((bf16[576,128]{1,0:T(8,128)(2,1)S(1)}, bf16[576,128]{1,0:T(8,128)(2,1)S(1)}, u32[]{:S(2)}, u32[]{:S(2)}) %collective-permute-start.12) | collective-permute-done | bytes 147488 | tf_op jit(solution)/shard_map/ppermute | solution.py:200
  45.1 8.7 %collective-permute-done.13.refs_12_ = bf16[576,128]{1,0:T(8,128)(2,1)S(1)} collective-permute-done((bf16[576,128]{1,0:T(8,128)(2,1)S(1)}, bf16[576,128]{1,0:T(8,128)(2,1)S(1)}, u32[]{:S(2)}, u32[]{:S(2)}) %collective-permute-start.13) | collective-permute-done | bytes 147488 | tf_op jit(solution)/shard_map/ppermute | solution.py:200
  53.8 4.1 %collective-permute-done.15.refs_14_ = bf16[576,128]{1,0:T(8,128)(2,1)S(1)} collective-permute-done((bf16[576,128]{1,0:T(8,128)(2,1)S(1)}, bf16[576,128]{1,0:T(8,128)(2,1)S(1)}, u32[]{:S(2)}, u32[]{:S(2)}) %collective-permute-start.15) | collective-permute-done | bytes 147488 | tf_op jit(solution)/shard_map/ppermute | solution.py:200
  57.9 3.9 %gram.1 = (f32[16,16,32]{2,1,0:T(8,128)S(1)}, f32[16,16,32]{2,1,0:T(8,128)S(1)}) custom-call(s32[2]{0:T(128)S(1)} %pad_add_fusion.place, s32[16]{0:T(128)S(1)} %copy-done.1, s32[16]{0:T(128)S(1)} %collective-permute-done.other_index, s32[256]{0:T(256)S(1)} %copy-done, bf16[576,128]{1,0:T(8,128)(2,1)S(1)} %collective-permute-done.1.refs_0_, ...), custom_call_target="tpu_custom_call" | custom-call | tf_op jit(solution)/shard_map/gram/pallas_call | solution.py:206
  61.8 0.5 collective-permute-start.16
  62.2 1.0 %collective-permute-done.16 = f32[16,16,32]{2,1,0:T(8,128)S(1)} collective-permute-done((f32[16,16,32]{2,1,0:T(8,128)S(1)}, f32[16,16,32]{2,1,0:T(8,128)S(1)}, u32[]{:S(2)}, u32[]{:S(2)}) %collective-permute-start.16) | collective-permute-done | bytes 32800 | tf_op jit(solution)/shard_map/ppermute | solution.py:218
  63.2 0.7 %pad_maximum_fusion = f32[32,16,32]{2,1,0:T(8,128)} fusion(f32[16,16,32]{2,1,0:T(8,128)S(1)} %get-tuple-element.42, f32[16,16,32]{2,1,0:T(8,128)S(1)} %get-tuple-element.41), kind=kLoop, calls=%fused_computation | loop fusion | flops 16384 | bytes 131072 | tf_op jit(solution)/shard_map/concatenate | solution.py:220
  (19 shorter events, 0.1 us)
Async XLA Ops:
  0.0 6.3 %copy-start.1 = (s32[16]{0:T(128)S(1)}, s32[16]{0:T(128)}, u32[]{:S(2)}) copy-start(s32[16]{0:T(128)} %own_index.1) | copy-start | bytes 196
  0.0 57.9 %copy-start = (s32[256]{0:T(256)S(1)}, s32[256]{0:T(256)}, u32[]{:S(2)}) copy-start(s32[256]{0:T(256)} %cycle_counts.1) | copy-start | bytes 3076
  2.7 8.0 %collective-permute-start.1 = (bf16[576,128]{1,0:T(8,128)(2,1)S(1)}, bf16[576,128]{1,0:T(8,128)(2,1)S(1)}, u32[]{:S(2)}, u32[]{:S(2)}) collective-permute-start(bf16[576,128]{1,0:T(8,128)(2,1)S(1)} %get-tuple-element.23), channel_id=1, source_target_pairs={{0,4},{1,5},{2,6},{3,7},{4,0},{5,1},{6,2},{7,3},{8,12},{9,13},{10,... | collective-permute-start | bytes 442376 | tf_op jit(solution)/shard_map/ppermute | solution.py:200
  2.7 16.2 %collective-permute-start.2 = (bf16[576,128]{1,0:T(8,128)(2,1)S(1)}, bf16[576,128]{1,0:T(8,128)(2,1)S(1)}, u32[]{:S(2)}, u32[]{:S(2)}) collective-permute-start(bf16[576,128]{1,0:T(8,128)(2,1)S(1)} %get-tuple-element.24), channel_id=1, source_target_pairs={{0,1},{1,0},{2,3},{3,2},{4,5},{5,4},{6,7},{7,6},{8,9},{9,8},{10,11... | collective-permute-start | bytes 442376 | tf_op jit(solution)/shard_map/ppermute | solution.py:200
  4.1 14.9 %collective-permute-start.3 = (bf16[576,128]{1,0:T(8,128)(2,1)S(1)}, bf16[576,128]{1,0:T(8,128)(2,1)S(1)}, u32[]{:S(2)}, u32[]{:S(2)}) collective-permute-start(bf16[576,128]{1,0:T(8,128)(2,1)S(1)} %get-tuple-element.25), channel_id=1, source_target_pairs={{0,5},{1,4},{2,7},{3,6},{4,1},{5,0},{6,3},{7,2},{8,13},{9,12},{10,... | collective-permute-start | bytes 442376 | tf_op jit(solution)/shard_map/ppermute | solution.py:200
  6.3 2.8 %collective-permute-start = (s32[16]{0:T(128)S(1)}, s32[16]{0:T(128)S(1)}, u32[]{:S(2)}, u32[]{:S(2)}) collective-permute-start(s32[16]{0:T(128)S(1)} %copy-done.1), channel_id=1, source_target_pairs={{0,8},{8,0},{1,9},{9,1},{2,10},{10,2},{3,11},{11,3},{4,12},{12,4},... | collective-permute-start | bytes 200 | tf_op jit(solution)/shard_map/ppermute | solution.py:203
  7.8 14.4 %collective-permute-start.4 = (bf16[576,128]{1,0:T(8,128)(2,1)S(1)}, bf16[576,128]{1,0:T(8,128)(2,1)S(1)}, u32[]{:S(2)}, u32[]{:S(2)}) collective-permute-start(bf16[576,128]{1,0:T(8,128)(2,1)S(1)} %get-tuple-element.26), channel_id=1, source_target_pairs={{0,2},{1,3},{2,0},{3,1},{4,6},{5,7},{6,4},{7,5},{8,10},{9,11},{10,... | collective-permute-start | bytes 442376 | tf_op jit(solution)/shard_map/ppermute | solution.py:200
  9.1 22.5 %collective-permute-start.5 = (bf16[576,128]{1,0:T(8,128)(2,1)S(1)}, bf16[576,128]{1,0:T(8,128)(2,1)S(1)}, u32[]{:S(2)}, u32[]{:S(2)}) collective-permute-start(bf16[576,128]{1,0:T(8,128)(2,1)S(1)} %get-tuple-element.27), channel_id=1, source_target_pairs={{0,6},{1,7},{2,4},{3,5},{4,2},{5,3},{6,0},{7,1},{8,14},{9,15},{10,... | collective-permute-start | bytes 442376 | tf_op jit(solution)/shard_map/ppermute | solution.py:200
  10.6 20.9 %collective-permute-start.6 = (bf16[576,128]{1,0:T(8,128)(2,1)S(1)}, bf16[576,128]{1,0:T(8,128)(2,1)S(1)}, u32[]{:S(2)}, u32[]{:S(2)}) collective-permute-start(bf16[576,128]{1,0:T(8,128)(2,1)S(1)} %get-tuple-element.28), channel_id=1, source_target_pairs={{0,3},{1,2},{2,1},{3,0},{4,7},{5,6},{6,5},{7,4},{8,11},{9,10},{10,... | collective-permute-start | bytes 442376 | tf_op jit(solution)/shard_map/ppermute | solution.py:200
  19.0 16.7 %collective-permute-start.7 = (bf16[576,128]{1,0:T(8,128)(2,1)S(1)}, bf16[576,128]{1,0:T(8,128)(2,1)S(1)}, u32[]{:S(2)}, u32[]{:S(2)}) collective-permute-start(bf16[576,128]{1,0:T(8,128)(2,1)S(1)} %get-tuple-element.29), channel_id=1, source_target_pairs={{0,7},{1,6},{2,5},{3,4},{4,3},{5,2},{6,1},{7,0},{8,15},{9,14},{10,... | collective-permute-start | bytes 442376 | tf_op jit(solution)/shard_map/ppermute | solution.py:200
  19.0 16.7 %collective-permute-start.8 = (bf16[576,128]{1,0:T(8,128)(2,1)S(1)}, bf16[576,128]{1,0:T(8,128)(2,1)S(1)}, u32[]{:S(2)}, u32[]{:S(2)}) collective-permute-start(bf16[576,128]{1,0:T(8,128)(2,1)S(1)} %get-tuple-element.30), channel_id=1, source_target_pairs={{0,9},{1,8},{2,11},{3,10},{4,13},{5,12},{6,15},{7,14},{8,1},{9,0},... | collective-permute-start | bytes 442376 | tf_op jit(solution)/shard_map/ppermute | solution.py:200
  22.2 14.1 %collective-permute-start.9 = (bf16[576,128]{1,0:T(8,128)(2,1)S(1)}, bf16[576,128]{1,0:T(8,128)(2,1)S(1)}, u32[]{:S(2)}, u32[]{:S(2)}) collective-permute-start(bf16[576,128]{1,0:T(8,128)(2,1)S(1)} %get-tuple-element.31), channel_id=1, source_target_pairs={{0,12},{1,13},{2,14},{3,15},{4,8},{5,9},{6,10},{7,11},{8,4},{9,5},... | collective-permute-start | bytes 442376 | tf_op jit(solution)/shard_map/ppermute | solution.py:200
  31.6 6.4 %collective-permute-start.10 = (bf16[576,128]{1,0:T(8,128)(2,1)S(1)}, bf16[576,128]{1,0:T(8,128)(2,1)S(1)}, u32[]{:S(2)}, u32[]{:S(2)}) collective-permute-start(bf16[576,128]{1,0:T(8,128)(2,1)S(1)} %get-tuple-element.32), channel_id=1, source_target_pairs={{0,10},{1,11},{2,8},{3,9},{4,14},{5,15},{6,12},{7,13},{8,2},{9,3},... | collective-permute-start | bytes 442376 | tf_op jit(solution)/shard_map/ppermute | solution.py:200
  31.6 10.3 %collective-permute-start.11 = (bf16[576,128]{1,0:T(8,128)(2,1)S(1)}, bf16[576,128]{1,0:T(8,128)(2,1)S(1)}, u32[]{:S(2)}, u32[]{:S(2)}) collective-permute-start(bf16[576,128]{1,0:T(8,128)(2,1)S(1)} %get-tuple-element.33), channel_id=1, source_target_pairs={{0,13},{1,12},{2,15},{3,14},{4,9},{5,8},{6,11},{7,10},{8,5},{9,4},... | collective-permute-start | bytes 442376 | tf_op jit(solution)/shard_map/ppermute | solution.py:200
  35.7 9.4 %collective-permute-start.12 = (bf16[576,128]{1,0:T(8,128)(2,1)S(1)}, bf16[576,128]{1,0:T(8,128)(2,1)S(1)}, u32[]{:S(2)}, u32[]{:S(2)}) collective-permute-start(bf16[576,128]{1,0:T(8,128)(2,1)S(1)} %get-tuple-element.34), channel_id=1, source_target_pairs={{0,11},{1,10},{2,9},{3,8},{4,15},{5,14},{6,13},{7,12},{8,3},{9,2},... | collective-permute-start | bytes 442376 | tf_op jit(solution)/shard_map/ppermute | solution.py:200
  35.7 18.1 %collective-permute-start.13 = (bf16[576,128]{1,0:T(8,128)(2,1)S(1)}, bf16[576,128]{1,0:T(8,128)(2,1)S(1)}, u32[]{:S(2)}, u32[]{:S(2)}) collective-permute-start(bf16[576,128]{1,0:T(8,128)(2,1)S(1)} %get-tuple-element.35), channel_id=1, source_target_pairs={{0,14},{1,15},{2,12},{3,13},{4,10},{5,11},{6,8},{7,9},{8,6},{9,7},... | collective-permute-start | bytes 442376 | tf_op jit(solution)/shard_map/ppermute | solution.py:200
  36.3 17.5 %collective-permute-start.14 = (bf16[576,128]{1,0:T(8,128)(2,1)S(1)}, bf16[576,128]{1,0:T(8,128)(2,1)S(1)}, u32[]{:S(2)}, u32[]{:S(2)}) collective-permute-start(bf16[576,128]{1,0:T(8,128)(2,1)S(1)} %get-tuple-element.36), channel_id=1, source_target_pairs={{0,8},{1,9},{2,10},{3,11},{4,12},{5,13},{6,14},{7,15},{8,0},{9,1},... | collective-permute-start | bytes 442376 | tf_op jit(solution)/shard_map/ppermute | solution.py:200
  38.0 19.9 %collective-permute-start.15 = (bf16[576,128]{1,0:T(8,128)(2,1)S(1)}, bf16[576,128]{1,0:T(8,128)(2,1)S(1)}, u32[]{:S(2)}, u32[]{:S(2)}) collective-permute-start(bf16[576,128]{1,0:T(8,128)(2,1)S(1)} %get-tuple-element.37), channel_id=1, source_target_pairs={{0,15},{1,14},{2,13},{3,12},{4,11},{5,10},{6,9},{7,8},{8,7},{9,6},... | collective-permute-start | bytes 442376 | tf_op jit(solution)/shard_map/ppermute | solution.py:200
  61.8 1.4 %collective-permute-start.16 = (f32[16,16,32]{2,1,0:T(8,128)S(1)}, f32[16,16,32]{2,1,0:T(8,128)S(1)}, u32[]{:S(2)}, u32[]{:S(2)}) collective-permute-start(f32[16,16,32]{2,1,0:T(8,128)S(1)} %get-tuple-element.40), channel_id=1, source_target_pairs={{0,8},{8,0},{1,9},{9,1},{2,10},{10,2},{3,11},{11,3},{4,12},{12,4},... | collective-permute-start | bytes 98312 | tf_op jit(solution)/shard_map/ppermute | solution.py:218

commit v4 on v3

--- a/solution.py
+++ b/solution.py
@@ -9,6 +9,8 @@
 
 LANES = 128
 ROWS = 16
+FIRST = 2
+ROOMS = (9, 10, 11, 12, 13)
 VMEM_LIMIT = 16 * 1024 * 1024
 
 
@@ -50,11 +52,49 @@
     return gram_tiles * live_counts[:, None, None] / (row_totals[:, :, None] * totals[:, None, :])
 
 
-def pack_kernel(n_pix, messages, place, frames, dark, *refs):
+def plan_kernel(rooms, slots, counts, position, branch):
+    receivers, units = position.shape
+    every = counts[...].astype(jnp.float32)
+    own = (
+        lax.broadcasted_iota(jnp.int32, (receivers, every.shape[1]), 1) // ROWS
+        == lax.broadcasted_iota(jnp.int32, (receivers, every.shape[1]), 0)
+    )
+    repeat = (
+        lax.broadcasted_iota(jnp.int32, (every.shape[1], units), 0) % ROWS
+        == lax.broadcasted_iota(jnp.int32, (every.shape[1], units), 1) % ROWS
+    )
+    count = pick(jnp.where(own, every, 0.0), jnp.where(repeat, 1.0, 0.0).astype(jnp.bfloat16))
+    tile = lax.broadcasted_iota(jnp.int32, (receivers, units), 1) // ROWS
+    live = count > (slots // 2 + tile * LANES).astype(jnp.float32)
+    flags = jnp.where(live, 1.0, 0.0)
+    before = (
+        lax.broadcasted_iota(jnp.int32, (units, units), 0)
+        < lax.broadcasted_iota(jnp.int32, (units, units), 1)
+    )
+    place = jnp.dot(
+        flags.astype(jnp.bfloat16),
+        jnp.where(before, 1.0, 0.0).astype(jnp.bfloat16),
+        preferred_element_type=jnp.float32,
+    )
+    position[...] = jnp.where(live, place, -1.0)
+    most = jnp.max(jnp.sum(flags, axis=1, keepdims=True)).astype(jnp.int32)
+    branch[0] = sum(jnp.where(most > room, 1, 0) for room in rooms[:-1])
+
+
+def chooser(position, receiver, room):
+    units = position.shape[1]
+    row = lax.broadcasted_iota(jnp.int32, (room, units), 0).astype(jnp.float32)
+    return jnp.where(row == position[pl.ds(receiver, 1), :], 1.0, 0.0)
+
+
+def pack_kernel(n_pix, room, messages, after, place, position, frames, dark, *refs):
     count = len(messages)
+    refs = refs[after:]
     outs, (raw, shade, raw_sem, shade_sem) = refs[:count], refs[count:]
     per_device, slots = frames.shape[0], frames.shape[-1]
     share = shade.shape[1]
+    lower = slots // 2 // LANES
+    units = lower * ROWS
     copies = []
     for n, k in enumerate(messages):
         dest, half = place[0] ^ (k % n_pix), place[1] ^ (k // n_pix)
@@ -66,15 +106,36 @@
         ))
         for copy in copies[-1]:
             copy.start()
-    for n in range(count):
+    for n, k in enumerate(messages):
         for copy in copies[n]:
             copy.wait()
         row = 0
-        for block, depth in ((raw, per_device), (shade, share)):
+        for block, depth, tiles in (
+            (raw, per_device, range(lower)),
+            (shade, share, range(shade.shape[-1] // LANES)),
+            (raw, per_device, range(lower, 2 * lower) if room == units else ()),
+        ):
             for f in range(depth):
-                for j in range(block.shape[-1] // LANES):
+                for j in tiles:
                     outs[n][pl.ds(row, ROWS), :] = block[n, f, :, pl.ds(j * LANES, LANES)]
                     row += ROWS
+        if room < units:
+            dest, half = place[0] ^ (k % n_pix), place[1] ^ (k // n_pix)
+            chosen = chooser(position, dest * 2 + half, room).astype(jnp.bfloat16)
+            upper = jnp.concatenate(
+                [
+                    jnp.concatenate(
+                        [raw[n, f, :, pl.ds(j * LANES, LANES)] for j in range(lower, 2 * lower)], axis=0
+                    )
+                    for f in range(per_device)
+                ],
+                axis=1,
+            )
+            live = jnp.dot(chosen, upper, preferred_element_type=jnp.float32)
+            live = jnp.concatenate(
+                [live[:, f * LANES : (f + 1) * LANES] for f in range(per_device)], axis=0
+            )
+            outs[n][pl.ds(row, per_device * room), :] = live.astype(jnp.bfloat16)
 
 
 def split3(x):
@@ -89,7 +150,9 @@
     return sum(jnp.dot(part, chosen, preferred_element_type=jnp.float32) for part in split3(x))
 
 
-def gram_kernel(n_pix, per_device, levels, order, place, own_index, other_index, cycle_counts, *refs):
+def gram_kernel(
+    n_pix, per_device, levels, room, order, place, own_index, other_index, cycle_counts, position, *refs
+):
     n_bufs = 2 * n_pix
     bufs, (mine, theirs, signal, dark) = dict(zip(order, refs)), refs[n_bufs:]
     me, core = place[0], place[1]
@@ -99,7 +162,12 @@
     slots = signal.shape[1]
     tiles = slots // LANES
     dark_tiles = tiles // n_pix
-    dark_row = per_device * tiles * ROWS
+    lower = tiles // 2
+    units = lower * ROWS
+    dark_row = per_device * units
+    upper_row = dark_row + share * dark_tiles * ROWS
+    if room < units:
+        chosen = chooser(position, me * 2 + core, units).T.astype(jnp.bfloat16)[:, :room]
     lane = lax.broadcasted_iota(jnp.int32, (ROWS, LANES), 1)
     cycle = lax.broadcasted_iota(jnp.int32, (ROWS, LANES), 0)
     counts = jnp.zeros((ROWS, LANES), jnp.int32)
@@ -119,12 +187,23 @@
     for k in range(n_bufs):
         source, half = me ^ (k % n_pix), core ^ (k // n_pix)
         index = own_index if k < n_pix else other_index
+        if room < units:
+            packed = [bufs[k][pl.ds(upper_row + f * room, room), :] for f in range(per_device)]
+            upper = jnp.dot(
+                chosen, jnp.concatenate(packed, axis=1), preferred_element_type=jnp.float32
+            )
         for f in range(per_device):
             frame = source * per_device + f
             first = pl.multiple_of(((k // n_pix) * frames_half + frame) * ROWS, ROWS)
             dark_first = pl.multiple_of(index[frame] * ROWS, ROWS)
             for j in range(tiles):
-                raw = bufs[k][pl.ds((f * tiles + j) * ROWS, ROWS), :].astype(jnp.float32)
+                unit = (j % lower) * ROWS
+                if j < lower:
+                    raw = bufs[k][pl.ds(f * units + unit, ROWS), :].astype(jnp.float32)
+                elif room < units:
+                    raw = upper[unit : unit + ROWS, f * LANES : (f + 1) * LANES]
+                else:
+                    raw = bufs[k][pl.ds(upper_row + f * units + unit, ROWS), :].astype(jnp.float32)
                 value = raw - dark[j, pl.ds(dark_first, ROWS), :]
                 value = jnp.where(live[j], value, 0.0)
                 signal[pl.ds(first, ROWS), pl.ds(j * LANES, LANES)] = value.astype(jnp.bfloat16)
@@ -166,55 +245,86 @@
     per_device, _, slots = frames.shape
     levels, _, dark_slots = dark.shape
     n_frames = 2 * per_device * n_pix
+    share = levels // 2
+    units = slots // 2 // LANES * ROWS
+    rooms = [units * part // 16 for part in ROOMS] + [units]
     swap = [(0, 1), (1, 0)]
-    split_frames = pltpu.with_memory_space_constraint(
-        frames.reshape(per_device, n_pix, 2, ROWS, slots), pltpu.HBM
-    )
-    split_dark = pltpu.with_memory_space_constraint(
-        dark.reshape(levels, n_pix, 2, ROWS, dark_slots), pltpu.HBM
-    )
-    share = levels // 2
-    place = jnp.stack([me, core]).astype(jnp.int32)
-    rows = (per_device * slots + share * dark_slots) // LANES * ROWS
     half = n_pix // 2
-    far = [t * n_pix + k for t in range(2) for k in range(half, n_pix)]
+    far = [t * n_pix + k for t in range(2) for k in [*range(half, n_pix, 2), *range(half + 1, n_pix, 2)]]
     near = [t * n_pix + k for t in range(2) for k in range(1, half)] + [n_pix]
-    order = [k for pair in zip(far, near) for k in pair] + far[len(near) :]
+    order = far[:1] + [k for pair in zip(far[1:], near) for k in pair]
     messages = order + [0]
     count = len(messages)
-    packed = pl.pallas_call(
-        functools.partial(pack_kernel, n_pix, messages),
-        out_shape=[jax.ShapeDtypeStruct((rows, LANES), frames.dtype)] * count,
-        in_specs=in_smem(1) + [pl.BlockSpec(memory_space=pltpu.HBM)] * 2,
-        out_specs=in_vmem(count),
-        scratch_shapes=[
-            pltpu.VMEM((count, per_device, ROWS, slots), frames.dtype),
-            pltpu.VMEM((count, share, ROWS, dark_slots), dark.dtype),
-            pltpu.SemaphoreType.DMA((count,)),
-            pltpu.SemaphoreType.DMA((count,)),
+
+    def exchange(room, place, position, frames, dark, own_index, other_index, cycle_counts):
+        rows = per_device * (units + room) + share * dark_slots // LANES * ROWS
+        packed = []
+        for group in (messages[:FIRST], messages[FIRST:]):
+            size, after = len(group), packed[:1]
+            packed += pl.pallas_call(
+                functools.partial(pack_kernel, n_pix, room, group, len(after)),
+                out_shape=[jax.ShapeDtypeStruct((rows, LANES), frames.dtype)] * size,
+                in_specs=in_smem(1) + in_vmem(1)
+                + [pl.BlockSpec(memory_space=pltpu.HBM)] * 2
+                + [pl.BlockSpec(memory_space=pl.ANY)] * len(after),
+                out_specs=in_vmem(size),
+                scratch_shapes=[
+                    pltpu.VMEM((size, per_device, ROWS, slots), frames.dtype),
+                    pltpu.VMEM((size, share, ROWS, dark_slots), dark.dtype),
+                    pltpu.SemaphoreType.DMA((size,)),
+                    pltpu.SemaphoreType.DMA((size,)),
+                ],
+                compiler_params=pltpu.CompilerParams(vmem_limit_bytes=VMEM_LIMIT),
+                name="pack",
+            )(
+                place,
+                position,
+                pltpu.with_memory_space_constraint(frames, pltpu.HBM),
+                pltpu.with_memory_space_constraint(dark, pltpu.HBM),
+                *after,
+            )
+        received = [
+            lax.ppermute(buffer, ("tm", "pix"), [(i, i ^ k) for i in range(count)]) if k else buffer
+            for k, buffer in zip(messages, packed)
+        ]
+        blocks = jax.ShapeDtypeStruct((ROWS, n_frames // 2, n_frames), jnp.float32)
+        mine, send = pl.pallas_call(
+            functools.partial(gram_kernel, n_pix, per_device, levels, room, messages),
+            out_shape=[blocks, blocks],
+            in_specs=in_smem(4) + in_vmem(1 + count),
+            out_specs=in_vmem(2),
+            scratch_shapes=[
+                pltpu.VMEM((n_frames * ROWS, slots), jnp.bfloat16),
+                pltpu.VMEM((slots // LANES, levels * ROWS, LANES), jnp.float32),
+            ],
+            compiler_params=pltpu.CompilerParams(vmem_limit_bytes=VMEM_LIMIT),
+            name="gram",
+        )(place, own_index, other_index, cycle_counts, position, *received)
+        return mine, send
+
+    place = jnp.stack([me, core]).astype(jnp.int32)
+    position, branch = pl.pallas_call(
+        functools.partial(plan_kernel, rooms, slots),
+        out_shape=[
+            jax.ShapeDtypeStruct((2 * n_pix, units), jnp.float32),
+            jax.ShapeDtypeStruct((1,), jnp.int32),
         ],
-        compiler_params=pltpu.CompilerParams(vmem_limit_bytes=VMEM_LIMIT),
-        name="pack",
-    )(place, split_frames, split_dark)
-    received = [
-        lax.ppermute(buffer, ("tm", "pix"), [(i, i ^ k) for i in range(2 * n_pix)]) if k else buffer
-        for k, buffer in zip(messages, packed)
-    ]
+        in_specs=in_vmem(1),
+        out_specs=in_vmem(1) + in_smem(1),
+        name="plan",
+    )(cycle_counts.reshape(1, -1))
     other_index = lax.ppermute(dark_index, "tm", swap)
-    width = n_frames * ROWS
-    blocks = jax.ShapeDtypeStruct((ROWS, n_frames // 2, n_frames), jnp.float32)
-    mine, send = pl.pallas_call(
-        functools.partial(gram_kernel, n_pix, per_device, levels, messages),
-        out_shape=[blocks, blocks],
-        in_specs=in_smem(4) + in_vmem(2 * n_pix),
-        out_specs=in_vmem(2),
-        scratch_shapes=[
-            pltpu.VMEM((width, slots), jnp.bfloat16),
-            pltpu.VMEM((slots // LANES, levels * ROWS, LANES), jnp.float32),
-        ],
-        compiler_params=pltpu.CompilerParams(vmem_limit_bytes=VMEM_LIMIT),
-        name="gram",
-    )(place, dark_index, other_index, cycle_counts, *received)
+    mine, send = lax.switch(
+        branch[0],
+        [functools.partial(exchange, room) for room in rooms],
+        place,
+        position,
+        frames.reshape(per_device, n_pix, 2, ROWS, slots),
+        dark.reshape(levels, n_pix, 2, ROWS, dark_slots),
+        dark_index,
+        other_index,
+        cycle_counts,
+    )
     theirs = lax.ppermute(send, "tm", swap)
     lower = core == 0
     return jnp.concatenate(
@@ -227,7 +337,7 @@
 
     def local(frames, dark, dark_index, cycle_counts):
         owned, slots = frames.shape[1] // n_pix, frames.shape[2]
-        fits = n_tm == 2 and owned == 2 * ROWS and n_pix & (n_pix - 1) == 0 and n_pix <= 8
+        fits = n_tm == 2 and owned == 2 * ROWS and slots % (2 * LANES) == 0 and n_pix & (n_pix - 1) == 0 and n_pix <= 8
         fits = fits and dark.shape[0] % 2 == 0 and dark.shape[2] % LANES == 0 and slots == dark.shape[2] * n_pix
         return (packed_local if fits else plain_local)(frames, dark, dark_index, cycle_counts)
 

time: 64.1 us -> 60.2 us (0.939)
  waiting for transfers between devices: 28.9 us -> 22.8 us
  Pallas kernels: 6.43 us -> 11.5 us
  starting transfers between devices: 27.8 us -> 23.5 us
    ppermute x15, waiting for transfers between devices: 27.9 us -> 21.8 us  [exchange(): lax.ppermute(buffer, ('tm', 'pix'), [(i, i ^ k) for i in range(count)])]
    pallas_call x2 -> x4, Pallas kernels: 6.43 us -> 11.5 us  [the longest x2 5.99 us: exchange(): pl.pallas_call(functools.partial(pack_kernel, n_pix, room, group, len(aft...]
    ppermute x15, starting transfers between devices: 25.8 us -> 22.5 us  [exchange(): lax.ppermute(buffer, ('tm', 'pix'), [(i, i ^ k) for i in range(count)])]
    ppermute x1, starting transfers between devices: 1.52 us -> 0.68 us  [packed_local(): other_index = lax.ppermute(dark_index, 'tm', swap)]
  transfers between devices with their start and end apart: 17 -> 17, of which waited for: 8 -> 9; matrix products, arithmetic and copies ran while one was open for 0% -> 0% of each run, Pallas kernels for 0% -> 9%
where the time goes in v4:
time: 60.2 us; the launch traced here: 60 us
  starting transfers between devices  23.5 us (39%)
  waiting for transfers between devices  22.8 us (38%)
  Pallas kernels  11.5 us (19%)
  other arithmetic  0.82 us (1%)
  between operations  0.68 us (1%)
    ppermute x15, starting transfers between devices, exchange(): lax.ppermute(buffer, ('tm', 'pix'), [(i, i ^ k) for i in range(count)])  22.5 us
    ppermute x15, waiting for transfers between devices, exchange(): lax.ppermute(buffer, ('tm', 'pix'), [(i, i ^ k) for i in range(count)])  21.8 us
    pallas_call x2, Pallas kernels, exchange(): pl.pallas_call(functools.partial(pack_kernel, n_pix, room, group, len(aft...  5.99 us
    pallas_call x1, Pallas kernels, exchange(): pl.pallas_call(functools.partial(gram_kernel, n_pix, per_device, levels,...  4.05 us
    pallas_call x1, Pallas kernels, packed_local(): pl.pallas_call(functools.partial(plan_kernel, rooms, slots), out_shape=[j...  1.48 us
  transfers between devices with their start and end apart: 17, of which 9 were waited for; matrix products, arithmetic and copies ran while one was open for 0% of the time, Pallas kernels for 9%

profile of v4, /device:TPU:17, one launch (start us, length us, event | category | flops | bytes accessed | tf_op | source)
XLA Modules:
  0.0 60.0 jit_solution(15581358235087279670)
XLA Ops:
  0.0 0.7 %collective-permute-start.90 = (s32[16]{0:T(128)}, s32[16]{0:T(128)S(1)}, u32[]{:S(2)}, u32[]{:S(2)}) collective-permute-start(s32[16]{0:T(128)} %param.12), channel_id=1, source_target_pairs={{0,8},{8,0},{1,9},{9,1},{2,10},{10,2},{3,11},{11,3},{4,12},{12,4},... | collective-permute-start | bytes 200 | tf_op jit(solution)/shard_map/ppermute | solution.py:316
  0.7 1.5 %plan.1 = (f32[16,128]{1,0:T(8,128)S(1)}, s32[1]{0:T(128)}) custom-call(s32[1,256]{1,0:T(1,128)} %bitcast.18), custom_call_target="tpu_custom_call" | custom-call | tf_op jit(solution)/shard_map/plan/pallas_call | solution.py:306
  2.9 54.9 %conditional.1 = ((f32[16,16,32]{2,1,0:T(8,128)S(1)}, f32[16,16,32]{2,1,0:T(8,128)S(1)})) conditional(s32[]{:T(128)} %bitcast.1, (s32[2]{0:T(128)S(1)}, f32[16,128]{1,0:T(8,128)S(1)}, bf16[2,8,2,16,2048]{4,3,2,1,0:T(8,128)(2,1)}, bf16[4,8,2,16,256]{4,3,2,1,0:T(8,128)(2,1)}, s32[16]{0:T(128)}, ...), branch_computations={%region_0.0_spmd, %region_1.0_spmd, %region_2.0_spmd, %region_3.0_... | conditional | bytes 8852376 | solution.py:317
  3.2 1.8 %pack.18 = (bf16[512,128]{1,0:T(8,128)(2,1)S(1)}, bf16[512,128]{1,0:T(8,128)(2,1)S(1)}) custom-call(s32[2]{0:T(128)S(1)} %get-tuple-element.158.place, f32[16,128]{1,0:T(8,128)S(1)} %get-tuple-element.162.position, bf16[2,8,2,16,2048]{4,3,2,1,0:T(8,128)(2,1)} %get-tuple-element.163.frames, bf16[4,8,2,16,256]{4,3,2,1,0:T(8,128)(2,1)} %get-tuple-element.164.dark), custom_call_target="tpu_custom_call" | custom-call | tf_op jit(solution)/shard_map/cond/branch_3_fun/pack/pallas_call | solution.py:264
  5.3 3.2 %collective-permute-start.45 = (bf16[512,128]{1,0:T(8,128)(2,1)S(1)}, bf16[512,128]{1,0:T(8,128)(2,1)S(1)}, u32[]{:S(2)}, u32[]{:S(2)}) collective-permute-start(bf16[512,128]{1,0:T(8,128)(2,1)S(1)} %get-tuple-element.165.refs_0_), channel_id=1, source_target_pairs={{0,4},{1,5},{2,6},{3,7},{4,0},{5,1},{6,2},{7,3},{8,12},{9,13},{10,... | collective-permute-start | bytes 393224 | tf_op jit(solution)/shard_map/cond/branch_3_fun/ppermute | solution.py:287
  8.5 4.2 %pack.19 = (bf16[512,128]{1,0:T(8,128)(2,1)S(1)}, bf16[512,128]{1,0:T(8,128)(2,1)S(1)}, bf16[512,128]{1,0:T(8,128)(2,1)S(1)}, bf16[512,128]{1,0:T(8,128)(2,1)S(1...) custom-call(s32[2]{0:T(128)S(1)} %get-tuple-element.158.place, ...), custom_call_target="tpu_custom_call" | custom-call | tf_op jit(solution)/shard_map/cond/branch_3_fun/pack/pallas_call | solution.py:264
  12.6 1.3 %collective-permute-start.47 = (bf16[512,128]{1,0:T(8,128)(2,1)S(1)}, bf16[512,128]{1,0:T(8,128)(2,1)S(1)}, u32[]{:S(2)}, u32[]{:S(2)}) collective-permute-start(bf16[512,128]{1,0:T(8,128)(2,1)S(1)} %get-tuple-element.167), channel_id=1, source_target_pairs={{0,1},{1,0},{2,3},{3,2},{4,5},{5,4},{6,7},{7,6},{8,9},{9,8},{10,11... | collective-permute-start | bytes 393224 | tf_op jit(solution)/shard_map/cond/branch_3_fun/ppermute | solution.py:287
  14.2 1.6 %collective-permute-done.46.refs_1_ = bf16[512,128]{1,0:T(8,128)(2,1)S(1)} collective-permute-done((bf16[512,128]{1,0:T(8,128)(2,1)S(1)}, bf16[512,128]{1,0:T(8,128)(2,1)S(1)}, u32[]{:S(2)}, u32[]{:S(2)}) %collective-permute-start.46) | collective-permute-done | bytes 131104 | tf_op jit(solution)/shard_map/cond/branch_3_fun/ppermute | solution.py:287
  15.8 1.7 %collective-permute-start.50 = (bf16[512,128]{1,0:T(8,128)(2,1)S(1)}, bf16[512,128]{1,0:T(8,128)(2,1)S(1)}, u32[]{:S(2)}, u32[]{:S(2)}) collective-permute-start(bf16[512,128]{1,0:T(8,128)(2,1)S(1)} %get-tuple-element.170), channel_id=1, source_target_pairs={{0,7},{1,6},{2,5},{3,4},{4,3},{5,2},{6,1},{7,0},{8,15},{9,14},{10,... | collective-permute-start | bytes 393224 | tf_op jit(solution)/shard_map/cond/branch_3_fun/ppermute | solution.py:287
  17.5 1.9 %collective-permute-done.45.refs_0_ = bf16[512,128]{1,0:T(8,128)(2,1)S(1)} collective-permute-done((bf16[512,128]{1,0:T(8,128)(2,1)S(1)}, bf16[512,128]{1,0:T(8,128)(2,1)S(1)}, u32[]{:S(2)}, u32[]{:S(2)}) %collective-permute-start.45) | collective-permute-done | bytes 131104 | tf_op jit(solution)/shard_map/cond/branch_3_fun/ppermute | solution.py:287
  19.4 4.0 %collective-permute-start.51 = (bf16[512,128]{1,0:T(8,128)(2,1)S(1)}, bf16[512,128]{1,0:T(8,128)(2,1)S(1)}, u32[]{:S(2)}, u32[]{:S(2)}) collective-permute-start(bf16[512,128]{1,0:T(8,128)(2,1)S(1)} %get-tuple-element.171), channel_id=1, source_target_pairs={{0,3},{1,2},{2,1},{3,0},{4,7},{5,6},{6,5},{7,4},{8,11},{9,10},{10,... | collective-permute-start | bytes 393224 | tf_op jit(solution)/shard_map/cond/branch_3_fun/ppermute | solution.py:287
  23.4 3.0 %collective-permute-start.52 = (bf16[512,128]{1,0:T(8,128)(2,1)S(1)}, bf16[512,128]{1,0:T(8,128)(2,1)S(1)}, u32[]{:S(2)}, u32[]{:S(2)}) collective-permute-start(bf16[512,128]{1,0:T(8,128)(2,1)S(1)} %get-tuple-element.172), channel_id=1, source_target_pairs={{0,12},{1,13},{2,14},{3,15},{4,8},{5,9},{6,10},{7,11},{8,4},{9,5},... | collective-permute-start | bytes 393224 | tf_op jit(solution)/shard_map/cond/branch_3_fun/ppermute | solution.py:287
  26.4 1.0 %collective-permute-start.53 = (bf16[512,128]{1,0:T(8,128)(2,1)S(1)}, bf16[512,128]{1,0:T(8,128)(2,1)S(1)}, u32[]{:S(2)}, u32[]{:S(2)}) collective-permute-start(bf16[512,128]{1,0:T(8,128)(2,1)S(1)} %get-tuple-element.173), channel_id=1, source_target_pairs={{0,9},{1,8},{2,11},{3,10},{4,13},{5,12},{6,15},{7,14},{8,1},{9,0},... | collective-permute-start | bytes 393224 | tf_op jit(solution)/shard_map/cond/branch_3_fun/ppermute | solution.py:287
  27.4 2.0 %collective-permute-start.54 = (bf16[512,128]{1,0:T(8,128)(2,1)S(1)}, bf16[512,128]{1,0:T(8,128)(2,1)S(1)}, u32[]{:S(2)}, u32[]{:S(2)}) collective-permute-start(bf16[512,128]{1,0:T(8,128)(2,1)S(1)} %get-tuple-element.174), channel_id=1, source_target_pairs={{0,14},{1,15},{2,12},{3,13},{4,10},{5,11},{6,8},{7,9},{8,6},{9,7},... | collective-permute-start | bytes 393224 | tf_op jit(solution)/shard_map/cond/branch_3_fun/ppermute | solution.py:287
  29.3 4.4 %collective-permute-done.50.refs_5_ = bf16[512,128]{1,0:T(8,128)(2,1)S(1)} collective-permute-done((bf16[512,128]{1,0:T(8,128)(2,1)S(1)}, bf16[512,128]{1,0:T(8,128)(2,1)S(1)}, u32[]{:S(2)}, u32[]{:S(2)}) %collective-permute-start.50) | collective-permute-done | bytes 131104 | tf_op jit(solution)/shard_map/cond/branch_3_fun/ppermute | solution.py:287
  34.3 2.1 %collective-permute-done.52.refs_7_ = bf16[512,128]{1,0:T(8,128)(2,1)S(1)} collective-permute-done((bf16[512,128]{1,0:T(8,128)(2,1)S(1)}, bf16[512,128]{1,0:T(8,128)(2,1)S(1)}, u32[]{:S(2)}, u32[]{:S(2)}) %collective-permute-start.52) | collective-permute-done | bytes 131104 | tf_op jit(solution)/shard_map/cond/branch_3_fun/ppermute | solution.py:287
  36.4 5.3 %collective-permute-start.57 = (bf16[512,128]{1,0:T(8,128)(2,1)S(1)}, bf16[512,128]{1,0:T(8,128)(2,1)S(1)}, u32[]{:S(2)}, u32[]{:S(2)}) collective-permute-start(bf16[512,128]{1,0:T(8,128)(2,1)S(1)} %get-tuple-element.177), channel_id=1, source_target_pairs={{0,11},{1,10},{2,9},{3,8},{4,15},{5,14},{6,13},{7,12},{8,3},{9,2},... | collective-permute-start | bytes 393224 | tf_op jit(solution)/shard_map/cond/branch_3_fun/ppermute | solution.py:287
  41.7 3.1 %collective-permute-done.54.refs_9_ = bf16[512,128]{1,0:T(8,128)(2,1)S(1)} collective-permute-done((bf16[512,128]{1,0:T(8,128)(2,1)S(1)}, bf16[512,128]{1,0:T(8,128)(2,1)S(1)}, u32[]{:S(2)}, u32[]{:S(2)}) %collective-permute-start.54) | collective-permute-done | bytes 131104 | tf_op jit(solution)/shard_map/cond/branch_3_fun/ppermute | solution.py:287
  44.8 1.1 %collective-permute-done.56.refs_11_ = bf16[512,128]{1,0:T(8,128)(2,1)S(1)} collective-permute-done((bf16[512,128]{1,0:T(8,128)(2,1)S(1)}, bf16[512,128]{1,0:T(8,128)(2,1)S(1)}, u32[]{:S(2)}, u32[]{:S(2)}) %collective-permute-start.56) | collective-permute-done | bytes 131104 | tf_op jit(solution)/shard_map/cond/branch_3_fun/ppermute | solution.py:287
  45.9 3.1 %collective-permute-done.57.refs_12_ = bf16[512,128]{1,0:T(8,128)(2,1)S(1)} collective-permute-done((bf16[512,128]{1,0:T(8,128)(2,1)S(1)}, bf16[512,128]{1,0:T(8,128)(2,1)S(1)}, u32[]{:S(2)}, u32[]{:S(2)}) %collective-permute-start.57) | collective-permute-done | bytes 131104 | tf_op jit(solution)/shard_map/cond/branch_3_fun/ppermute | solution.py:287
  49.1 4.4 %collective-permute-done.58.refs_13_ = bf16[512,128]{1,0:T(8,128)(2,1)S(1)} collective-permute-done((bf16[512,128]{1,0:T(8,128)(2,1)S(1)}, bf16[512,128]{1,0:T(8,128)(2,1)S(1)}, u32[]{:S(2)}, u32[]{:S(2)}) %collective-permute-start.58) | collective-permute-done | bytes 131104 | tf_op jit(solution)/shard_map/cond/branch_3_fun/ppermute | solution.py:287
  53.5 4.1 %gram.9 = (f32[16,16,32]{2,1,0:T(8,128)S(1)}, f32[16,16,32]{2,1,0:T(8,128)S(1)}) custom-call(s32[2]{0:T(128)S(1)} %get-tuple-element.158.place, s32[16]{0:T(128)S(1)} %copy-done.9, s32[16]{0:T(128)S(1)} %get-tuple-element.160.other_index, s32[256]{0:T(256)S(1)} %copy-done.3, f32[16,128]{1,0:T(8,128)S(1)} %get-tuple-element.162.position, ...), custom_call_target="tpu_custom_call" | custom-call | tf_op jit(solution)/shard_map/cond/branch_3_fun/gram/pallas_call | solution.py:291
  58.2 1.1 %collective-permute-done.91 = f32[16,16,32]{2,1,0:T(8,128)S(1)} collective-permute-done((f32[16,16,32]{2,1,0:T(8,128)S(1)}, f32[16,16,32]{2,1,0:T(8,128)S(1)}, u32[]{:S(2)}, u32[]{:S(2)}) %collective-permute-start.91) | collective-permute-done | bytes 32800 | tf_op jit(solution)/shard_map/ppermute | solution.py:328
  59.3 0.7 %pad_maximum_fusion = f32[32,16,32]{2,1,0:T(8,128)} fusion(f32[16,16,32]{2,1,0:T(8,128)S(1)} %get-tuple-element.236, f32[16,16,32]{2,1,0:T(8,128)S(1)} %get-tuple-element.235), kind=kLoop, calls=%fused_computation | loop fusion | flops 16384 | bytes 131072 | tf_op jit(solution)/shard_map/concatenate | solution.py:330
  (22 shorter events, 1.6 us)
Async XLA Ops:
  0.0 2.9 %collective-permute-start.90 = (s32[16]{0:T(128)}, s32[16]{0:T(128)S(1)}, u32[]{:S(2)}, u32[]{:S(2)}) collective-permute-start(s32[16]{0:T(128)} %param.12), channel_id=1, source_target_pairs={{0,8},{8,0},{1,9},{9,1},{2,10},{10,2},{3,11},{11,3},{4,12},{12,4},... | collective-permute-start | bytes 200 | tf_op jit(solution)/shard_map/ppermute | solution.py:316
  3.2 50.3 %copy-start.3 = (s32[256]{0:T(256)S(1)}, s32[256]{0:T(256)}, u32[]{:S(2)}) copy-start(s32[256]{0:T(256)} %get-tuple-element.161.cycle_counts) | copy-start | bytes 3076 | tf_op jit(solution)/shard_map/cond
  3.2 50.3 %copy-start.9 = (s32[16]{0:T(128)S(1)}, s32[16]{0:T(128)}, u32[]{:S(2)}) copy-start(s32[16]{0:T(128)} %get-tuple-element.159.own_index) | copy-start | bytes 196 | tf_op jit(solution)/shard_map/cond
  5.0 10.8 %collective-permute-start.46 = (bf16[512,128]{1,0:T(8,128)(2,1)S(1)}, bf16[512,128]{1,0:T(8,128)(2,1)S(1)}, u32[]{:S(2)}, u32[]{:S(2)}) collective-permute-start(bf16[512,128]{1,0:T(8,128)(2,1)S(1)} %get-tuple-element.166), channel_id=1, source_target_pairs={{0,6},{1,7},{2,4},{3,5},{4,2},{5,3},{6,0},{7,1},{8,14},{9,15},{10,... | collective-permute-start | bytes 393224 | tf_op jit(solution)/shard_map/cond/branch_3_fun/ppermute | solution.py:287
  5.3 14.1 %collective-permute-start.45 = (bf16[512,128]{1,0:T(8,128)(2,1)S(1)}, bf16[512,128]{1,0:T(8,128)(2,1)S(1)}, u32[]{:S(2)}, u32[]{:S(2)}) collective-permute-start(bf16[512,128]{1,0:T(8,128)(2,1)S(1)} %get-tuple-element.165.refs_0_), channel_id=1, source_target_pairs={{0,4},{1,5},{2,6},{3,7},{4,0},{5,1},{6,2},{7,3},{8,12},{9,13},{10,... | collective-permute-start | bytes 393224 | tf_op jit(solution)/shard_map/cond/branch_3_fun/ppermute | solution.py:287
  12.6 10.8 %collective-permute-start.47 = (bf16[512,128]{1,0:T(8,128)(2,1)S(1)}, bf16[512,128]{1,0:T(8,128)(2,1)S(1)}, u32[]{:S(2)}, u32[]{:S(2)}) collective-permute-start(bf16[512,128]{1,0:T(8,128)(2,1)S(1)} %get-tuple-element.167), channel_id=1, source_target_pairs={{0,1},{1,0},{2,3},{3,2},{4,5},{5,4},{6,7},{7,6},{8,9},{9,8},{10,11... | collective-permute-start | bytes 393224 | tf_op jit(solution)/shard_map/cond/branch_3_fun/ppermute | solution.py:287
  13.9 12.5 %collective-permute-start.48 = (bf16[512,128]{1,0:T(8,128)(2,1)S(1)}, bf16[512,128]{1,0:T(8,128)(2,1)S(1)}, u32[]{:S(2)}, u32[]{:S(2)}) collective-permute-start(bf16[512,128]{1,0:T(8,128)(2,1)S(1)} %get-tuple-element.168), channel_id=1, source_target_pairs={{0,5},{1,4},{2,7},{3,6},{4,1},{5,0},{6,3},{7,2},{8,13},{9,12},{10,... | collective-permute-start | bytes 393224 | tf_op jit(solution)/shard_map/cond/branch_3_fun/ppermute | solution.py:287
  13.9 13.4 %collective-permute-start.49 = (bf16[512,128]{1,0:T(8,128)(2,1)S(1)}, bf16[512,128]{1,0:T(8,128)(2,1)S(1)}, u32[]{:S(2)}, u32[]{:S(2)}) collective-permute-start(bf16[512,128]{1,0:T(8,128)(2,1)S(1)} %get-tuple-element.169), channel_id=1, source_target_pairs={{0,2},{1,3},{2,0},{3,1},{4,6},{5,7},{6,4},{7,5},{8,10},{9,11},{10,... | collective-permute-start | bytes 393224 | tf_op jit(solution)/shard_map/cond/branch_3_fun/ppermute | solution.py:287
  15.8 17.9 %collective-permute-start.50 = (bf16[512,128]{1,0:T(8,128)(2,1)S(1)}, bf16[512,128]{1,0:T(8,128)(2,1)S(1)}, u32[]{:S(2)}, u32[]{:S(2)}) collective-permute-start(bf16[512,128]{1,0:T(8,128)(2,1)S(1)} %get-tuple-element.170), channel_id=1, source_target_pairs={{0,7},{1,6},{2,5},{3,4},{4,3},{5,2},{6,1},{7,0},{8,15},{9,14},{10,... | collective-permute-start | bytes 393224 | tf_op jit(solution)/shard_map/cond/branch_3_fun/ppermute | solution.py:287
  19.4 14.3 %collective-permute-start.51 = (bf16[512,128]{1,0:T(8,128)(2,1)S(1)}, bf16[512,128]{1,0:T(8,128)(2,1)S(1)}, u32[]{:S(2)}, u32[]{:S(2)}) collective-permute-start(bf16[512,128]{1,0:T(8,128)(2,1)S(1)} %get-tuple-element.171), channel_id=1, source_target_pairs={{0,3},{1,2},{2,1},{3,0},{4,7},{5,6},{6,5},{7,4},{8,11},{9,10},{10,... | collective-permute-start | bytes 393224 | tf_op jit(solution)/shard_map/cond/branch_3_fun/ppermute | solution.py:287
  23.4 13.0 %collective-permute-start.52 = (bf16[512,128]{1,0:T(8,128)(2,1)S(1)}, bf16[512,128]{1,0:T(8,128)(2,1)S(1)}, u32[]{:S(2)}, u32[]{:S(2)}) collective-permute-start(bf16[512,128]{1,0:T(8,128)(2,1)S(1)} %get-tuple-element.172), channel_id=1, source_target_pairs={{0,12},{1,13},{2,14},{3,15},{4,8},{5,9},{6,10},{7,11},{8,4},{9,5},... | collective-permute-start | bytes 393224 | tf_op jit(solution)/shard_map/cond/branch_3_fun/ppermute | solution.py:287
  26.4 15.3 %collective-permute-start.53 = (bf16[512,128]{1,0:T(8,128)(2,1)S(1)}, bf16[512,128]{1,0:T(8,128)(2,1)S(1)}, u32[]{:S(2)}, u32[]{:S(2)}) collective-permute-start(bf16[512,128]{1,0:T(8,128)(2,1)S(1)} %get-tuple-element.173), channel_id=1, source_target_pairs={{0,9},{1,8},{2,11},{3,10},{4,13},{5,12},{6,15},{7,14},{8,1},{9,0},... | collective-permute-start | bytes 393224 | tf_op jit(solution)/shard_map/cond/branch_3_fun/ppermute | solution.py:287
  27.4 17.4 %collective-permute-start.54 = (bf16[512,128]{1,0:T(8,128)(2,1)S(1)}, bf16[512,128]{1,0:T(8,128)(2,1)S(1)}, u32[]{:S(2)}, u32[]{:S(2)}) collective-permute-start(bf16[512,128]{1,0:T(8,128)(2,1)S(1)} %get-tuple-element.174), channel_id=1, source_target_pairs={{0,14},{1,15},{2,12},{3,13},{4,10},{5,11},{6,8},{7,9},{8,6},{9,7},... | collective-permute-start | bytes 393224 | tf_op jit(solution)/shard_map/cond/branch_3_fun/ppermute | solution.py:287
  33.7 11.1 %collective-permute-start.55 = (bf16[512,128]{1,0:T(8,128)(2,1)S(1)}, bf16[512,128]{1,0:T(8,128)(2,1)S(1)}, u32[]{:S(2)}, u32[]{:S(2)}) collective-permute-start(bf16[512,128]{1,0:T(8,128)(2,1)S(1)} %get-tuple-element.175), channel_id=1, source_target_pairs={{0,10},{1,11},{2,8},{3,9},{4,14},{5,15},{6,12},{7,13},{8,2},{9,3},... | collective-permute-start | bytes 393224 | tf_op jit(solution)/shard_map/cond/branch_3_fun/ppermute | solution.py:287
  33.7 12.2 %collective-permute-start.56 = (bf16[512,128]{1,0:T(8,128)(2,1)S(1)}, bf16[512,128]{1,0:T(8,128)(2,1)S(1)}, u32[]{:S(2)}, u32[]{:S(2)}) collective-permute-start(bf16[512,128]{1,0:T(8,128)(2,1)S(1)} %get-tuple-element.176), channel_id=1, source_target_pairs={{0,13},{1,12},{2,15},{3,14},{4,9},{5,8},{6,11},{7,10},{8,5},{9,4},... | collective-permute-start | bytes 393224 | tf_op jit(solution)/shard_map/cond/branch_3_fun/ppermute | solution.py:287
  36.4 12.7 %collective-permute-start.57 = (bf16[512,128]{1,0:T(8,128)(2,1)S(1)}, bf16[512,128]{1,0:T(8,128)(2,1)S(1)}, u32[]{:S(2)}, u32[]{:S(2)}) collective-permute-start(bf16[512,128]{1,0:T(8,128)(2,1)S(1)} %get-tuple-element.177), channel_id=1, source_target_pairs={{0,11},{1,10},{2,9},{3,8},{4,15},{5,14},{6,13},{7,12},{8,3},{9,2},... | collective-permute-start | bytes 393224 | tf_op jit(solution)/shard_map/cond/branch_3_fun/ppermute | solution.py:287
  41.7 11.8 %collective-permute-start.58 = (bf16[512,128]{1,0:T(8,128)(2,1)S(1)}, bf16[512,128]{1,0:T(8,128)(2,1)S(1)}, u32[]{:S(2)}, u32[]{:S(2)}) collective-permute-start(bf16[512,128]{1,0:T(8,128)(2,1)S(1)} %get-tuple-element.178), channel_id=1, source_target_pairs={{0,15},{1,14},{2,13},{3,12},{4,11},{5,10},{6,9},{7,8},{8,7},{9,6},... | collective-permute-start | bytes 393224 | tf_op jit(solution)/shard_map/cond/branch_3_fun/ppermute | solution.py:287
  44.8 8.7 %collective-permute-start.59 = (bf16[512,128]{1,0:T(8,128)(2,1)S(1)}, bf16[512,128]{1,0:T(8,128)(2,1)S(1)}, u32[]{:S(2)}, u32[]{:S(2)}) collective-permute-start(bf16[512,128]{1,0:T(8,128)(2,1)S(1)} %get-tuple-element.179), channel_id=1, source_target_pairs={{0,8},{1,9},{2,10},{3,11},{4,12},{5,13},{6,14},{7,15},{8,0},{9,1},... | collective-permute-start | bytes 393224 | tf_op jit(solution)/shard_map/cond/branch_3_fun/ppermute | solution.py:287
  57.8 1.4 %collective-permute-start.91 = (f32[16,16,32]{2,1,0:T(8,128)S(1)}, f32[16,16,32]{2,1,0:T(8,128)S(1)}, u32[]{:S(2)}, u32[]{:S(2)}) collective-permute-start(f32[16,16,32]{2,1,0:T(8,128)S(1)} %get-tuple-element.234), channel_id=1, source_target_pairs={{0,8},{8,0},{1,9},{9,1},{2,10},{10,2},{3,11},{11,3},{4,12},{12,4},... | collective-permute-start | bytes 98312 | tf_op jit(solution)/shard_map/ppermute | solution.py:328

commit v5 on v4

--- a/solution.py
+++ b/solution.py
@@ -54,7 +54,7 @@
 
 def plan_kernel(rooms, slots, counts, position, branch):
     receivers, units = position.shape
-    every = counts[...].astype(jnp.float32)
+    every = (jnp.maximum(counts[...] - slots // 2, 0) + LANES - 1) // LANES
     own = (
         lax.broadcasted_iota(jnp.int32, (receivers, every.shape[1]), 1) // ROWS
         == lax.broadcasted_iota(jnp.int32, (receivers, every.shape[1]), 0)
@@ -63,9 +63,13 @@
         lax.broadcasted_iota(jnp.int32, (every.shape[1], units), 0) % ROWS
         == lax.broadcasted_iota(jnp.int32, (every.shape[1], units), 1) % ROWS
     )
-    count = pick(jnp.where(own, every, 0.0), jnp.where(repeat, 1.0, 0.0).astype(jnp.bfloat16))
+    number = jnp.dot(
+        jnp.where(own, every, 0).astype(jnp.float32).astype(jnp.bfloat16),
+        jnp.where(repeat, 1.0, 0.0).astype(jnp.bfloat16),
+        preferred_element_type=jnp.float32,
+    )
     tile = lax.broadcasted_iota(jnp.int32, (receivers, units), 1) // ROWS
-    live = count > (slots // 2 + tile * LANES).astype(jnp.float32)
+    live = tile.astype(jnp.float32) < number
     flags = jnp.where(live, 1.0, 0.0)
     before = (
         lax.broadcasted_iota(jnp.int32, (units, units), 0)
@@ -256,7 +260,7 @@
     messages = order + [0]
     count = len(messages)
 
-    def exchange(room, place, position, frames, dark, own_index, other_index, cycle_counts):
+    def exchange(room, place, position, frames, dark, own_index, cycle_counts):
         rows = per_device * (units + room) + share * dark_slots // LANES * ROWS
         packed = []
         for group in (messages[:FIRST], messages[FIRST:]):
@@ -283,6 +287,7 @@
                 pltpu.with_memory_space_constraint(dark, pltpu.HBM),
                 *after,
             )
+        other_index = lax.ppermute(own_index, "tm", swap)
         received = [
             lax.ppermute(buffer, ("tm", "pix"), [(i, i ^ k) for i in range(count)]) if k else buffer
             for k, buffer in zip(messages, packed)
@@ -313,7 +318,6 @@
         out_specs=in_vmem(1) + in_smem(1),
         name="plan",
     )(cycle_counts.reshape(1, -1))
-    other_index = lax.ppermute(dark_index, "tm", swap)
     mine, send = lax.switch(
         branch[0],
         [functools.partial(exchange, room) for room in rooms],
@@ -322,7 +326,6 @@
         frames.reshape(per_device, n_pix, 2, ROWS, slots),
         dark.reshape(levels, n_pix, 2, ROWS, dark_slots),
         dark_index,
-        other_index,
         cycle_counts,
     )
     theirs = lax.ppermute(send, "tm", swap)

time: 60.2 us -> 59.6 us (0.990)
  waiting for transfers between devices: 22.8 us -> 13.2 us
  starting transfers between devices: 23.5 us -> 32.4 us
    ppermute x15, waiting for transfers between devices: 21.8 us -> 11.1 us  [exchange(): lax.ppermute(buffer, ('tm', 'pix'), [(i, i ^ k) for i in range(count)])]
    ppermute x15, starting transfers between devices: 22.5 us -> 30.8 us  [exchange(): lax.ppermute(buffer, ('tm', 'pix'), [(i, i ^ k) for i in range(count)])]
    ppermute x1, starting transfers between devices: 0.68 us -> 1.51 us  [exchange(): other_index = lax.ppermute(own_index, 'tm', swap)]
    ppermute x1, waiting for transfers between devices: 0.01 us -> 0.82 us  [exchange(): other_index = lax.ppermute(own_index, 'tm', swap)]
  transfers between devices with their start and end apart: 17 -> 17, of which waited for: 9 -> 5; matrix products, arithmetic and copies ran while one was open for 0% -> 0% of each run, Pallas kernels for 9% -> 7%
where the time goes in v5:
time: 59.6 us; the launch traced here: 59.3 us
  starting transfers between devices  32.4 us (54%)
  waiting for transfers between devices  13.2 us (22%)
  Pallas kernels  11.5 us (19%)
  other arithmetic  0.82 us (1%)
  between operations  0.69 us (1%)
  loops' own time  0.61 us (1%)
    ppermute x15, starting transfers between devices, exchange(): lax.ppermute(buffer, ('tm', 'pix'), [(i, i ^ k) for i in range(count)])  30.8 us
    ppermute x15, waiting for transfers between devices, exchange(): lax.ppermute(buffer, ('tm', 'pix'), [(i, i ^ k) for i in range(count)])  11.1 us
    pallas_call x2, Pallas kernels, exchange(): pl.pallas_call(functools.partial(pack_kernel, n_pix, room, group, len(aft...  5.99 us
    pallas_call x1, Pallas kernels, exchange(): pl.pallas_call(functools.partial(gram_kernel, n_pix, per_device, levels,...  4.05 us
    ppermute x1, starting transfers between devices, exchange(): other_index = lax.ppermute(own_index, 'tm', swap)  1.51 us
    pallas_call x1, Pallas kernels, packed_local(): pl.pallas_call(functools.partial(plan_kernel, rooms, slots), out_shape=[j...  1.46 us
    ppermute x1, waiting for transfers between devices, packed_local(): theirs = lax.ppermute(send, 'tm', swap)  1.33 us
  transfers between devices with their start and end apart: 17, of which 5 were waited for; matrix products, arithmetic and copies ran while one was open for 0% of the time, Pallas kernels for 7%

profile of v5, /device:TPU:17, one launch (start us, length us, event | category | flops | bytes accessed | tf_op | source)
XLA Modules:
  0.0 59.3 jit_solution(16576556401465010016)
XLA Ops:
  0.0 1.5 %plan.1 = (f32[16,128]{1,0:T(8,128)S(1)}, s32[1]{0:T(128)}) custom-call(s32[1,256]{1,0:T(1,128)} %bitcast.18), custom_call_target="tpu_custom_call" | custom-call | tf_op jit(solution)/shard_map/plan/pallas_call | solution.py:311
  2.2 54.9 %conditional.1 = ((f32[16,16,32]{2,1,0:T(8,128)S(1)}, f32[16,16,32]{2,1,0:T(8,128)S(1)})) conditional(s32[]{:T(128)} %bitcast.1, (s32[16]{0:T(128)}, s32[2]{0:T(128)S(1)}, f32[16,128]{1,0:T(8,128)S(1)}, bf16[2,8,2,16,2048]{4,3,2,1,0:T(8,128)(2,1)}, bf16[4,8,2,16,256]{4,3,2,1,0:T(8,128)(2,1)}, ...), branch_computations={%region_0.0_spmd, %region_1.0_spmd, %region_2.0_spmd, %region_3.0_... | conditional | bytes 8852672 | solution.py:321
  2.5 1.8 %pack.18 = (bf16[512,128]{1,0:T(8,128)(2,1)S(1)}, bf16[512,128]{1,0:T(8,128)(2,1)S(1)}) custom-call(s32[2]{0:T(128)S(1)} %get-tuple-element.143.place, f32[16,128]{1,0:T(8,128)S(1)} %get-tuple-element.146.position, bf16[2,8,2,16,2048]{4,3,2,1,0:T(8,128)(2,1)} %get-tuple-element.147.frames, bf16[4,8,2,16,256]{4,3,2,1,0:T(8,128)(2,1)} %get-tuple-element.148.dark), custom_call_target="tpu_custom_call" | custom-call | tf_op jit(solution)/shard_map/cond/branch_3_fun/pack/pallas_call | solution.py:268
  4.3 0.2 collective-permute-start.50
  4.6 3.2 %collective-permute-start.49 = (bf16[512,128]{1,0:T(8,128)(2,1)S(1)}, bf16[512,128]{1,0:T(8,128)(2,1)S(1)}, u32[]{:S(2)}, u32[]{:S(2)}) collective-permute-start(bf16[512,128]{1,0:T(8,128)(2,1)S(1)} %get-tuple-element.149.refs_0_), channel_id=1, source_target_pairs={{0,4},{1,5},{2,6},{3,7},{4,0},{5,1},{6,2},{7,3},{8,12},{9,13},{10,... | collective-permute-start | bytes 393224 | tf_op jit(solution)/shard_map/cond/branch_3_fun/ppermute | solution.py:292
  7.8 4.2 %pack.19 = (bf16[512,128]{1,0:T(8,128)(2,1)S(1)}, bf16[512,128]{1,0:T(8,128)(2,1)S(1)}, bf16[512,128]{1,0:T(8,128)(2,1)S(1)}, bf16[512,128]{1,0:T(8,128)(2,1)S(1...) custom-call(s32[2]{0:T(128)S(1)} %get-tuple-element.143.place, ...), custom_call_target="tpu_custom_call" | custom-call | tf_op jit(solution)/shard_map/cond/branch_3_fun/pack/pallas_call | solution.py:268
  11.9 1.3 %collective-permute-start.51 = (bf16[512,128]{1,0:T(8,128)(2,1)S(1)}, bf16[512,128]{1,0:T(8,128)(2,1)S(1)}, u32[]{:S(2)}, u32[]{:S(2)}) collective-permute-start(bf16[512,128]{1,0:T(8,128)(2,1)S(1)} %get-tuple-element.151), channel_id=1, source_target_pairs={{0,1},{1,0},{2,3},{3,2},{4,5},{5,4},{6,7},{7,6},{8,9},{9,8},{10,11... | collective-permute-start | bytes 393224 | tf_op jit(solution)/shard_map/cond/branch_3_fun/ppermute | solution.py:292
  13.2 1.5 %collective-permute-start.48 = (s32[16]{0:T(128)S(1)}, s32[16]{0:T(128)S(1)}, u32[]{:S(2)}, u32[]{:S(2)}) collective-permute-start(s32[16]{0:T(128)S(1)} %copy-done.9), channel_id=1, source_target_pairs={{0,8},{8,0},{1,9},{9,1},{2,10},{10,2},{3,11},{11,3},{4,12},{12,4},... | collective-permute-start | bytes 200 | tf_op jit(solution)/shard_map/cond/branch_3_fun/ppermute | solution.py:290
  14.8 0.8 %collective-permute-done.48.other_index = s32[16]{0:T(128)S(1)} collective-permute-done((s32[16]{0:T(128)S(1)}, s32[16]{0:T(128)S(1)}, u32[]{:S(2)}, u32[]{:S(2)}) %collective-permute-start.48) | collective-permute-done | bytes 96 | tf_op jit(solution)/shard_map/cond/branch_3_fun/ppermute | solution.py:290
  15.6 2.7 %collective-permute-start.54 = (bf16[512,128]{1,0:T(8,128)(2,1)S(1)}, bf16[512,128]{1,0:T(8,128)(2,1)S(1)}, u32[]{:S(2)}, u32[]{:S(2)}) collective-permute-start(bf16[512,128]{1,0:T(8,128)(2,1)S(1)} %get-tuple-element.154), channel_id=1, source_target_pairs={{0,7},{1,6},{2,5},{3,4},{4,3},{5,2},{6,1},{7,0},{8,15},{9,14},{10,... | collective-permute-start | bytes 393224 | tf_op jit(solution)/shard_map/cond/branch_3_fun/ppermute | solution.py:292
  18.3 1.0 %collective-permute-start.55 = (bf16[512,128]{1,0:T(8,128)(2,1)S(1)}, bf16[512,128]{1,0:T(8,128)(2,1)S(1)}, u32[]{:S(2)}, u32[]{:S(2)}) collective-permute-start(bf16[512,128]{1,0:T(8,128)(2,1)S(1)} %get-tuple-element.155), channel_id=1, source_target_pairs={{0,3},{1,2},{2,1},{3,0},{4,7},{5,6},{6,5},{7,4},{8,11},{9,10},{10,... | collective-permute-start | bytes 393224 | tf_op jit(solution)/shard_map/cond/branch_3_fun/ppermute | solution.py:292
  19.3 4.8 %collective-permute-start.56 = (bf16[512,128]{1,0:T(8,128)(2,1)S(1)}, bf16[512,128]{1,0:T(8,128)(2,1)S(1)}, u32[]{:S(2)}, u32[]{:S(2)}) collective-permute-start(bf16[512,128]{1,0:T(8,128)(2,1)S(1)} %get-tuple-element.156), channel_id=1, source_target_pairs={{0,12},{1,13},{2,14},{3,15},{4,8},{5,9},{6,10},{7,11},{8,4},{9,5},... | collective-permute-start | bytes 393224 | tf_op jit(solution)/shard_map/cond/branch_3_fun/ppermute | solution.py:292
  24.2 3.2 %collective-permute-start.57 = (bf16[512,128]{1,0:T(8,128)(2,1)S(1)}, bf16[512,128]{1,0:T(8,128)(2,1)S(1)}, u32[]{:S(2)}, u32[]{:S(2)}) collective-permute-start(bf16[512,128]{1,0:T(8,128)(2,1)S(1)} %get-tuple-element.157), channel_id=1, source_target_pairs={{0,9},{1,8},{2,11},{3,10},{4,13},{5,12},{6,15},{7,14},{8,1},{9,0},... | collective-permute-start | bytes 393224 | tf_op jit(solution)/shard_map/cond/branch_3_fun/ppermute | solution.py:292
  27.4 1.1 %collective-permute-start.58 = (bf16[512,128]{1,0:T(8,128)(2,1)S(1)}, bf16[512,128]{1,0:T(8,128)(2,1)S(1)}, u32[]{:S(2)}, u32[]{:S(2)}) collective-permute-start(bf16[512,128]{1,0:T(8,128)(2,1)S(1)} %get-tuple-element.158), channel_id=1, source_target_pairs={{0,14},{1,15},{2,12},{3,13},{4,10},{5,11},{6,8},{7,9},{8,6},{9,7},... | collective-permute-start | bytes 393224 | tf_op jit(solution)/shard_map/cond/branch_3_fun/ppermute | solution.py:292
  28.5 1.0 %collective-permute-done.54.refs_5_ = bf16[512,128]{1,0:T(8,128)(2,1)S(1)} collective-permute-done((bf16[512,128]{1,0:T(8,128)(2,1)S(1)}, bf16[512,128]{1,0:T(8,128)(2,1)S(1)}, u32[]{:S(2)}, u32[]{:S(2)}) %collective-permute-start.54) | collective-permute-done | bytes 131104 | tf_op jit(solution)/shard_map/cond/branch_3_fun/ppermute | solution.py:292
  29.5 2.3 %collective-permute-start.59 = (bf16[512,128]{1,0:T(8,128)(2,1)S(1)}, bf16[512,128]{1,0:T(8,128)(2,1)S(1)}, u32[]{:S(2)}, u32[]{:S(2)}) collective-permute-start(bf16[512,128]{1,0:T(8,128)(2,1)S(1)} %get-tuple-element.159), channel_id=1, source_target_pairs={{0,10},{1,11},{2,8},{3,9},{4,14},{5,15},{6,12},{7,13},{8,2},{9,3},... | collective-permute-start | bytes 393224 | tf_op jit(solution)/shard_map/cond/branch_3_fun/ppermute | solution.py:292
  31.8 2.3 %collective-permute-start.60 = (bf16[512,128]{1,0:T(8,128)(2,1)S(1)}, bf16[512,128]{1,0:T(8,128)(2,1)S(1)}, u32[]{:S(2)}, u32[]{:S(2)}) collective-permute-start(bf16[512,128]{1,0:T(8,128)(2,1)S(1)} %get-tuple-element.160), channel_id=1, source_target_pairs={{0,13},{1,12},{2,15},{3,14},{4,9},{5,8},{6,11},{7,10},{8,5},{9,4},... | collective-permute-start | bytes 393224 | tf_op jit(solution)/shard_map/cond/branch_3_fun/ppermute | solution.py:292
  34.0 5.4 %collective-permute-start.61 = (bf16[512,128]{1,0:T(8,128)(2,1)S(1)}, bf16[512,128]{1,0:T(8,128)(2,1)S(1)}, u32[]{:S(2)}, u32[]{:S(2)}) collective-permute-start(bf16[512,128]{1,0:T(8,128)(2,1)S(1)} %get-tuple-element.161), channel_id=1, source_target_pairs={{0,11},{1,10},{2,9},{3,8},{4,15},{5,14},{6,13},{7,12},{8,3},{9,2},... | collective-permute-start | bytes 393224 | tf_op jit(solution)/shard_map/cond/branch_3_fun/ppermute | solution.py:292
  39.4 3.3 %collective-permute-start.62 = (bf16[512,128]{1,0:T(8,128)(2,1)S(1)}, bf16[512,128]{1,0:T(8,128)(2,1)S(1)}, u32[]{:S(2)}, u32[]{:S(2)}) collective-permute-start(bf16[512,128]{1,0:T(8,128)(2,1)S(1)} %get-tuple-element.162), channel_id=1, source_target_pairs={{0,15},{1,14},{2,13},{3,12},{4,11},{5,10},{6,9},{7,8},{8,7},{9,6},... | collective-permute-start | bytes 393224 | tf_op jit(solution)/shard_map/cond/branch_3_fun/ppermute | solution.py:292
  42.7 2.2 %collective-permute-done.58.refs_9_ = bf16[512,128]{1,0:T(8,128)(2,1)S(1)} collective-permute-done((bf16[512,128]{1,0:T(8,128)(2,1)S(1)}, bf16[512,128]{1,0:T(8,128)(2,1)S(1)}, u32[]{:S(2)}, u32[]{:S(2)}) %collective-permute-start.58) | collective-permute-done | bytes 131104 | tf_op jit(solution)/shard_map/cond/branch_3_fun/ppermute | solution.py:292
  44.9 7.9 %collective-permute-done.62.refs_13_ = bf16[512,128]{1,0:T(8,128)(2,1)S(1)} collective-permute-done((bf16[512,128]{1,0:T(8,128)(2,1)S(1)}, bf16[512,128]{1,0:T(8,128)(2,1)S(1)}, u32[]{:S(2)}, u32[]{:S(2)}) %collective-permute-start.62) | collective-permute-done | bytes 131104 | tf_op jit(solution)/shard_map/cond/branch_3_fun/ppermute | solution.py:292
  52.8 4.0 %gram.9 = (f32[16,16,32]{2,1,0:T(8,128)S(1)}, f32[16,16,32]{2,1,0:T(8,128)S(1)}) custom-call(s32[2]{0:T(128)S(1)} %get-tuple-element.143.place, s32[16]{0:T(128)S(1)} %copy-done.9, s32[16]{0:T(128)S(1)} %collective-permute-done.48.other_index, s32[256]{0:T(256)S(1)} %copy-done.3, f32[16,128]{1,0:T(8,128)S(1)} %get-tuple-element.146.position, ...), custom_call_target="tpu_custom_call" | custom-call | tf_op jit(solution)/shard_map/cond/branch_3_fun/gram/pallas_call | solution.py:296
  57.2 1.3 %collective-permute-done.96 = f32[16,16,32]{2,1,0:T(8,128)S(1)} collective-permute-done((f32[16,16,32]{2,1,0:T(8,128)S(1)}, f32[16,16,32]{2,1,0:T(8,128)S(1)}, u32[]{:S(2)}, u32[]{:S(2)}) %collective-permute-start.96) | collective-permute-done | bytes 32800 | tf_op jit(solution)/shard_map/ppermute | solution.py:331
  58.6 0.7 %pad_maximum_fusion = f32[32,16,32]{2,1,0:T(8,128)} fusion(f32[16,16,32]{2,1,0:T(8,128)S(1)} %get-tuple-element.218, f32[16,16,32]{2,1,0:T(8,128)S(1)} %get-tuple-element.217), kind=kLoop, calls=%fused_computation | loop fusion | flops 16384 | bytes 131072 | tf_op jit(solution)/shard_map/concatenate | solution.py:333
  (22 shorter events, 0.2 us)
Async XLA Ops:
  2.5 10.8 %copy-start.9 = (s32[16]{0:T(128)S(1)}, s32[16]{0:T(128)}, u32[]{:S(2)}) copy-start(s32[16]{0:T(128)} %get-tuple-element.144.own_index) | copy-start | bytes 196 | tf_op jit(solution)/shard_map/cond
  2.5 50.3 %copy-start.3 = (s32[256]{0:T(256)S(1)}, s32[256]{0:T(256)}, u32[]{:S(2)}) copy-start(s32[256]{0:T(256)} %get-tuple-element.145.cycle_counts) | copy-start | bytes 3076 | tf_op jit(solution)/shard_map/cond
  4.3 11.3 %collective-permute-start.50 = (bf16[512,128]{1,0:T(8,128)(2,1)S(1)}, bf16[512,128]{1,0:T(8,128)(2,1)S(1)}, u32[]{:S(2)}, u32[]{:S(2)}) collective-permute-start(bf16[512,128]{1,0:T(8,128)(2,1)S(1)} %get-tuple-element.150), channel_id=1, source_target_pairs={{0,6},{1,7},{2,4},{3,5},{4,2},{5,3},{6,0},{7,1},{8,14},{9,15},{10,... | collective-permute-start | bytes 393224 | tf_op jit(solution)/shard_map/cond/branch_3_fun/ppermute | solution.py:292
  4.6 13.8 %collective-permute-start.49 = (bf16[512,128]{1,0:T(8,128)(2,1)S(1)}, bf16[512,128]{1,0:T(8,128)(2,1)S(1)}, u32[]{:S(2)}, u32[]{:S(2)}) collective-permute-start(bf16[512,128]{1,0:T(8,128)(2,1)S(1)} %get-tuple-element.149.refs_0_), channel_id=1, source_target_pairs={{0,4},{1,5},{2,6},{3,7},{4,0},{5,1},{6,2},{7,3},{8,12},{9,13},{10,... | collective-permute-start | bytes 393224 | tf_op jit(solution)/shard_map/cond/branch_3_fun/ppermute | solution.py:292
  11.9 7.4 %collective-permute-start.51 = (bf16[512,128]{1,0:T(8,128)(2,1)S(1)}, bf16[512,128]{1,0:T(8,128)(2,1)S(1)}, u32[]{:S(2)}, u32[]{:S(2)}) collective-permute-start(bf16[512,128]{1,0:T(8,128)(2,1)S(1)} %get-tuple-element.151), channel_id=1, source_target_pairs={{0,1},{1,0},{2,3},{3,2},{4,5},{5,4},{6,7},{7,6},{8,9},{9,8},{10,11... | collective-permute-start | bytes 393224 | tf_op jit(solution)/shard_map/cond/branch_3_fun/ppermute | solution.py:292
  13.2 2.3 %collective-permute-start.48 = (s32[16]{0:T(128)S(1)}, s32[16]{0:T(128)S(1)}, u32[]{:S(2)}, u32[]{:S(2)}) collective-permute-start(s32[16]{0:T(128)S(1)} %copy-done.9), channel_id=1, source_target_pairs={{0,8},{8,0},{1,9},{9,1},{2,10},{10,2},{3,11},{11,3},{4,12},{12,4},... | collective-permute-start | bytes 200 | tf_op jit(solution)/shard_map/cond/branch_3_fun/ppermute | solution.py:290
  14.7 9.4 %collective-permute-start.52 = (bf16[512,128]{1,0:T(8,128)(2,1)S(1)}, bf16[512,128]{1,0:T(8,128)(2,1)S(1)}, u32[]{:S(2)}, u32[]{:S(2)}) collective-permute-start(bf16[512,128]{1,0:T(8,128)(2,1)S(1)} %get-tuple-element.152), channel_id=1, source_target_pairs={{0,5},{1,4},{2,7},{3,6},{4,1},{5,0},{6,3},{7,2},{8,13},{9,12},{10,... | collective-permute-start | bytes 393224 | tf_op jit(solution)/shard_map/cond/branch_3_fun/ppermute | solution.py:292
  15.6 11.8 %collective-permute-start.53 = (bf16[512,128]{1,0:T(8,128)(2,1)S(1)}, bf16[512,128]{1,0:T(8,128)(2,1)S(1)}, u32[]{:S(2)}, u32[]{:S(2)}) collective-permute-start(bf16[512,128]{1,0:T(8,128)(2,1)S(1)} %get-tuple-element.153), channel_id=1, source_target_pairs={{0,2},{1,3},{2,0},{3,1},{4,6},{5,7},{6,4},{7,5},{8,10},{9,11},{10,... | collective-permute-start | bytes 393224 | tf_op jit(solution)/shard_map/cond/branch_3_fun/ppermute | solution.py:292
  15.6 13.9 %collective-permute-start.54 = (bf16[512,128]{1,0:T(8,128)(2,1)S(1)}, bf16[512,128]{1,0:T(8,128)(2,1)S(1)}, u32[]{:S(2)}, u32[]{:S(2)}) collective-permute-start(bf16[512,128]{1,0:T(8,128)(2,1)S(1)} %get-tuple-element.154), channel_id=1, source_target_pairs={{0,7},{1,6},{2,5},{3,4},{4,3},{5,2},{6,1},{7,0},{8,15},{9,14},{10,... | collective-permute-start | bytes 393224 | tf_op jit(solution)/shard_map/cond/branch_3_fun/ppermute | solution.py:292
  18.3 13.5 %collective-permute-start.55 = (bf16[512,128]{1,0:T(8,128)(2,1)S(1)}, bf16[512,128]{1,0:T(8,128)(2,1)S(1)}, u32[]{:S(2)}, u32[]{:S(2)}) collective-permute-start(bf16[512,128]{1,0:T(8,128)(2,1)S(1)} %get-tuple-element.155), channel_id=1, source_target_pairs={{0,3},{1,2},{2,1},{3,0},{4,7},{5,6},{6,5},{7,4},{8,11},{9,10},{10,... | collective-permute-start | bytes 393224 | tf_op jit(solution)/shard_map/cond/branch_3_fun/ppermute | solution.py:292
  19.3 14.7 %collective-permute-start.56 = (bf16[512,128]{1,0:T(8,128)(2,1)S(1)}, bf16[512,128]{1,0:T(8,128)(2,1)S(1)}, u32[]{:S(2)}, u32[]{:S(2)}) collective-permute-start(bf16[512,128]{1,0:T(8,128)(2,1)S(1)} %get-tuple-element.156), channel_id=1, source_target_pairs={{0,12},{1,13},{2,14},{3,15},{4,8},{5,9},{6,10},{7,11},{8,4},{9,5},... | collective-permute-start | bytes 393224 | tf_op jit(solution)/shard_map/cond/branch_3_fun/ppermute | solution.py:292
  24.2 15.2 %collective-permute-start.57 = (bf16[512,128]{1,0:T(8,128)(2,1)S(1)}, bf16[512,128]{1,0:T(8,128)(2,1)S(1)}, u32[]{:S(2)}, u32[]{:S(2)}) collective-permute-start(bf16[512,128]{1,0:T(8,128)(2,1)S(1)} %get-tuple-element.157), channel_id=1, source_target_pairs={{0,9},{1,8},{2,11},{3,10},{4,13},{5,12},{6,15},{7,14},{8,1},{9,0},... | collective-permute-start | bytes 393224 | tf_op jit(solution)/shard_map/cond/branch_3_fun/ppermute | solution.py:292
  27.4 17.5 %collective-permute-start.58 = (bf16[512,128]{1,0:T(8,128)(2,1)S(1)}, bf16[512,128]{1,0:T(8,128)(2,1)S(1)}, u32[]{:S(2)}, u32[]{:S(2)}) collective-permute-start(bf16[512,128]{1,0:T(8,128)(2,1)S(1)} %get-tuple-element.158), channel_id=1, source_target_pairs={{0,14},{1,15},{2,12},{3,13},{4,10},{5,11},{6,8},{7,9},{8,6},{9,7},... | collective-permute-start | bytes 393224 | tf_op jit(solution)/shard_map/cond/branch_3_fun/ppermute | solution.py:292
  29.5 15.4 %collective-permute-start.59 = (bf16[512,128]{1,0:T(8,128)(2,1)S(1)}, bf16[512,128]{1,0:T(8,128)(2,1)S(1)}, u32[]{:S(2)}, u32[]{:S(2)}) collective-permute-start(bf16[512,128]{1,0:T(8,128)(2,1)S(1)} %get-tuple-element.159), channel_id=1, source_target_pairs={{0,10},{1,11},{2,8},{3,9},{4,14},{5,15},{6,12},{7,13},{8,2},{9,3},... | collective-permute-start | bytes 393224 | tf_op jit(solution)/shard_map/cond/branch_3_fun/ppermute | solution.py:292
  31.8 13.1 %collective-permute-start.60 = (bf16[512,128]{1,0:T(8,128)(2,1)S(1)}, bf16[512,128]{1,0:T(8,128)(2,1)S(1)}, u32[]{:S(2)}, u32[]{:S(2)}) collective-permute-start(bf16[512,128]{1,0:T(8,128)(2,1)S(1)} %get-tuple-element.160), channel_id=1, source_target_pairs={{0,13},{1,12},{2,15},{3,14},{4,9},{5,8},{6,11},{7,10},{8,5},{9,4},... | collective-permute-start | bytes 393224 | tf_op jit(solution)/shard_map/cond/branch_3_fun/ppermute | solution.py:292
  34.0 10.8 %collective-permute-start.61 = (bf16[512,128]{1,0:T(8,128)(2,1)S(1)}, bf16[512,128]{1,0:T(8,128)(2,1)S(1)}, u32[]{:S(2)}, u32[]{:S(2)}) collective-permute-start(bf16[512,128]{1,0:T(8,128)(2,1)S(1)} %get-tuple-element.161), channel_id=1, source_target_pairs={{0,11},{1,10},{2,9},{3,8},{4,15},{5,14},{6,13},{7,12},{8,3},{9,2},... | collective-permute-start | bytes 393224 | tf_op jit(solution)/shard_map/cond/branch_3_fun/ppermute | solution.py:292
  39.4 13.4 %collective-permute-start.62 = (bf16[512,128]{1,0:T(8,128)(2,1)S(1)}, bf16[512,128]{1,0:T(8,128)(2,1)S(1)}, u32[]{:S(2)}, u32[]{:S(2)}) collective-permute-start(bf16[512,128]{1,0:T(8,128)(2,1)S(1)} %get-tuple-element.162), channel_id=1, source_target_pairs={{0,15},{1,14},{2,13},{3,12},{4,11},{5,10},{6,9},{7,8},{8,7},{9,6},... | collective-permute-start | bytes 393224 | tf_op jit(solution)/shard_map/cond/branch_3_fun/ppermute | solution.py:292
  44.8 7.9 %collective-permute-start.63 = (bf16[512,128]{1,0:T(8,128)(2,1)S(1)}, bf16[512,128]{1,0:T(8,128)(2,1)S(1)}, u32[]{:S(2)}, u32[]{:S(2)}) collective-permute-start(bf16[512,128]{1,0:T(8,128)(2,1)S(1)} %get-tuple-element.163), channel_id=1, source_target_pairs={{0,8},{1,9},{2,10},{3,11},{4,12},{5,13},{6,14},{7,15},{8,0},{9,1},... | collective-permute-start | bytes 393224 | tf_op jit(solution)/shard_map/cond/branch_3_fun/ppermute | solution.py:292
  57.2 1.4 %collective-permute-start.96 = (f32[16,16,32]{2,1,0:T(8,128)S(1)}, f32[16,16,32]{2,1,0:T(8,128)S(1)}, u32[]{:S(2)}, u32[]{:S(2)}) collective-permute-start(f32[16,16,32]{2,1,0:T(8,128)S(1)} %get-tuple-element.216), channel_id=1, source_target_pairs={{0,8},{8,0},{1,9},{9,1},{2,10},{10,2},{3,11},{11,3},{4,12},{12,4},... | collective-permute-start | bytes 98312 | tf_op jit(solution)/shard_map/ppermute | solution.py:331

commit v6 on v5

--- a/solution.py
+++ b/solution.py
@@ -192,9 +192,12 @@
         source, half = me ^ (k % n_pix), core ^ (k // n_pix)
         index = own_index if k < n_pix else other_index
         if room < units:
-            packed = [bufs[k][pl.ds(upper_row + f * room, room), :] for f in range(per_device)]
+            packed = bufs[k][pl.ds(upper_row, per_device * room), :].astype(jnp.float32)
+            packed = [packed[f * room : (f + 1) * room] for f in range(per_device)]
             upper = jnp.dot(
-                chosen, jnp.concatenate(packed, axis=1), preferred_element_type=jnp.float32
+                chosen,
+                jnp.concatenate(packed, axis=1).astype(jnp.bfloat16),
+                preferred_element_type=jnp.float32,
             )
         for f in range(per_device):
             frame = source * per_device + f
@@ -219,9 +222,11 @@
     )
     products = lax.dot_general(every, every, contract, preferred_element_type=jnp.float32)
     products = jnp.concatenate([products, totals], axis=0)
-    row = lax.broadcasted_iota(jnp.int32, products.shape, 0)
-    col = lax.broadcasted_iota(jnp.int32, products.shape, 1)
-    products = jnp.where(row % ROWS == col % ROWS, products, 0.0)
+    same = (
+        lax.broadcasted_iota(jnp.int32, (ROWS, width), 0)
+        == lax.broadcasted_iota(jnp.int32, (ROWS, width), 1) % ROWS
+    )
+    products = jnp.where(same[None], products.reshape(-1, ROWS, width), 0.0).reshape(-1, width)
     frame = lax.broadcasted_iota(jnp.int32, (width, LANES), 0) // ROWS
     lane = lax.broadcasted_iota(jnp.int32, (width, LANES), 1)
     place_out = (frame + core * frames_half) % n_frames
@@ -340,8 +345,10 @@
 
     def local(frames, dark, dark_index, cycle_counts):
         owned, slots = frames.shape[1] // n_pix, frames.shape[2]
-        fits = n_tm == 2 and owned == 2 * ROWS and slots % (2 * LANES) == 0 and n_pix & (n_pix - 1) == 0 and n_pix <= 8
-        fits = fits and dark.shape[0] % 2 == 0 and dark.shape[2] % LANES == 0 and slots == dark.shape[2] * n_pix
+        fits = n_tm == 2 and owned == 2 * ROWS and n_pix & (n_pix - 1) == 0 and 2 < n_pix <= 8
+        fits = fits and slots % (2 * LANES) == 0 and slots // 2 // LANES * ROWS % LANES == 0
+        fits = fits and 4 * frames.shape[0] * n_pix <= LANES
+        fits = fits and frames.shape[0] % 2 == 0 and dark.shape[0] % 2 == 0 and dark.shape[2] % LANES == 0 and slots == dark.shape[2] * n_pix
         return (packed_local if fits else plain_local)(frames, dark, dark_index, cycle_counts)
 
     in_specs = (

time: 59.6 us -> 59 us (0.990); the launches traced: 59.3 us -> 58 us
  starting transfers between devices: 32.4 us -> 31.4 us
    ppermute x15, starting transfers between devices: 30.8 us -> 29.8 us  [exchange(): lax.ppermute(buffer, ('tm', 'pix'), [(i, i ^ k) for i in range(count)])]
  transfers between devices with their start and end apart: 17 -> 17, of which waited for: 5 -> 6; matrix products, arithmetic and copies ran while one was open for 0% -> 0% of each run, Pallas kernels for 7% -> 7%
where the time goes in v6:
time: 59 us; the launch traced here: 58 us
  starting transfers between devices  31.4 us (53%)
  waiting for transfers between devices  12.9 us (22%)
  Pallas kernels  11.4 us (19%)
  other arithmetic  0.82 us (1%)
  loops' own time  0.8 us (1%)
  between operations  0.69 us (1%)
    ppermute x15, starting transfers between devices, exchange(): lax.ppermute(buffer, ('tm', 'pix'), [(i, i ^ k) for i in range(count)])  29.8 us
    ppermute x15, waiting for transfers between devices, exchange(): lax.ppermute(buffer, ('tm', 'pix'), [(i, i ^ k) for i in range(count)])  10.7 us
    pallas_call x2, Pallas kernels, exchange(): pl.pallas_call(functools.partial(pack_kernel, n_pix, room, group, len(aft...  5.97 us
    pallas_call x1, Pallas kernels, exchange(): pl.pallas_call(functools.partial(gram_kernel, n_pix, per_device, levels,...  3.95 us
    ppermute x1, starting transfers between devices, exchange(): other_index = lax.ppermute(own_index, 'tm', swap)  1.52 us
    pallas_call x1, Pallas kernels, packed_local(): pl.pallas_call(functools.partial(plan_kernel, rooms, slots), out_shape=[j...  1.46 us
    ppermute x1, waiting for transfers between devices, packed_local(): theirs = lax.ppermute(send, 'tm', swap)  1.33 us
  transfers between devices with their start and end apart: 17, of which 6 were waited for; matrix products, arithmetic and copies ran while one was open for 0% of the time, Pallas kernels for 7%

profile of v6, /device:TPU:17, one launch (start us, length us, event | category | flops | bytes accessed | tf_op | source)
XLA Modules:
  0.0 58.0 jit_solution(9359577978687971143)
XLA Ops:
  0.0 1.5 %plan.1 = (f32[16,128]{1,0:T(8,128)S(1)}, s32[1]{0:T(128)}) custom-call(s32[1,256]{1,0:T(1,128)} %bitcast.18), custom_call_target="tpu_custom_call" | custom-call | tf_op jit(solution)/shard_map/plan/pallas_call | solution.py:316
  2.2 53.6 %conditional.1 = ((f32[16,16,32]{2,1,0:T(8,128)S(1)}, f32[16,16,32]{2,1,0:T(8,128)S(1)})) conditional(s32[]{:T(128)} %bitcast.1, (s32[16]{0:T(128)}, s32[2]{0:T(128)S(1)}, f32[16,128]{1,0:T(8,128)S(1)}, bf16[2,8,2,16,2048]{4,3,2,1,0:T(8,128)(2,1)}, bf16[4,8,2,16,256]{4,3,2,1,0:T(8,128)(2,1)}, ...), branch_computations={%region_0.0_spmd, %region_1.0_spmd, %region_2.0_spmd, %region_3.0_... | conditional | bytes 8852672 | solution.py:326
  2.4 1.8 %pack.16 = (bf16[496,128]{1,0:T(8,128)(2,1)S(1)}, bf16[496,128]{1,0:T(8,128)(2,1)S(1)}) custom-call(s32[2]{0:T(128)S(1)} %get-tuple-element.121.place, f32[16,128]{1,0:T(8,128)S(1)} %get-tuple-element.124.position, bf16[2,8,2,16,2048]{4,3,2,1,0:T(8,128)(2,1)} %get-tuple-element.125.frames, bf16[4,8,2,16,256]{4,3,2,1,0:T(8,128)(2,1)} %get-tuple-element.126.dark), custom_call_target="tpu_custom_call" | custom-call | tf_op jit(solution)/shard_map/cond/branch_2_fun/pack/pallas_call | solution.py:273
  4.5 3.2 %collective-permute-start.33 = (bf16[496,128]{1,0:T(8,128)(2,1)S(1)}, bf16[496,128]{1,0:T(8,128)(2,1)S(1)}, u32[]{:S(2)}, u32[]{:S(2)}) collective-permute-start(bf16[496,128]{1,0:T(8,128)(2,1)S(1)} %get-tuple-element.127.refs_0_), channel_id=1, source_target_pairs={{0,4},{1,5},{2,6},{3,7},{4,0},{5,1},{6,2},{7,3},{8,12},{9,13},{10,... | collective-permute-start | bytes 380936 | tf_op jit(solution)/shard_map/cond/branch_2_fun/ppermute | solution.py:297
  7.7 4.1 %pack.17 = (bf16[496,128]{1,0:T(8,128)(2,1)S(1)}, bf16[496,128]{1,0:T(8,128)(2,1)S(1)}, bf16[496,128]{1,0:T(8,128)(2,1)S(1)}, bf16[496,128]{1,0:T(8,128)(2,1)S(1...) custom-call(s32[2]{0:T(128)S(1)} %get-tuple-element.121.place, ...), custom_call_target="tpu_custom_call" | custom-call | tf_op jit(solution)/shard_map/cond/branch_2_fun/pack/pallas_call | solution.py:273
  11.9 1.3 %collective-permute-start.35 = (bf16[496,128]{1,0:T(8,128)(2,1)S(1)}, bf16[496,128]{1,0:T(8,128)(2,1)S(1)}, u32[]{:S(2)}, u32[]{:S(2)}) collective-permute-start(bf16[496,128]{1,0:T(8,128)(2,1)S(1)} %get-tuple-element.129), channel_id=1, source_target_pairs={{0,1},{1,0},{2,3},{3,2},{4,5},{5,4},{6,7},{7,6},{8,9},{9,8},{10,11... | collective-permute-start | bytes 380936 | tf_op jit(solution)/shard_map/cond/branch_2_fun/ppermute | solution.py:297
  13.2 1.5 %collective-permute-start.32 = (s32[16]{0:T(128)S(1)}, s32[16]{0:T(128)S(1)}, u32[]{:S(2)}, u32[]{:S(2)}) collective-permute-start(s32[16]{0:T(128)S(1)} %copy-done.8), channel_id=1, source_target_pairs={{0,8},{8,0},{1,9},{9,1},{2,10},{10,2},{3,11},{11,3},{4,12},{12,4},... | collective-permute-start | bytes 200 | tf_op jit(solution)/shard_map/cond/branch_2_fun/ppermute | solution.py:295
  14.7 0.8 %collective-permute-done.32.other_index = s32[16]{0:T(128)S(1)} collective-permute-done((s32[16]{0:T(128)S(1)}, s32[16]{0:T(128)S(1)}, u32[]{:S(2)}, u32[]{:S(2)}) %collective-permute-start.32) | collective-permute-done | bytes 96 | tf_op jit(solution)/shard_map/cond/branch_2_fun/ppermute | solution.py:295
  15.5 2.7 %collective-permute-start.38 = (bf16[496,128]{1,0:T(8,128)(2,1)S(1)}, bf16[496,128]{1,0:T(8,128)(2,1)S(1)}, u32[]{:S(2)}, u32[]{:S(2)}) collective-permute-start(bf16[496,128]{1,0:T(8,128)(2,1)S(1)} %get-tuple-element.132), channel_id=1, source_target_pairs={{0,7},{1,6},{2,5},{3,4},{4,3},{5,2},{6,1},{7,0},{8,15},{9,14},{10,... | collective-permute-start | bytes 380936 | tf_op jit(solution)/shard_map/cond/branch_2_fun/ppermute | solution.py:297
  18.3 0.9 %collective-permute-start.39 = (bf16[496,128]{1,0:T(8,128)(2,1)S(1)}, bf16[496,128]{1,0:T(8,128)(2,1)S(1)}, u32[]{:S(2)}, u32[]{:S(2)}) collective-permute-start(bf16[496,128]{1,0:T(8,128)(2,1)S(1)} %get-tuple-element.133), channel_id=1, source_target_pairs={{0,3},{1,2},{2,1},{3,0},{4,7},{5,6},{6,5},{7,4},{8,11},{9,10},{10,... | collective-permute-start | bytes 380936 | tf_op jit(solution)/shard_map/cond/branch_2_fun/ppermute | solution.py:297
  19.2 4.5 %collective-permute-start.40 = (bf16[496,128]{1,0:T(8,128)(2,1)S(1)}, bf16[496,128]{1,0:T(8,128)(2,1)S(1)}, u32[]{:S(2)}, u32[]{:S(2)}) collective-permute-start(bf16[496,128]{1,0:T(8,128)(2,1)S(1)} %get-tuple-element.134), channel_id=1, source_target_pairs={{0,12},{1,13},{2,14},{3,15},{4,8},{5,9},{6,10},{7,11},{8,4},{9,5},... | collective-permute-start | bytes 380936 | tf_op jit(solution)/shard_map/cond/branch_2_fun/ppermute | solution.py:297
  23.7 2.9 %collective-permute-start.41 = (bf16[496,128]{1,0:T(8,128)(2,1)S(1)}, bf16[496,128]{1,0:T(8,128)(2,1)S(1)}, u32[]{:S(2)}, u32[]{:S(2)}) collective-permute-start(bf16[496,128]{1,0:T(8,128)(2,1)S(1)} %get-tuple-element.135), channel_id=1, source_target_pairs={{0,9},{1,8},{2,11},{3,10},{4,13},{5,12},{6,15},{7,14},{8,1},{9,0},... | collective-permute-start | bytes 380936 | tf_op jit(solution)/shard_map/cond/branch_2_fun/ppermute | solution.py:297
  26.6 1.2 %collective-permute-start.42 = (bf16[496,128]{1,0:T(8,128)(2,1)S(1)}, bf16[496,128]{1,0:T(8,128)(2,1)S(1)}, u32[]{:S(2)}, u32[]{:S(2)}) collective-permute-start(bf16[496,128]{1,0:T(8,128)(2,1)S(1)} %get-tuple-element.136), channel_id=1, source_target_pairs={{0,14},{1,15},{2,12},{3,13},{4,10},{5,11},{6,8},{7,9},{8,6},{9,7},... | collective-permute-start | bytes 380936 | tf_op jit(solution)/shard_map/cond/branch_2_fun/ppermute | solution.py:297
  27.8 0.9 %collective-permute-done.38.refs_5_ = bf16[496,128]{1,0:T(8,128)(2,1)S(1)} collective-permute-done((bf16[496,128]{1,0:T(8,128)(2,1)S(1)}, bf16[496,128]{1,0:T(8,128)(2,1)S(1)}, u32[]{:S(2)}, u32[]{:S(2)}) %collective-permute-start.38) | collective-permute-done | bytes 127008 | tf_op jit(solution)/shard_map/cond/branch_2_fun/ppermute | solution.py:297
  28.7 2.3 %collective-permute-start.43 = (bf16[496,128]{1,0:T(8,128)(2,1)S(1)}, bf16[496,128]{1,0:T(8,128)(2,1)S(1)}, u32[]{:S(2)}, u32[]{:S(2)}) collective-permute-start(bf16[496,128]{1,0:T(8,128)(2,1)S(1)} %get-tuple-element.137), channel_id=1, source_target_pairs={{0,10},{1,11},{2,8},{3,9},{4,14},{5,15},{6,12},{7,13},{8,2},{9,3},... | collective-permute-start | bytes 380936 | tf_op jit(solution)/shard_map/cond/branch_2_fun/ppermute | solution.py:297
  31.0 2.4 %collective-permute-start.44 = (bf16[496,128]{1,0:T(8,128)(2,1)S(1)}, bf16[496,128]{1,0:T(8,128)(2,1)S(1)}, u32[]{:S(2)}, u32[]{:S(2)}) collective-permute-start(bf16[496,128]{1,0:T(8,128)(2,1)S(1)} %get-tuple-element.138), channel_id=1, source_target_pairs={{0,13},{1,12},{2,15},{3,14},{4,9},{5,8},{6,11},{7,10},{8,5},{9,4},... | collective-permute-start | bytes 380936 | tf_op jit(solution)/shard_map/cond/branch_2_fun/ppermute | solution.py:297
  33.3 5.0 %collective-permute-start.45 = (bf16[496,128]{1,0:T(8,128)(2,1)S(1)}, bf16[496,128]{1,0:T(8,128)(2,1)S(1)}, u32[]{:S(2)}, u32[]{:S(2)}) collective-permute-start(bf16[496,128]{1,0:T(8,128)(2,1)S(1)} %get-tuple-element.139), channel_id=1, source_target_pairs={{0,11},{1,10},{2,9},{3,8},{4,15},{5,14},{6,13},{7,12},{8,3},{9,2},... | collective-permute-start | bytes 380936 | tf_op jit(solution)/shard_map/cond/branch_2_fun/ppermute | solution.py:297
  38.4 3.1 %collective-permute-start.46 = (bf16[496,128]{1,0:T(8,128)(2,1)S(1)}, bf16[496,128]{1,0:T(8,128)(2,1)S(1)}, u32[]{:S(2)}, u32[]{:S(2)}) collective-permute-start(bf16[496,128]{1,0:T(8,128)(2,1)S(1)} %get-tuple-element.140), channel_id=1, source_target_pairs={{0,15},{1,14},{2,13},{3,12},{4,11},{5,10},{6,9},{7,8},{8,7},{9,6},... | collective-permute-start | bytes 380936 | tf_op jit(solution)/shard_map/cond/branch_2_fun/ppermute | solution.py:297
  41.5 2.1 %collective-permute-done.42.refs_9_ = bf16[496,128]{1,0:T(8,128)(2,1)S(1)} collective-permute-done((bf16[496,128]{1,0:T(8,128)(2,1)S(1)}, bf16[496,128]{1,0:T(8,128)(2,1)S(1)}, u32[]{:S(2)}, u32[]{:S(2)}) %collective-permute-start.42) | collective-permute-done | bytes 127008 | tf_op jit(solution)/shard_map/cond/branch_2_fun/ppermute | solution.py:297
  43.6 1.2 %collective-permute-done.45.refs_12_ = bf16[496,128]{1,0:T(8,128)(2,1)S(1)} collective-permute-done((bf16[496,128]{1,0:T(8,128)(2,1)S(1)}, bf16[496,128]{1,0:T(8,128)(2,1)S(1)}, u32[]{:S(2)}, u32[]{:S(2)}) %collective-permute-start.45) | collective-permute-done | bytes 127008 | tf_op jit(solution)/shard_map/cond/branch_2_fun/ppermute | solution.py:297
  44.8 6.5 %collective-permute-done.46.refs_13_ = bf16[496,128]{1,0:T(8,128)(2,1)S(1)} collective-permute-done((bf16[496,128]{1,0:T(8,128)(2,1)S(1)}, bf16[496,128]{1,0:T(8,128)(2,1)S(1)}, u32[]{:S(2)}, u32[]{:S(2)}) %collective-permute-start.46) | collective-permute-done | bytes 127008 | tf_op jit(solution)/shard_map/cond/branch_2_fun/ppermute | solution.py:297
  51.3 4.0 %gram.8 = (f32[16,16,32]{2,1,0:T(8,128)S(1)}, f32[16,16,32]{2,1,0:T(8,128)S(1)}) custom-call(s32[2]{0:T(128)S(1)} %get-tuple-element.121.place, s32[16]{0:T(128)S(1)} %copy-done.8, s32[16]{0:T(128)S(1)} %collective-permute-done.32.other_index, s32[256]{0:T(256)S(1)} %copy-done.2, f32[16,128]{1,0:T(8,128)S(1)} %get-tuple-element.124.position, ...), custom_call_target="tpu_custom_call" | custom-call | tf_op jit(solution)/shard_map/cond/branch_2_fun/gram/pallas_call | solution.py:301
  55.9 1.3 %collective-permute-done.96 = f32[16,16,32]{2,1,0:T(8,128)S(1)} collective-permute-done((f32[16,16,32]{2,1,0:T(8,128)S(1)}, f32[16,16,32]{2,1,0:T(8,128)S(1)}, u32[]{:S(2)}, u32[]{:S(2)}) %collective-permute-start.96) | collective-permute-done | bytes 32800 | tf_op jit(solution)/shard_map/ppermute | solution.py:336
  57.3 0.7 %pad_maximum_fusion = f32[32,16,32]{2,1,0:T(8,128)} fusion(f32[16,16,32]{2,1,0:T(8,128)S(1)} %get-tuple-element.218, f32[16,16,32]{2,1,0:T(8,128)S(1)} %get-tuple-element.217), kind=kLoop, calls=%fused_computation | loop fusion | flops 16384 | bytes 131072 | tf_op jit(solution)/shard_map/concatenate | solution.py:338
  (22 shorter events, 0.5 us)
Async XLA Ops:
  2.4 10.8 %copy-start.8 = (s32[16]{0:T(128)S(1)}, s32[16]{0:T(128)}, u32[]{:S(2)}) copy-start(s32[16]{0:T(128)} %get-tuple-element.122.own_index) | copy-start | bytes 196 | tf_op jit(solution)/shard_map/cond
  2.4 48.9 %copy-start.2 = (s32[256]{0:T(256)S(1)}, s32[256]{0:T(256)}, u32[]{:S(2)}) copy-start(s32[256]{0:T(256)} %get-tuple-element.123.cycle_counts) | copy-start | bytes 3076 | tf_op jit(solution)/shard_map/cond
  4.3 11.2 %collective-permute-start.34 = (bf16[496,128]{1,0:T(8,128)(2,1)S(1)}, bf16[496,128]{1,0:T(8,128)(2,1)S(1)}, u32[]{:S(2)}, u32[]{:S(2)}) collective-permute-start(bf16[496,128]{1,0:T(8,128)(2,1)S(1)} %get-tuple-element.128), channel_id=1, source_target_pairs={{0,6},{1,7},{2,4},{3,5},{4,2},{5,3},{6,0},{7,1},{8,14},{9,15},{10,... | collective-permute-start | bytes 380936 | tf_op jit(solution)/shard_map/cond/branch_2_fun/ppermute | solution.py:297
  4.5 13.7 %collective-permute-start.33 = (bf16[496,128]{1,0:T(8,128)(2,1)S(1)}, bf16[496,128]{1,0:T(8,128)(2,1)S(1)}, u32[]{:S(2)}, u32[]{:S(2)}) collective-permute-start(bf16[496,128]{1,0:T(8,128)(2,1)S(1)} %get-tuple-element.127.refs_0_), channel_id=1, source_target_pairs={{0,4},{1,5},{2,6},{3,7},{4,0},{5,1},{6,2},{7,3},{8,12},{9,13},{10,... | collective-permute-start | bytes 380936 | tf_op jit(solution)/shard_map/cond/branch_2_fun/ppermute | solution.py:297
  11.9 7.3 %collective-permute-start.35 = (bf16[496,128]{1,0:T(8,128)(2,1)S(1)}, bf16[496,128]{1,0:T(8,128)(2,1)S(1)}, u32[]{:S(2)}, u32[]{:S(2)}) collective-permute-start(bf16[496,128]{1,0:T(8,128)(2,1)S(1)} %get-tuple-element.129), channel_id=1, source_target_pairs={{0,1},{1,0},{2,3},{3,2},{4,5},{5,4},{6,7},{7,6},{8,9},{9,8},{10,11... | collective-permute-start | bytes 380936 | tf_op jit(solution)/shard_map/cond/branch_2_fun/ppermute | solution.py:297
  13.2 2.3 %collective-permute-start.32 = (s32[16]{0:T(128)S(1)}, s32[16]{0:T(128)S(1)}, u32[]{:S(2)}, u32[]{:S(2)}) collective-permute-start(s32[16]{0:T(128)S(1)} %copy-done.8), channel_id=1, source_target_pairs={{0,8},{8,0},{1,9},{9,1},{2,10},{10,2},{3,11},{11,3},{4,12},{12,4},... | collective-permute-start | bytes 200 | tf_op jit(solution)/shard_map/cond/branch_2_fun/ppermute | solution.py:295
  14.7 9.0 %collective-permute-start.36 = (bf16[496,128]{1,0:T(8,128)(2,1)S(1)}, bf16[496,128]{1,0:T(8,128)(2,1)S(1)}, u32[]{:S(2)}, u32[]{:S(2)}) collective-permute-start(bf16[496,128]{1,0:T(8,128)(2,1)S(1)} %get-tuple-element.130), channel_id=1, source_target_pairs={{0,5},{1,4},{2,7},{3,6},{4,1},{5,0},{6,3},{7,2},{8,13},{9,12},{10,... | collective-permute-start | bytes 380936 | tf_op jit(solution)/shard_map/cond/branch_2_fun/ppermute | solution.py:297
  15.5 11.1 %collective-permute-start.37 = (bf16[496,128]{1,0:T(8,128)(2,1)S(1)}, bf16[496,128]{1,0:T(8,128)(2,1)S(1)}, u32[]{:S(2)}, u32[]{:S(2)}) collective-permute-start(bf16[496,128]{1,0:T(8,128)(2,1)S(1)} %get-tuple-element.131), channel_id=1, source_target_pairs={{0,2},{1,3},{2,0},{3,1},{4,6},{5,7},{6,4},{7,5},{8,10},{9,11},{10,... | collective-permute-start | bytes 380936 | tf_op jit(solution)/shard_map/cond/branch_2_fun/ppermute | solution.py:297
  15.5 13.2 %collective-permute-start.38 = (bf16[496,128]{1,0:T(8,128)(2,1)S(1)}, bf16[496,128]{1,0:T(8,128)(2,1)S(1)}, u32[]{:S(2)}, u32[]{:S(2)}) collective-permute-start(bf16[496,128]{1,0:T(8,128)(2,1)S(1)} %get-tuple-element.132), channel_id=1, source_target_pairs={{0,7},{1,6},{2,5},{3,4},{4,3},{5,2},{6,1},{7,0},{8,15},{9,14},{10,... | collective-permute-start | bytes 380936 | tf_op jit(solution)/shard_map/cond/branch_2_fun/ppermute | solution.py:297
  18.3 12.7 %collective-permute-start.39 = (bf16[496,128]{1,0:T(8,128)(2,1)S(1)}, bf16[496,128]{1,0:T(8,128)(2,1)S(1)}, u32[]{:S(2)}, u32[]{:S(2)}) collective-permute-start(bf16[496,128]{1,0:T(8,128)(2,1)S(1)} %get-tuple-element.133), channel_id=1, source_target_pairs={{0,3},{1,2},{2,1},{3,0},{4,7},{5,6},{6,5},{7,4},{8,11},{9,10},{10,... | collective-permute-start | bytes 380936 | tf_op jit(solution)/shard_map/cond/branch_2_fun/ppermute | solution.py:297
  19.2 14.2 %collective-permute-start.40 = (bf16[496,128]{1,0:T(8,128)(2,1)S(1)}, bf16[496,128]{1,0:T(8,128)(2,1)S(1)}, u32[]{:S(2)}, u32[]{:S(2)}) collective-permute-start(bf16[496,128]{1,0:T(8,128)(2,1)S(1)} %get-tuple-element.134), channel_id=1, source_target_pairs={{0,12},{1,13},{2,14},{3,15},{4,8},{5,9},{6,10},{7,11},{8,4},{9,5},... | collective-permute-start | bytes 380936 | tf_op jit(solution)/shard_map/cond/branch_2_fun/ppermute | solution.py:297
  23.7 14.7 %collective-permute-start.41 = (bf16[496,128]{1,0:T(8,128)(2,1)S(1)}, bf16[496,128]{1,0:T(8,128)(2,1)S(1)}, u32[]{:S(2)}, u32[]{:S(2)}) collective-permute-start(bf16[496,128]{1,0:T(8,128)(2,1)S(1)} %get-tuple-element.135), channel_id=1, source_target_pairs={{0,9},{1,8},{2,11},{3,10},{4,13},{5,12},{6,15},{7,14},{8,1},{9,0},... | collective-permute-start | bytes 380936 | tf_op jit(solution)/shard_map/cond/branch_2_fun/ppermute | solution.py:297
  26.6 17.0 %collective-permute-start.42 = (bf16[496,128]{1,0:T(8,128)(2,1)S(1)}, bf16[496,128]{1,0:T(8,128)(2,1)S(1)}, u32[]{:S(2)}, u32[]{:S(2)}) collective-permute-start(bf16[496,128]{1,0:T(8,128)(2,1)S(1)} %get-tuple-element.136), channel_id=1, source_target_pairs={{0,14},{1,15},{2,12},{3,13},{4,10},{5,11},{6,8},{7,9},{8,6},{9,7},... | collective-permute-start | bytes 380936 | tf_op jit(solution)/shard_map/cond/branch_2_fun/ppermute | solution.py:297
  28.7 15.0 %collective-permute-start.43 = (bf16[496,128]{1,0:T(8,128)(2,1)S(1)}, bf16[496,128]{1,0:T(8,128)(2,1)S(1)}, u32[]{:S(2)}, u32[]{:S(2)}) collective-permute-start(bf16[496,128]{1,0:T(8,128)(2,1)S(1)} %get-tuple-element.137), channel_id=1, source_target_pairs={{0,10},{1,11},{2,8},{3,9},{4,14},{5,15},{6,12},{7,13},{8,2},{9,3},... | collective-permute-start | bytes 380936 | tf_op jit(solution)/shard_map/cond/branch_2_fun/ppermute | solution.py:297
  31.0 12.7 %collective-permute-start.44 = (bf16[496,128]{1,0:T(8,128)(2,1)S(1)}, bf16[496,128]{1,0:T(8,128)(2,1)S(1)}, u32[]{:S(2)}, u32[]{:S(2)}) collective-permute-start(bf16[496,128]{1,0:T(8,128)(2,1)S(1)} %get-tuple-element.138), channel_id=1, source_target_pairs={{0,13},{1,12},{2,15},{3,14},{4,9},{5,8},{6,11},{7,10},{8,5},{9,4},... | collective-permute-start | bytes 380936 | tf_op jit(solution)/shard_map/cond/branch_2_fun/ppermute | solution.py:297
  33.3 11.5 %collective-permute-start.45 = (bf16[496,128]{1,0:T(8,128)(2,1)S(1)}, bf16[496,128]{1,0:T(8,128)(2,1)S(1)}, u32[]{:S(2)}, u32[]{:S(2)}) collective-permute-start(bf16[496,128]{1,0:T(8,128)(2,1)S(1)} %get-tuple-element.139), channel_id=1, source_target_pairs={{0,11},{1,10},{2,9},{3,8},{4,15},{5,14},{6,13},{7,12},{8,3},{9,2},... | collective-permute-start | bytes 380936 | tf_op jit(solution)/shard_map/cond/branch_2_fun/ppermute | solution.py:297
  38.4 13.0 %collective-permute-start.46 = (bf16[496,128]{1,0:T(8,128)(2,1)S(1)}, bf16[496,128]{1,0:T(8,128)(2,1)S(1)}, u32[]{:S(2)}, u32[]{:S(2)}) collective-permute-start(bf16[496,128]{1,0:T(8,128)(2,1)S(1)} %get-tuple-element.140), channel_id=1, source_target_pairs={{0,15},{1,14},{2,13},{3,12},{4,11},{5,10},{6,9},{7,8},{8,7},{9,6},... | collective-permute-start | bytes 380936 | tf_op jit(solution)/shard_map/cond/branch_2_fun/ppermute | solution.py:297
  43.6 7.7 %collective-permute-start.47 = (bf16[496,128]{1,0:T(8,128)(2,1)S(1)}, bf16[496,128]{1,0:T(8,128)(2,1)S(1)}, u32[]{:S(2)}, u32[]{:S(2)}) collective-permute-start(bf16[496,128]{1,0:T(8,128)(2,1)S(1)} %get-tuple-element.141), channel_id=1, source_target_pairs={{0,8},{1,9},{2,10},{3,11},{4,12},{5,13},{6,14},{7,15},{8,0},{9,1},... | collective-permute-start | bytes 380936 | tf_op jit(solution)/shard_map/cond/branch_2_fun/ppermute | solution.py:297
  55.8 1.4 %collective-permute-start.96 = (f32[16,16,32]{2,1,0:T(8,128)S(1)}, f32[16,16,32]{2,1,0:T(8,128)S(1)}, u32[]{:S(2)}, u32[]{:S(2)}) collective-permute-start(f32[16,16,32]{2,1,0:T(8,128)S(1)} %get-tuple-element.216), channel_id=1, source_target_pairs={{0,8},{8,0},{1,9},{9,1},{2,10},{10,2},{3,11},{11,3},{4,12},{12,4},... | collective-permute-start | bytes 98312 | tf_op jit(solution)/shard_map/ppermute | solution.py:336

commit v7 on v6

--- a/solution.py
+++ b/solution.py
@@ -142,16 +142,15 @@
             outs[n][pl.ds(row, per_device * room), :] = live.astype(jnp.bfloat16)
 
 
-def split3(x):
+def split2(x):
     high = x.astype(jnp.bfloat16)
     rest = x - high.astype(jnp.float32)
     middle = rest.astype(jnp.bfloat16)
-    low = (rest - middle.astype(jnp.float32)).astype(jnp.bfloat16)
-    return high, middle, low
+    return high, middle
 
 
 def pick(x, chosen):
-    return sum(jnp.dot(part, chosen, preferred_element_type=jnp.float32) for part in split3(x))
+    return sum(jnp.dot(part, chosen, preferred_element_type=jnp.float32) for part in split2(x))
 
 
 def gram_kernel(

time: 59 us -> 59.4 us (level); the launches traced: 58 us -> 59.1 us
  starting transfers between devices: 31.4 us -> 32.4 us
    ppermute x15, starting transfers between devices: 29.8 us -> 30.8 us  [exchange(): lax.ppermute(buffer, ('tm', 'pix'), [(i, i ^ k) for i in range(count)])]
  transfers between devices with their start and end apart: 17 -> 17, of which waited for: 6 -> 5; matrix products, arithmetic and copies ran while one was open for 0% -> 0% of each run, Pallas kernels for 7% -> 7%
where the time goes in v7:
time: 59.4 us; the launch traced here: 59.1 us
  starting transfers between devices  32.4 us (55%)
  waiting for transfers between devices  13.2 us (22%)
  Pallas kernels  11.3 us (19%)
  other arithmetic  0.82 us (1%)
  between operations  0.69 us (1%)
  loops' own time  0.61 us (1%)
    ppermute x15, starting transfers between devices, exchange(): lax.ppermute(buffer, ('tm', 'pix'), [(i, i ^ k) for i in range(count)])  30.8 us
    ppermute x15, waiting for transfers between devices, exchange(): lax.ppermute(buffer, ('tm', 'pix'), [(i, i ^ k) for i in range(count)])  11.1 us
    pallas_call x2, Pallas kernels, exchange(): pl.pallas_call(functools.partial(pack_kernel, n_pix, room, group, len(aft...  5.99 us
    pallas_call x1, Pallas kernels, exchange(): pl.pallas_call(functools.partial(gram_kernel, n_pix, per_device, levels,...  3.83 us
    ppermute x1, starting transfers between devices, exchange(): other_index = lax.ppermute(own_index, 'tm', swap)  1.51 us
    pallas_call x1, Pallas kernels, packed_local(): pl.pallas_call(functools.partial(plan_kernel, rooms, slots), out_shape=[j...  1.46 us
    ppermute x1, waiting for transfers between devices, packed_local(): theirs = lax.ppermute(send, 'tm', swap)  1.33 us
  transfers between devices with their start and end apart: 17, of which 5 were waited for; matrix products, arithmetic and copies ran while one was open for 0% of the time, Pallas kernels for 7%

profile of v7, /device:TPU:17, one launch (start us, length us, event | category | flops | bytes accessed | tf_op | source)
XLA Modules:
  0.0 59.1 jit_solution(17491923550187774246)
XLA Ops:
  0.0 1.5 %plan.1 = (f32[16,128]{1,0:T(8,128)S(1)}, s32[1]{0:T(128)}) custom-call(s32[1,256]{1,0:T(1,128)} %bitcast.18), custom_call_target="tpu_custom_call" | custom-call | tf_op jit(solution)/shard_map/plan/pallas_call | solution.py:315
  2.2 54.7 %conditional.1 = ((f32[16,16,32]{2,1,0:T(8,128)S(1)}, f32[16,16,32]{2,1,0:T(8,128)S(1)})) conditional(s32[]{:T(128)} %bitcast.1, (s32[16]{0:T(128)}, s32[2]{0:T(128)S(1)}, f32[16,128]{1,0:T(8,128)S(1)}, bf16[2,8,2,16,2048]{4,3,2,1,0:T(8,128)(2,1)}, bf16[4,8,2,16,256]{4,3,2,1,0:T(8,128)(2,1)}, ...), branch_computations={%region_0.0_spmd, %region_1.0_spmd, %region_2.0_spmd, %region_3.0_... | conditional | bytes 8852672 | solution.py:325
  2.5 1.8 %pack.18 = (bf16[512,128]{1,0:T(8,128)(2,1)S(1)}, bf16[512,128]{1,0:T(8,128)(2,1)S(1)}) custom-call(s32[2]{0:T(128)S(1)} %get-tuple-element.143.place, f32[16,128]{1,0:T(8,128)S(1)} %get-tuple-element.146.position, bf16[2,8,2,16,2048]{4,3,2,1,0:T(8,128)(2,1)} %get-tuple-element.147.frames, bf16[4,8,2,16,256]{4,3,2,1,0:T(8,128)(2,1)} %get-tuple-element.148.dark), custom_call_target="tpu_custom_call" | custom-call | tf_op jit(solution)/shard_map/cond/branch_3_fun/pack/pallas_call | solution.py:272
  4.3 0.2 collective-permute-start.50
  4.6 3.2 %collective-permute-start.49 = (bf16[512,128]{1,0:T(8,128)(2,1)S(1)}, bf16[512,128]{1,0:T(8,128)(2,1)S(1)}, u32[]{:S(2)}, u32[]{:S(2)}) collective-permute-start(bf16[512,128]{1,0:T(8,128)(2,1)S(1)} %get-tuple-element.149.refs_0_), channel_id=1, source_target_pairs={{0,4},{1,5},{2,6},{3,7},{4,0},{5,1},{6,2},{7,3},{8,12},{9,13},{10,... | collective-permute-start | bytes 393224 | tf_op jit(solution)/shard_map/cond/branch_3_fun/ppermute | solution.py:296
  7.8 4.2 %pack.19 = (bf16[512,128]{1,0:T(8,128)(2,1)S(1)}, bf16[512,128]{1,0:T(8,128)(2,1)S(1)}, bf16[512,128]{1,0:T(8,128)(2,1)S(1)}, bf16[512,128]{1,0:T(8,128)(2,1)S(1...) custom-call(s32[2]{0:T(128)S(1)} %get-tuple-element.143.place, ...), custom_call_target="tpu_custom_call" | custom-call | tf_op jit(solution)/shard_map/cond/branch_3_fun/pack/pallas_call | solution.py:272
  11.9 1.3 %collective-permute-start.51 = (bf16[512,128]{1,0:T(8,128)(2,1)S(1)}, bf16[512,128]{1,0:T(8,128)(2,1)S(1)}, u32[]{:S(2)}, u32[]{:S(2)}) collective-permute-start(bf16[512,128]{1,0:T(8,128)(2,1)S(1)} %get-tuple-element.151), channel_id=1, source_target_pairs={{0,1},{1,0},{2,3},{3,2},{4,5},{5,4},{6,7},{7,6},{8,9},{9,8},{10,11... | collective-permute-start | bytes 393224 | tf_op jit(solution)/shard_map/cond/branch_3_fun/ppermute | solution.py:296
  13.2 1.5 %collective-permute-start.48 = (s32[16]{0:T(128)S(1)}, s32[16]{0:T(128)S(1)}, u32[]{:S(2)}, u32[]{:S(2)}) collective-permute-start(s32[16]{0:T(128)S(1)} %copy-done.9), channel_id=1, source_target_pairs={{0,8},{8,0},{1,9},{9,1},{2,10},{10,2},{3,11},{11,3},{4,12},{12,4},... | collective-permute-start | bytes 200 | tf_op jit(solution)/shard_map/cond/branch_3_fun/ppermute | solution.py:294
  14.8 0.8 %collective-permute-done.48.other_index = s32[16]{0:T(128)S(1)} collective-permute-done((s32[16]{0:T(128)S(1)}, s32[16]{0:T(128)S(1)}, u32[]{:S(2)}, u32[]{:S(2)}) %collective-permute-start.48) | collective-permute-done | bytes 96 | tf_op jit(solution)/shard_map/cond/branch_3_fun/ppermute | solution.py:294
  15.6 2.7 %collective-permute-start.54 = (bf16[512,128]{1,0:T(8,128)(2,1)S(1)}, bf16[512,128]{1,0:T(8,128)(2,1)S(1)}, u32[]{:S(2)}, u32[]{:S(2)}) collective-permute-start(bf16[512,128]{1,0:T(8,128)(2,1)S(1)} %get-tuple-element.154), channel_id=1, source_target_pairs={{0,7},{1,6},{2,5},{3,4},{4,3},{5,2},{6,1},{7,0},{8,15},{9,14},{10,... | collective-permute-start | bytes 393224 | tf_op jit(solution)/shard_map/cond/branch_3_fun/ppermute | solution.py:296
  18.3 1.0 %collective-permute-start.55 = (bf16[512,128]{1,0:T(8,128)(2,1)S(1)}, bf16[512,128]{1,0:T(8,128)(2,1)S(1)}, u32[]{:S(2)}, u32[]{:S(2)}) collective-permute-start(bf16[512,128]{1,0:T(8,128)(2,1)S(1)} %get-tuple-element.155), channel_id=1, source_target_pairs={{0,3},{1,2},{2,1},{3,0},{4,7},{5,6},{6,5},{7,4},{8,11},{9,10},{10,... | collective-permute-start | bytes 393224 | tf_op jit(solution)/shard_map/cond/branch_3_fun/ppermute | solution.py:296
  19.3 4.8 %collective-permute-start.56 = (bf16[512,128]{1,0:T(8,128)(2,1)S(1)}, bf16[512,128]{1,0:T(8,128)(2,1)S(1)}, u32[]{:S(2)}, u32[]{:S(2)}) collective-permute-start(bf16[512,128]{1,0:T(8,128)(2,1)S(1)} %get-tuple-element.156), channel_id=1, source_target_pairs={{0,12},{1,13},{2,14},{3,15},{4,8},{5,9},{6,10},{7,11},{8,4},{9,5},... | collective-permute-start | bytes 393224 | tf_op jit(solution)/shard_map/cond/branch_3_fun/ppermute | solution.py:296
  24.2 3.2 %collective-permute-start.57 = (bf16[512,128]{1,0:T(8,128)(2,1)S(1)}, bf16[512,128]{1,0:T(8,128)(2,1)S(1)}, u32[]{:S(2)}, u32[]{:S(2)}) collective-permute-start(bf16[512,128]{1,0:T(8,128)(2,1)S(1)} %get-tuple-element.157), channel_id=1, source_target_pairs={{0,9},{1,8},{2,11},{3,10},{4,13},{5,12},{6,15},{7,14},{8,1},{9,0},... | collective-permute-start | bytes 393224 | tf_op jit(solution)/shard_map/cond/branch_3_fun/ppermute | solution.py:296
  27.4 1.1 %collective-permute-start.58 = (bf16[512,128]{1,0:T(8,128)(2,1)S(1)}, bf16[512,128]{1,0:T(8,128)(2,1)S(1)}, u32[]{:S(2)}, u32[]{:S(2)}) collective-permute-start(bf16[512,128]{1,0:T(8,128)(2,1)S(1)} %get-tuple-element.158), channel_id=1, source_target_pairs={{0,14},{1,15},{2,12},{3,13},{4,10},{5,11},{6,8},{7,9},{8,6},{9,7},... | collective-permute-start | bytes 393224 | tf_op jit(solution)/shard_map/cond/branch_3_fun/ppermute | solution.py:296
  28.5 1.0 %collective-permute-done.54.refs_5_ = bf16[512,128]{1,0:T(8,128)(2,1)S(1)} collective-permute-done((bf16[512,128]{1,0:T(8,128)(2,1)S(1)}, bf16[512,128]{1,0:T(8,128)(2,1)S(1)}, u32[]{:S(2)}, u32[]{:S(2)}) %collective-permute-start.54) | collective-permute-done | bytes 131104 | tf_op jit(solution)/shard_map/cond/branch_3_fun/ppermute | solution.py:296
  29.5 2.3 %collective-permute-start.59 = (bf16[512,128]{1,0:T(8,128)(2,1)S(1)}, bf16[512,128]{1,0:T(8,128)(2,1)S(1)}, u32[]{:S(2)}, u32[]{:S(2)}) collective-permute-start(bf16[512,128]{1,0:T(8,128)(2,1)S(1)} %get-tuple-element.159), channel_id=1, source_target_pairs={{0,10},{1,11},{2,8},{3,9},{4,14},{5,15},{6,12},{7,13},{8,2},{9,3},... | collective-permute-start | bytes 393224 | tf_op jit(solution)/shard_map/cond/branch_3_fun/ppermute | solution.py:296
  31.8 2.3 %collective-permute-start.60 = (bf16[512,128]{1,0:T(8,128)(2,1)S(1)}, bf16[512,128]{1,0:T(8,128)(2,1)S(1)}, u32[]{:S(2)}, u32[]{:S(2)}) collective-permute-start(bf16[512,128]{1,0:T(8,128)(2,1)S(1)} %get-tuple-element.160), channel_id=1, source_target_pairs={{0,13},{1,12},{2,15},{3,14},{4,9},{5,8},{6,11},{7,10},{8,5},{9,4},... | collective-permute-start | bytes 393224 | tf_op jit(solution)/shard_map/cond/branch_3_fun/ppermute | solution.py:296
  34.0 5.4 %collective-permute-start.61 = (bf16[512,128]{1,0:T(8,128)(2,1)S(1)}, bf16[512,128]{1,0:T(8,128)(2,1)S(1)}, u32[]{:S(2)}, u32[]{:S(2)}) collective-permute-start(bf16[512,128]{1,0:T(8,128)(2,1)S(1)} %get-tuple-element.161), channel_id=1, source_target_pairs={{0,11},{1,10},{2,9},{3,8},{4,15},{5,14},{6,13},{7,12},{8,3},{9,2},... | collective-permute-start | bytes 393224 | tf_op jit(solution)/shard_map/cond/branch_3_fun/ppermute | solution.py:296
  39.4 3.3 %collective-permute-start.62 = (bf16[512,128]{1,0:T(8,128)(2,1)S(1)}, bf16[512,128]{1,0:T(8,128)(2,1)S(1)}, u32[]{:S(2)}, u32[]{:S(2)}) collective-permute-start(bf16[512,128]{1,0:T(8,128)(2,1)S(1)} %get-tuple-element.162), channel_id=1, source_target_pairs={{0,15},{1,14},{2,13},{3,12},{4,11},{5,10},{6,9},{7,8},{8,7},{9,6},... | collective-permute-start | bytes 393224 | tf_op jit(solution)/shard_map/cond/branch_3_fun/ppermute | solution.py:296
  42.7 2.2 %collective-permute-done.58.refs_9_ = bf16[512,128]{1,0:T(8,128)(2,1)S(1)} collective-permute-done((bf16[512,128]{1,0:T(8,128)(2,1)S(1)}, bf16[512,128]{1,0:T(8,128)(2,1)S(1)}, u32[]{:S(2)}, u32[]{:S(2)}) %collective-permute-start.58) | collective-permute-done | bytes 131104 | tf_op jit(solution)/shard_map/cond/branch_3_fun/ppermute | solution.py:296
  44.9 7.9 %collective-permute-done.62.refs_13_ = bf16[512,128]{1,0:T(8,128)(2,1)S(1)} collective-permute-done((bf16[512,128]{1,0:T(8,128)(2,1)S(1)}, bf16[512,128]{1,0:T(8,128)(2,1)S(1)}, u32[]{:S(2)}, u32[]{:S(2)}) %collective-permute-start.62) | collective-permute-done | bytes 131104 | tf_op jit(solution)/shard_map/cond/branch_3_fun/ppermute | solution.py:296
  52.8 3.8 %gram.9 = (f32[16,16,32]{2,1,0:T(8,128)S(1)}, f32[16,16,32]{2,1,0:T(8,128)S(1)}) custom-call(s32[2]{0:T(128)S(1)} %get-tuple-element.143.place, s32[16]{0:T(128)S(1)} %copy-done.9, s32[16]{0:T(128)S(1)} %collective-permute-done.48.other_index, s32[256]{0:T(256)S(1)} %copy-done.3, f32[16,128]{1,0:T(8,128)S(1)} %get-tuple-element.146.position, ...), custom_call_target="tpu_custom_call" | custom-call | tf_op jit(solution)/shard_map/cond/branch_3_fun/gram/pallas_call | solution.py:300
  57.0 1.3 %collective-permute-done.96 = f32[16,16,32]{2,1,0:T(8,128)S(1)} collective-permute-done((f32[16,16,32]{2,1,0:T(8,128)S(1)}, f32[16,16,32]{2,1,0:T(8,128)S(1)}, u32[]{:S(2)}, u32[]{:S(2)}) %collective-permute-start.96) | collective-permute-done | bytes 32800 | tf_op jit(solution)/shard_map/ppermute | solution.py:335
  58.4 0.7 %pad_maximum_fusion = f32[32,16,32]{2,1,0:T(8,128)} fusion(f32[16,16,32]{2,1,0:T(8,128)S(1)} %get-tuple-element.218, f32[16,16,32]{2,1,0:T(8,128)S(1)} %get-tuple-element.217), kind=kLoop, calls=%fused_computation | loop fusion | flops 16384 | bytes 131072 | tf_op jit(solution)/shard_map/concatenate | solution.py:337
  (22 shorter events, 0.2 us)
Async XLA Ops:
  2.5 10.8 %copy-start.9 = (s32[16]{0:T(128)S(1)}, s32[16]{0:T(128)}, u32[]{:S(2)}) copy-start(s32[16]{0:T(128)} %get-tuple-element.144.own_index) | copy-start | bytes 196 | tf_op jit(solution)/shard_map/cond
  2.5 50.3 %copy-start.3 = (s32[256]{0:T(256)S(1)}, s32[256]{0:T(256)}, u32[]{:S(2)}) copy-start(s32[256]{0:T(256)} %get-tuple-element.145.cycle_counts) | copy-start | bytes 3076 | tf_op jit(solution)/shard_map/cond
  4.3 11.3 %collective-permute-start.50 = (bf16[512,128]{1,0:T(8,128)(2,1)S(1)}, bf16[512,128]{1,0:T(8,128)(2,1)S(1)}, u32[]{:S(2)}, u32[]{:S(2)}) collective-permute-start(bf16[512,128]{1,0:T(8,128)(2,1)S(1)} %get-tuple-element.150), channel_id=1, source_target_pairs={{0,6},{1,7},{2,4},{3,5},{4,2},{5,3},{6,0},{7,1},{8,14},{9,15},{10,... | collective-permute-start | bytes 393224 | tf_op jit(solution)/shard_map/cond/branch_3_fun/ppermute | solution.py:296
  4.6 13.8 %collective-permute-start.49 = (bf16[512,128]{1,0:T(8,128)(2,1)S(1)}, bf16[512,128]{1,0:T(8,128)(2,1)S(1)}, u32[]{:S(2)}, u32[]{:S(2)}) collective-permute-start(bf16[512,128]{1,0:T(8,128)(2,1)S(1)} %get-tuple-element.149.refs_0_), channel_id=1, source_target_pairs={{0,4},{1,5},{2,6},{3,7},{4,0},{5,1},{6,2},{7,3},{8,12},{9,13},{10,... | collective-permute-start | bytes 393224 | tf_op jit(solution)/shard_map/cond/branch_3_fun/ppermute | solution.py:296
  11.9 7.4 %collective-permute-start.51 = (bf16[512,128]{1,0:T(8,128)(2,1)S(1)}, bf16[512,128]{1,0:T(8,128)(2,1)S(1)}, u32[]{:S(2)}, u32[]{:S(2)}) collective-permute-start(bf16[512,128]{1,0:T(8,128)(2,1)S(1)} %get-tuple-element.151), channel_id=1, source_target_pairs={{0,1},{1,0},{2,3},{3,2},{4,5},{5,4},{6,7},{7,6},{8,9},{9,8},{10,11... | collective-permute-start | bytes 393224 | tf_op jit(solution)/shard_map/cond/branch_3_fun/ppermute | solution.py:296
  13.2 2.3 %collective-permute-start.48 = (s32[16]{0:T(128)S(1)}, s32[16]{0:T(128)S(1)}, u32[]{:S(2)}, u32[]{:S(2)}) collective-permute-start(s32[16]{0:T(128)S(1)} %copy-done.9), channel_id=1, source_target_pairs={{0,8},{8,0},{1,9},{9,1},{2,10},{10,2},{3,11},{11,3},{4,12},{12,4},... | collective-permute-start | bytes 200 | tf_op jit(solution)/shard_map/cond/branch_3_fun/ppermute | solution.py:294
  14.7 9.4 %collective-permute-start.52 = (bf16[512,128]{1,0:T(8,128)(2,1)S(1)}, bf16[512,128]{1,0:T(8,128)(2,1)S(1)}, u32[]{:S(2)}, u32[]{:S(2)}) collective-permute-start(bf16[512,128]{1,0:T(8,128)(2,1)S(1)} %get-tuple-element.152), channel_id=1, source_target_pairs={{0,5},{1,4},{2,7},{3,6},{4,1},{5,0},{6,3},{7,2},{8,13},{9,12},{10,... | collective-permute-start | bytes 393224 | tf_op jit(solution)/shard_map/cond/branch_3_fun/ppermute | solution.py:296
  15.6 11.8 %collective-permute-start.53 = (bf16[512,128]{1,0:T(8,128)(2,1)S(1)}, bf16[512,128]{1,0:T(8,128)(2,1)S(1)}, u32[]{:S(2)}, u32[]{:S(2)}) collective-permute-start(bf16[512,128]{1,0:T(8,128)(2,1)S(1)} %get-tuple-element.153), channel_id=1, source_target_pairs={{0,2},{1,3},{2,0},{3,1},{4,6},{5,7},{6,4},{7,5},{8,10},{9,11},{10,... | collective-permute-start | bytes 393224 | tf_op jit(solution)/shard_map/cond/branch_3_fun/ppermute | solution.py:296
  15.6 13.9 %collective-permute-start.54 = (bf16[512,128]{1,0:T(8,128)(2,1)S(1)}, bf16[512,128]{1,0:T(8,128)(2,1)S(1)}, u32[]{:S(2)}, u32[]{:S(2)}) collective-permute-start(bf16[512,128]{1,0:T(8,128)(2,1)S(1)} %get-tuple-element.154), channel_id=1, source_target_pairs={{0,7},{1,6},{2,5},{3,4},{4,3},{5,2},{6,1},{7,0},{8,15},{9,14},{10,... | collective-permute-start | bytes 393224 | tf_op jit(solution)/shard_map/cond/branch_3_fun/ppermute | solution.py:296
  18.3 13.5 %collective-permute-start.55 = (bf16[512,128]{1,0:T(8,128)(2,1)S(1)}, bf16[512,128]{1,0:T(8,128)(2,1)S(1)}, u32[]{:S(2)}, u32[]{:S(2)}) collective-permute-start(bf16[512,128]{1,0:T(8,128)(2,1)S(1)} %get-tuple-element.155), channel_id=1, source_target_pairs={{0,3},{1,2},{2,1},{3,0},{4,7},{5,6},{6,5},{7,4},{8,11},{9,10},{10,... | collective-permute-start | bytes 393224 | tf_op jit(solution)/shard_map/cond/branch_3_fun/ppermute | solution.py:296
  19.3 14.7 %collective-permute-start.56 = (bf16[512,128]{1,0:T(8,128)(2,1)S(1)}, bf16[512,128]{1,0:T(8,128)(2,1)S(1)}, u32[]{:S(2)}, u32[]{:S(2)}) collective-permute-start(bf16[512,128]{1,0:T(8,128)(2,1)S(1)} %get-tuple-element.156), channel_id=1, source_target_pairs={{0,12},{1,13},{2,14},{3,15},{4,8},{5,9},{6,10},{7,11},{8,4},{9,5},... | collective-permute-start | bytes 393224 | tf_op jit(solution)/shard_map/cond/branch_3_fun/ppermute | solution.py:296
  24.2 15.2 %collective-permute-start.57 = (bf16[512,128]{1,0:T(8,128)(2,1)S(1)}, bf16[512,128]{1,0:T(8,128)(2,1)S(1)}, u32[]{:S(2)}, u32[]{:S(2)}) collective-permute-start(bf16[512,128]{1,0:T(8,128)(2,1)S(1)} %get-tuple-element.157), channel_id=1, source_target_pairs={{0,9},{1,8},{2,11},{3,10},{4,13},{5,12},{6,15},{7,14},{8,1},{9,0},... | collective-permute-start | bytes 393224 | tf_op jit(solution)/shard_map/cond/branch_3_fun/ppermute | solution.py:296
  27.4 17.5 %collective-permute-start.58 = (bf16[512,128]{1,0:T(8,128)(2,1)S(1)}, bf16[512,128]{1,0:T(8,128)(2,1)S(1)}, u32[]{:S(2)}, u32[]{:S(2)}) collective-permute-start(bf16[512,128]{1,0:T(8,128)(2,1)S(1)} %get-tuple-element.158), channel_id=1, source_target_pairs={{0,14},{1,15},{2,12},{3,13},{4,10},{5,11},{6,8},{7,9},{8,6},{9,7},... | collective-permute-start | bytes 393224 | tf_op jit(solution)/shard_map/cond/branch_3_fun/ppermute | solution.py:296
  29.5 15.4 %collective-permute-start.59 = (bf16[512,128]{1,0:T(8,128)(2,1)S(1)}, bf16[512,128]{1,0:T(8,128)(2,1)S(1)}, u32[]{:S(2)}, u32[]{:S(2)}) collective-permute-start(bf16[512,128]{1,0:T(8,128)(2,1)S(1)} %get-tuple-element.159), channel_id=1, source_target_pairs={{0,10},{1,11},{2,8},{3,9},{4,14},{5,15},{6,12},{7,13},{8,2},{9,3},... | collective-permute-start | bytes 393224 | tf_op jit(solution)/shard_map/cond/branch_3_fun/ppermute | solution.py:296
  31.8 13.1 %collective-permute-start.60 = (bf16[512,128]{1,0:T(8,128)(2,1)S(1)}, bf16[512,128]{1,0:T(8,128)(2,1)S(1)}, u32[]{:S(2)}, u32[]{:S(2)}) collective-permute-start(bf16[512,128]{1,0:T(8,128)(2,1)S(1)} %get-tuple-element.160), channel_id=1, source_target_pairs={{0,13},{1,12},{2,15},{3,14},{4,9},{5,8},{6,11},{7,10},{8,5},{9,4},... | collective-permute-start | bytes 393224 | tf_op jit(solution)/shard_map/cond/branch_3_fun/ppermute | solution.py:296
  34.0 10.8 %collective-permute-start.61 = (bf16[512,128]{1,0:T(8,128)(2,1)S(1)}, bf16[512,128]{1,0:T(8,128)(2,1)S(1)}, u32[]{:S(2)}, u32[]{:S(2)}) collective-permute-start(bf16[512,128]{1,0:T(8,128)(2,1)S(1)} %get-tuple-element.161), channel_id=1, source_target_pairs={{0,11},{1,10},{2,9},{3,8},{4,15},{5,14},{6,13},{7,12},{8,3},{9,2},... | collective-permute-start | bytes 393224 | tf_op jit(solution)/shard_map/cond/branch_3_fun/ppermute | solution.py:296
  39.4 13.4 %collective-permute-start.62 = (bf16[512,128]{1,0:T(8,128)(2,1)S(1)}, bf16[512,128]{1,0:T(8,128)(2,1)S(1)}, u32[]{:S(2)}, u32[]{:S(2)}) collective-permute-start(bf16[512,128]{1,0:T(8,128)(2,1)S(1)} %get-tuple-element.162), channel_id=1, source_target_pairs={{0,15},{1,14},{2,13},{3,12},{4,11},{5,10},{6,9},{7,8},{8,7},{9,6},... | collective-permute-start | bytes 393224 | tf_op jit(solution)/shard_map/cond/branch_3_fun/ppermute | solution.py:296
  44.8 7.9 %collective-permute-start.63 = (bf16[512,128]{1,0:T(8,128)(2,1)S(1)}, bf16[512,128]{1,0:T(8,128)(2,1)S(1)}, u32[]{:S(2)}, u32[]{:S(2)}) collective-permute-start(bf16[512,128]{1,0:T(8,128)(2,1)S(1)} %get-tuple-element.163), channel_id=1, source_target_pairs={{0,8},{1,9},{2,10},{3,11},{4,12},{5,13},{6,14},{7,15},{8,0},{9,1},... | collective-permute-start | bytes 393224 | tf_op jit(solution)/shard_map/cond/branch_3_fun/ppermute | solution.py:296
  56.9 1.4 %collective-permute-start.96 = (f32[16,16,32]{2,1,0:T(8,128)S(1)}, f32[16,16,32]{2,1,0:T(8,128)S(1)}, u32[]{:S(2)}, u32[]{:S(2)}) collective-permute-start(f32[16,16,32]{2,1,0:T(8,128)S(1)} %get-tuple-element.216), channel_id=1, source_target_pairs={{0,8},{8,0},{1,9},{9,1},{2,10},{10,2},{3,11},{11,3},{4,12},{12,4},... | collective-permute-start | bytes 98312 | tf_op jit(solution)/shard_map/ppermute | solution.py:335
